TPU v7x, 32 devices: a whole 2x2x4 slice. The times are simulated.
32 devices in a mesh: dp: 8 (over z, y), tensor: 4 (over x, core).
Axes of the slice: x: 2, y: 2, z: 4, core: 2. Of those that a mesh axis runs over, the one named last changes fastest.
Arguments:
- states: bfloat16 [4096, 2048], P('dp'), may hold values from -6 to 6
- teacher: bfloat16 [4096, 2048], P('dp'), may hold values from -6 to 6
- segments: int32 [4096], P('dp'), may hold values from 0 to 9, as said below
- positions: int32 [4096], P('dp'), may hold values from 0 to 511, as said below
- w_q: bfloat16 [2048, 2048], P('dp', 'tensor'), may hold values from -0.125 to 0.125
- key_matrix: bfloat16 [2048, 1024], P('dp', 'tensor'), may hold values from -0.125 to 0.125
- value_matrix: bfloat16 [2048, 1024], P('dp', 'tensor'), may hold values from -0.125 to 0.125
- w_o: bfloat16 [2048, 2048], P('tensor', 'dp'), may hold values from -0.75 to 0.75
- w_gate: bfloat16 [2048, 8192], P('dp', 'tensor'), may hold values from -0.125 to 0.125
- w_up: bfloat16 [2048, 8192], P('dp', 'tensor'), may hold values from -0.125 to 0.125
- w_down: bfloat16 [8192, 2048], P('tensor', 'dp'), may hold values from -0.0625 to 0.0625
- norm1_gain: bfloat16 [2048], P('dp'), may hold values from 0.5 to 1.5
- norm2_gain: bfloat16 [2048], P('dp'), may hold values from 0.5 to 1.5
Outputs:
- out_states: bfloat16 [4096, 2048], P('dp')
- grad_states: float32 [4096, 2048], P('dp')
- loss_value: float32 [], replicated
- grad_w_q: float32 [2048, 2048], P('dp', 'tensor')
- grad_w_k: float32 [2048, 1024], P('dp', 'tensor')
- grad_w_v: float32 [2048, 1024], P('dp', 'tensor')
- grad_w_o: float32 [2048, 2048], P('tensor', 'dp')
- grad_w_gate: float32 [2048, 8192], P('dp', 'tensor')
- grad_w_up: float32 [2048, 8192], P('dp', 'tensor')
- grad_w_down: float32 [8192, 2048], P('tensor', 'dp')
- grad_norm1_gain: float32 [2048], P('dp')
- grad_norm2_gain: float32 [2048], P('dp')
Inputs may be any that keep to these rules, and one draw needn't show every extreme that they name: `segments`: each run of 512 slots is one sequence: documents numbered 1, 2, 3 in order, each of 60 to 512 tokens except that the last may be cut short, then padding numbered 0; the first sequence has no padding and only documents of 60 tokens, its last possibly cut; the last sequence has no padding and a first document of exactly 512 tokens. `positions`: each token's place within its document, counted from 0; 0 on padding.
All inputs are finite; a program needn't handle non-finite values.
Results may differ from a plain program's by a relative error of at most 0.014.
Values may be sent and summed in bfloat16 or wider, within the bound.
No kernel may reach another device: no remote copies, remote signals or barrier semaphores. Data moves between devices by JAX's collectives and lax.ppermute only.
A program may use at most 192 MiB of HBM per device.

v0:
```python
import math

import jax
import jax.numpy as jnp
from jax import lax
from jax.sharding import PartitionSpec as P

MODEL_WIDTH = 2048
HEAD_SIZE = 256


EPS = 1e-06
THETA = 1000042.0


def tables(places, width):
    halfway = width // 2
    counter = jnp.arange(halfway, dtype=jnp.float32)
    inverse = jnp.exp(counter * (-2.0 * math.log(THETA) / width))
    angles = places.astype(jnp.float32)[..., None] * inverse
    return (jnp.cos(angles), jnp.sin(angles))


def rotate(value_rows, cos_table, sin_table):
    halfway = value_rows.shape[-1] // 2
    first_half = value_rows[..., :halfway]
    second_half = value_rows[..., halfway:]
    return jnp.concatenate(
        [
            first_half * cos_table - second_half * sin_table,
            second_half * cos_table + first_half * sin_table,
        ],
        axis=-1,
    )


def unrotate(grads_in, cos_table, sin_table):
    halfway = grads_in.shape[-1] // 2
    first_half = grads_in[..., :halfway]
    second_half = grads_in[..., halfway:]
    return jnp.concatenate(
        [
            first_half * cos_table + second_half * sin_table,
            second_half * cos_table - first_half * sin_table,
        ],
        axis=-1,
    )


def rms_scale(value_rows):
    return lax.rsqrt(jnp.mean(value_rows * value_rows, axis=-1, keepdims=True) + EPS)


def norm_back(grad_normed, unit_rows, recip_rows, gain_full):
    scaled = grad_normed * gain_full
    gain_grad = jnp.sum(grad_normed * unit_rows, axis=0)
    grad_rows = recip_rows * (
        scaled - unit_rows * jnp.mean(scaled * unit_rows, axis=-1, keepdims=True)
    )
    return (gain_grad, grad_rows)


def token_dot(left, right):
    return lax.dot_general(
        left, right, (((0,), (0,)), ((), ())), preferred_element_type=jnp.float32
    )


def dot_trans(left, right):
    return lax.dot_general(
        left, right, (((1,), (1,)), ((), ())), preferred_element_type=jnp.float32
    )


def per_device(
    states,
    teacher,
    segments,
    positions,
    w_q,
    key_matrix,
    value_matrix,
    w_o,
    w_gate,
    w_up,
    w_down,
    norm1_gain,
    norm2_gain,
):
    gathered = (
        lax.all_gather(w_q, "dp", axis=0, tiled=True),
        lax.all_gather(key_matrix, "dp", axis=0, tiled=True),
        lax.all_gather(value_matrix, "dp", axis=0, tiled=True),
        lax.all_gather(w_o, "dp", axis=1, tiled=True),
        lax.all_gather(w_gate, "dp", axis=0, tiled=True),
        lax.all_gather(w_up, "dp", axis=0, tiled=True),
        lax.all_gather(w_down, "dp", axis=1, tiled=True),
        lax.all_gather(norm1_gain, "dp", axis=0, tiled=True),
        lax.all_gather(norm2_gain, "dp", axis=0, tiled=True),
    )
    full_q, full_k, full_v, full_o, full_gate, full_up, full_down, gain_raw_one, gain_raw_two = (
        gathered
    )
    gain_one = gain_raw_one.astype(jnp.float32)
    gain_two = gain_raw_two.astype(jnp.float32)
    sequence_length = states.shape[0]
    heads_q = full_q.shape[1] // HEAD_SIZE
    heads_kv = full_k.shape[1] // HEAD_SIZE
    repeat_factor = heads_q // heads_kv
    inputs = states.astype(jnp.float32)
    recip_one = rms_scale(inputs)
    unit_one = inputs * recip_one
    normed = (unit_one * gain_one).astype(jnp.bfloat16)
    query_rows = jnp.dot(normed, full_q, preferred_element_type=jnp.float32)
    query_rows = query_rows.reshape(sequence_length, heads_kv, repeat_factor, HEAD_SIZE).transpose(
        1, 2, 0, 3
    )
    unrotated_keys = jnp.dot(normed, full_k, preferred_element_type=jnp.float32)
    unrotated_keys = unrotated_keys.reshape(sequence_length, heads_kv, HEAD_SIZE).transpose(1, 0, 2)
    value_rows = jnp.dot(normed, full_v, preferred_element_type=jnp.float32).astype(jnp.bfloat16)
    value_rows = value_rows.reshape(sequence_length, heads_kv, HEAD_SIZE).transpose(1, 0, 2)
    cos_table, sin_table = tables(positions, HEAD_SIZE)
    rotated_query = rotate(query_rows, cos_table, sin_table).astype(jnp.bfloat16)
    rotated_k = rotate(unrotated_keys, cos_table, sin_table).astype(jnp.bfloat16)
    rows_per_block = min(512, sequence_length)
    score_scale = 1.0 / math.sqrt(HEAD_SIZE)
    key_index = jnp.arange(sequence_length, dtype=jnp.int32)

    def block_scores(offset):
        scores = (
            jnp.einsum(
                "krbe,kte->krbt", rotated_query, rotated_k, preferred_element_type=jnp.float32
            )
            * score_scale
        )
        allowed = (segments[offset : offset + rows_per_block, None] == segments[None, :]) & (
            key_index[None, :] <= key_index[offset : offset + rows_per_block, None]
        )
        return (rotated_query, jnp.where(allowed, scores, -1e30))

    offsets = list(range(0, sequence_length, rows_per_block))
    out_pieces = []
    lse_pieces = []
    for offset in offsets:
        query_block, scores = block_scores(offset)
        largest = jnp.max(scores, axis=-1, keepdims=True)
        exponent = jnp.exp(scores - largest)
        row_total = jnp.sum(exponent, axis=-1, keepdims=True)
        weights = exponent / row_total
        lse_pieces.append(largest + jnp.log(row_total))
        out_pieces.append(
            jnp.einsum(
                "krbt,kte->krbe",
                weights.astype(jnp.bfloat16),
                value_rows,
                preferred_element_type=jnp.float32,
            )
        )
    attended_rows = (
        out_pieces[0].transpose(2, 0, 1, 3).reshape(sequence_length, heads_q * HEAD_SIZE)
    )
    attended_rows = attended_rows.astype(jnp.bfloat16)
    attn_sum = lax.psum(
        jnp.dot(attended_rows, full_o, preferred_element_type=jnp.float32), "tensor"
    )
    hidden = inputs + attn_sum
    recip_two = rms_scale(hidden)
    unit_two = hidden * recip_two
    normed_two = (unit_two * gain_two).astype(jnp.bfloat16)
    gate_proj = jnp.dot(normed_two, full_gate, preferred_element_type=jnp.float32)
    up_proj = jnp.dot(normed_two, full_up, preferred_element_type=jnp.float32)
    sigmoid_gate = jax.nn.sigmoid(gate_proj)
    silu_gate = gate_proj * sigmoid_gate
    active = (silu_gate * up_proj).astype(jnp.bfloat16)
    mlp_sum = lax.psum(jnp.dot(active, full_down, preferred_element_type=jnp.float32), "tensor")
    output = hidden + mlp_sum
    live_mask = (segments > 0).astype(jnp.float32)
    error = (output - teacher.astype(jnp.float32)) * live_mask[:, None]
    squares_sum, live_count = lax.psum((jnp.sum(error * error), jnp.sum(live_mask)), "dp")
    loss_value = squares_sum / (live_count * MODEL_WIDTH)
    factor = lax.axis_size("dp") * sequence_length / live_count
    grad_out = error * factor
    grad_out_low = grad_out.astype(jnp.bfloat16)
    grad_wdown = token_dot(active, grad_out_low)
    grad_active = dot_trans(grad_out_low, full_down)
    grad_gate = (
        grad_active * up_proj * sigmoid_gate * (1.0 + gate_proj * (1.0 - sigmoid_gate))
    ).astype(jnp.bfloat16)
    grad_up = (grad_active * silu_gate).astype(jnp.bfloat16)
    grad_wgate = token_dot(normed_two, grad_gate)
    grad_wup = token_dot(normed_two, grad_up)
    back_two = lax.psum(dot_trans(grad_gate, full_gate) + dot_trans(grad_up, full_up), "tensor")
    gain_two_grad, hidden_from_norm = norm_back(back_two, unit_two, recip_two, gain_two)
    grad_hidden = grad_out + hidden_from_norm
    grad_hidden_low = grad_hidden.astype(jnp.bfloat16)
    grad_wo = token_dot(attended_rows, grad_hidden_low)
    grad_attended = dot_trans(grad_hidden_low, full_o).astype(jnp.bfloat16)
    grad_attended = grad_attended.reshape(
        sequence_length, heads_kv, repeat_factor, HEAD_SIZE
    ).transpose(1, 2, 0, 3)
    grad_keys = jnp.zeros((heads_kv, sequence_length, HEAD_SIZE), jnp.float32)
    grad_values = jnp.zeros((heads_kv, sequence_length, HEAD_SIZE), jnp.float32)
    grad_q_pieces = []
    for number, offset in enumerate(offsets):
        query_block, scores = block_scores(offset)
        weights = jnp.exp(scores - lse_pieces[number])
        grad_weights = jnp.einsum(
            "krbe,kte->krbt", grad_attended, value_rows, preferred_element_type=jnp.float32
        )
        inner = jnp.sum(weights * grad_weights, axis=-1, keepdims=True)
        grad_scores = (weights * (grad_weights - inner)).astype(jnp.bfloat16)
        grad_q_pieces.append(
            jnp.einsum("krbt,kte->krbe", grad_scores, rotated_k, preferred_element_type=jnp.float32)
            * score_scale
        )
        grad_keys = (
            jnp.einsum(
                "krbt,krbe->kte", grad_scores, query_block, preferred_element_type=jnp.float32
            )
            * score_scale
        )
        grad_values = jnp.einsum(
            "krbt,krbe->kte",
            weights.astype(jnp.bfloat16),
            grad_attended,
            preferred_element_type=jnp.float32,
        )
    grad_queries = unrotate(grad_q_pieces[0], cos_table, sin_table).astype(jnp.bfloat16)
    grad_queries = grad_queries.transpose(2, 0, 1, 3).reshape(sequence_length, heads_q * HEAD_SIZE)
    grad_keys_low = unrotate(grad_keys, cos_table, sin_table).astype(jnp.bfloat16)
    grad_keys_low = grad_keys_low.transpose(1, 0, 2).reshape(sequence_length, heads_kv * HEAD_SIZE)
    grad_values_low = (
        grad_values.astype(jnp.bfloat16)
        .transpose(1, 0, 2)
        .reshape(sequence_length, heads_kv * HEAD_SIZE)
    )
    grad_wq = token_dot(normed, grad_queries)
    grad_wk = token_dot(normed, grad_keys_low)
    grad_wv = token_dot(normed, grad_values_low)
    back_one = lax.psum(
        (
            dot_trans(grad_queries, full_q)
            + dot_trans(grad_keys_low, full_k)
            + dot_trans(grad_values_low, full_v)
        ).astype(jnp.bfloat16),
        "tensor",
    ).astype(jnp.float32)
    gain_one_grad, input_from_norm = norm_back(back_one, unit_one, recip_one, gain_one)
    grad_input = grad_hidden + input_from_norm
    sent_all = (
        lax.psum_scatter(
            grad_wq.astype(jnp.bfloat16), "dp", scatter_dimension=0, tiled=True
        ).astype(jnp.float32),
        lax.psum_scatter(
            grad_wk.astype(jnp.bfloat16), "dp", scatter_dimension=0, tiled=True
        ).astype(jnp.float32),
        lax.psum_scatter(
            grad_wv.astype(jnp.bfloat16), "dp", scatter_dimension=0, tiled=True
        ).astype(jnp.float32),
        lax.psum_scatter(
            grad_wo.astype(jnp.bfloat16), "dp", scatter_dimension=1, tiled=True
        ).astype(jnp.float32),
        lax.psum_scatter(
            grad_wgate.astype(jnp.bfloat16), "dp", scatter_dimension=0, tiled=True
        ).astype(jnp.float32),
        lax.psum_scatter(
            grad_wup.astype(jnp.bfloat16), "dp", scatter_dimension=0, tiled=True
        ).astype(jnp.float32),
        lax.psum_scatter(
            grad_wdown.astype(jnp.bfloat16), "dp", scatter_dimension=1, tiled=True
        ).astype(jnp.float32),
        lax.psum_scatter(
            gain_one_grad.astype(jnp.bfloat16), "dp", scatter_dimension=0, tiled=True
        ).astype(jnp.float32),
        lax.psum_scatter(
            gain_two_grad.astype(jnp.bfloat16), "dp", scatter_dimension=0, tiled=True
        ).astype(jnp.float32),
    )
    (
        result_q,
        result_k,
        result_v,
        result_o,
        result_gate,
        result_up,
        result_down,
        result_g1,
        result_g2,
    ) = sent_all
    return (
        output.astype(jnp.bfloat16),
        grad_input,
        loss_value,
        result_q,
        result_k,
        result_v,
        result_o,
        result_gate,
        result_up,
        result_down,
        result_g1,
        result_g2,
    )


def solution(mesh):
    in_specs = (
        P("dp", None),
        P("dp", None),
        P("dp"),
        P("dp"),
        P("dp", "tensor"),
        P("dp", "tensor"),
        P("dp", "tensor"),
        P("tensor", "dp"),
        P("dp", "tensor"),
        P("dp", "tensor"),
        P("tensor", "dp"),
        P("dp"),
        P("dp"),
    )
    out_specs = (
        P("dp", None),
        P("dp", None),
        P(),
        P("dp", "tensor"),
        P("dp", "tensor"),
        P("dp", "tensor"),
        P("tensor", "dp"),
        P("dp", "tensor"),
        P("dp", "tensor"),
        P("tensor", "dp"),
        P("dp"),
        P("dp"),
    )
    return jax.shard_map(
        per_device, mesh=mesh, in_specs=in_specs, out_specs=out_specs, check_vma=False
    )
```

profile of v0, /device:TPU:0, one launch (start us, length us, event | category | flops | bytes accessed | tf_op | source)
XLA Modules:
  0.0 1720.6 jit_solution(16340130157134163626)
XLA Ops:
  11.4 22.3 %all-gather = bf16[8,1,256]{2,1,0:T(2,128)(2,1)S(1)} all-gather(bf16[1,1,256]{2,1,0:T(2,128)(2,1)S(1)} %reshape.355), channel_id=1, replica_groups=mesh['dp'=8,'tensor'=4] {'dp'}, dimensions={0}, use_global_device_ids=true | all-gather | bytes 4608 | tf_op jit(solution)/shard_map/all_gather | solution.py:98
  37.9 15.1 all-gather.12.cloned.1.call-done
  56.9 37.1 %all-gather.14.cloned.1.call-done = bf16[2048,256]{1,0:T(8,128)(2,1)} async-done(((bf16[256,256]{1,0:T(8,128)(2,1)}), bf16[2048,256]{1,0:T(8,128)(2,1)}) %all-gather.14.cloned.1.call-update) | async-done | bytes 1048592 | tf_op jit(solution)/shard_map/all_gather | solution.py:93
  96.7 47.5 %all-gather.10.cloned.1.call-done = bf16[2048,512]{1,0:T(8,128)(2,1)} async-done(((bf16[256,512]{1,0:T(8,128)(2,1)}), bf16[2048,512]{1,0:T(8,128)(2,1)}) %all-gather.10.cloned.1.call-update) | async-done | bytes 2097168 | tf_op jit(solution)/shard_map/all_gather | solution.py:91
  151.6 44.1 %all-gather.16.cloned.1.call-done = bf16[512,2048]{1,0:T(8,128)(2,1)} async-done(((bf16[512,256]{1,0:T(8,128)(2,1)}), bf16[512,2048]{1,0:T(8,128)(2,1)}) %all-gather.16.cloned.1.call-update) | async-done | bytes 2097168 | tf_op jit(solution)/shard_map/all_gather | solution.py:94
  202.8 17.9 %all-gather.1 = bf16[8,1,256]{2,1,0:T(2,128)(2,1)S(1)} all-gather(bf16[1,1,256]{2,1,0:T(2,128)(2,1)S(1)} %reshape.357), channel_id=1, replica_groups=mesh['dp'=8,'tensor'=4] {'dp'}, dimensions={0}, use_global_device_ids=true | all-gather | bytes 4608 | tf_op jit(solution)/shard_map/all_gather | solution.py:99
  220.7 63.7 %all-reduce.9.cloned.1.call-done = f32[512,2048]{1,0:T(8,128)} async-done(((f32[512,2048]{1,0:T(8,128)}), f32[512,2048]{1,0:T(8,128)}) %all-reduce.9.cloned.1.call-update) | async-done | bytes 4194320 | tf_op jit(solution)/shard_map/psum | solution.py:163
  291.7 120.1 %all-gather.18.cloned.1.call-done = bf16[2048,2048]{1,0:T(8,128)(2,1)} async-done(((bf16[256,2048]{1,0:T(8,128)(2,1)}), bf16[2048,2048]{1,0:T(8,128)(2,1)}) %all-gather.18.cloned.1.call-update) | async-done | bytes 8388624 | tf_op jit(solution)/shard_map/all_gather | solution.py:95
  422.2 115.0 %all-gather.20.cloned.1.call-done = bf16[2048,2048]{1,0:T(8,128)(2,1)} async-done(((bf16[256,2048]{1,0:T(8,128)(2,1)}), bf16[2048,2048]{1,0:T(8,128)(2,1)}) %all-gather.20.cloned.1.call-update) | async-done | bytes 8388624 | tf_op jit(solution)/shard_map/all_gather | solution.py:96
  537.2 12.5 multiply_convert_fusion.2
  549.7 113.4 %all-gather.22.cloned.1.call-done = bf16[2048,2048]{1,0:T(8,128)(2,1)} async-done(((bf16[2048,256]{1,0:T(8,128)(2,1)}), bf16[2048,2048]{1,0:T(8,128)(2,1)}) %all-gather.22.cloned.1.call-update) | async-done | bytes 8388624 | tf_op jit(solution)/shard_map/all_gather | solution.py:97
  674.9 82.6 %all-reduce.11.cloned.1.call-done = f32[512,2048]{1,0:T(8,128)} async-done(((f32[512,2048]{1,0:T(8,128)}), f32[512,2048]{1,0:T(8,128)}) %all-reduce.11.cloned.1.call-update) | async-done | bytes 4194320 | tf_op jit(solution)/shard_map/psum | solution.py:175
  766.5 22.0 %all-reduce.2 = (f32[]{:T(128)}, f32[]{:T(128)}) all-reduce(f32[]{:T(128)} %fusion.56, f32[]{:T(128)} %get-tuple-element.20), channel_id=1, replica_groups=mesh['dp'=8,'tensor'=4] {'dp'}, use_global_device_ids=true, to_apply=%region_7.8 | all-reduce | flops 2 | bytes 16 | tf_op jit(solution)/shard_map/psum | solution.py:179
  789.2 12.5 multiply_convert_fusion
  820.1 81.8 %all-reduce.13.cloned.1.call-done = f32[512,2048]{1,0:T(8,128)} async-done(((f32[512,2048]{1,0:T(8,128)}), f32[512,2048]{1,0:T(8,128)}) %all-reduce.13.cloned.1.call-update) | async-done | bytes 4194320 | tf_op jit(solution)/shard_map/psum | solution.py:192
  941.0 10.8 convolution_convert_fusion
  983.0 21.7 %all-reduce.3 = (bf16[2048]{0:T(1024)(128)(2,1)S(1)}, bf16[2048]{0:T(1024)(128)(2,1)S(1)}) all-reduce(bf16[2048]{0:T(1024)(128)(2,1)S(1)} %get-tuple-element.14, bf16[2048]{0:T(1024)(128)(2,1)S(1)} %copy-done.22), channel_id=9, replica_groups=mesh['dp'=8,'tensor'=4] {'dp'}, use_global_device_ids=true, to_apply=%region_23.24.clone | all-reduce | flops 4096 | bytes 16384
  1011.4 35.4 %reduce-scatter.12.cloned.1.call-done = bf16[256,256]{1,0:T(8,128)(2,1)} async-done(((bf16[2048,256]{1,0:T(8,128)(2,1)}), bf16[256,256]{1,0:T(8,128)(2,1)}) %reduce-scatter.12.cloned.1.call-update) | async-done | bytes 131088 | tf_op jit(solution)/shard_map/reduce_scatter | solution.py:257
  1048.5 64.7 %reduce-scatter.10.cloned.1.call-done = bf16[256,256]{1,0:T(8,128)(2,1)} async-done(((bf16[2048,256]{1,0:T(8,128)(2,1)}), bf16[256,256]{1,0:T(8,128)(2,1)}) %reduce-scatter.10.cloned.1.call-update) | async-done | bytes 131088 | tf_op jit(solution)/shard_map/reduce_scatter | solution.py:254
  1114.8 68.9 %reduce-scatter.14.cloned.1.call-done = bf16[512,256]{1,0:T(8,128)(2,1)} async-done(((bf16[512,2048]{1,0:T(8,128)(2,1)}), bf16[512,256]{1,0:T(8,128)(2,1)}) %reduce-scatter.14.cloned.1.call-update) | async-done | bytes 262160 | tf_op jit(solution)/shard_map/reduce_scatter | solution.py:260
  1185.5 68.5 %reduce-scatter.8.cloned.1.call-done = bf16[256,512]{1,0:T(8,128)(2,1)} async-done(((bf16[2048,512]{1,0:T(8,128)(2,1)}), bf16[256,512]{1,0:T(8,128)(2,1)}) %reduce-scatter.8.cloned.1.call-update) | async-done | bytes 262160 | tf_op jit(solution)/shard_map/reduce_scatter | solution.py:251
  1255.7 150.1 %reduce-scatter.20.cloned.1.call-done = bf16[2048,256]{1,0:T(8,128)(2,1)} async-done(((bf16[2048,2048]{1,0:T(8,128)(2,1)}), bf16[2048,256]{1,0:T(8,128)(2,1)}) %reduce-scatter.20.cloned.1.call-update) | async-done | bytes 1048592 | tf_op jit(solution)/shard_map/reduce_scatter | solution.py:269
  1408.5 149.3 %reduce-scatter.18.cloned.1.call-done = bf16[256,2048]{1,0:T(8,128)(2,1)} async-done(((bf16[2048,2048]{1,0:T(8,128)(2,1)}), bf16[256,2048]{1,0:T(8,128)(2,1)}) %reduce-scatter.18.cloned.1.call-update) | async-done | bytes 1048592 | tf_op jit(solution)/shard_map/reduce_scatter | solution.py:266
  1560.6 148.8 %reduce-scatter.16.cloned.1.call-done = bf16[256,2048]{1,0:T(8,128)(2,1)} async-done(((bf16[2048,2048]{1,0:T(8,128)(2,1)}), bf16[256,2048]{1,0:T(8,128)(2,1)}) %reduce-scatter.16.cloned.1.call-update) | async-done | bytes 1048592 | tf_op jit(solution)/shard_map/reduce_scatter | solution.py:263
  (161 shorter events, 175.9 us)
Async XLA Ops:
  7.2 45.8 %all-gather.12.cloned.1.call-start = ((), (), s32[]{:S(2)}) async-start(), calls=%async_computation.8 | async-start | bytes 1179648 | tf_op jit(solution)/shard_map/all_gather | solution.py:92
  7.9 86.1 %all-gather.14.cloned.1.call-start = ((), (), s32[]{:S(2)}) async-start(), calls=%async_computation.9 | async-start | bytes 1179648 | tf_op jit(solution)/shard_map/all_gather | solution.py:93
  8.7 135.6 %all-gather.10.cloned.1.call-start = ((), (), s32[]{:S(2)}) async-start(), calls=%async_computation.7 | async-start | bytes 2359296 | tf_op jit(solution)/shard_map/all_gather | solution.py:91
  9.4 186.3 %all-gather.16.cloned.1.call-start = ((), (), s32[]{:S(2)}) async-start(), calls=%async_computation.10 | async-start | bytes 2359296 | tf_op jit(solution)/shard_map/all_gather | solution.py:94
  10.0 274.5 %all-reduce.9.cloned.1.call-start = ((), (), s32[]{:S(2)}) async-start(), calls=%async_computation.11 | async-start | bytes 8388608 | tf_op jit(solution)/shard_map/psum | solution.py:163
  33.7 23.3 %copy-start.23 = (f32[128]{0:T(128)}, f32[128]{0:T(128)S(1)}, u32[]{:S(2)}) copy-start(f32[128]{0:T(128)S(1)} %multiply_exponential_fusion) | copy-start | bytes 1540
  33.7 60.4 %copy-start.2 = (bf16[512,2048]{1,0:T(8,128)(2,1)S(1)}, bf16[512,2048]{1,0:T(8,128)(2,1)}, u32[]{:S(2)}) copy-start(bf16[512,2048]{1,0:T(8,128)(2,1)} %param.13) | copy-start | bytes 6291460
  35.9 108.3 %copy-start.20 = (f32[512]{0:T(512)}, f32[512]{0:T(512)S(1)}, u32[]{:S(2)}) copy-start(f32[512]{0:T(512)S(1)} %add_rsqrt_fusion.1) | copy-start | bytes 6148
  56.9 93.0 %copy-start.9 = (bf16[512,128]{0,1:T(8,128)(2,1)}, bf16[512,128]{0,1:T(8,128)(2,1)S(1)}, u32[]{:S(2)}) copy-start(bf16[512,128]{0,1:T(8,128)(2,1)S(1)} %get-tuple-element.34) | copy-start | bytes 393220
  151.6 49.0 %copy-start.12 = (bf16[2,512,256]{1,2,0:T(8,128)(2,1)}, bf16[2,512,256]{1,2,0:T(8,128)(2,1)S(1)}, u32[]{:S(2)}) copy-start(bf16[2,512,256]{1,2,0:T(8,128)(2,1)S(1)} %convolution_convert_fusion.8) | copy-start | bytes 1572868
  200.6 211.1 %all-gather.18.cloned.1.call-start = ((), (), s32[]{:S(2)}) async-start(), calls=%async_computation.12 | async-start | bytes 9437184 | tf_op jit(solution)/shard_map/all_gather | solution.py:95
  201.2 336.0 %all-gather.20.cloned.1.call-start = ((), (), s32[]{:S(2)}) async-start(), calls=%async_computation.13 | async-start | bytes 9437184 | tf_op jit(solution)/shard_map/all_gather | solution.py:96
  202.0 461.1 %all-gather.22.cloned.1.call-start = ((), (), s32[]{:S(2)}) async-start(), calls=%async_computation.14 | async-start | bytes 9437184 | tf_op jit(solution)/shard_map/all_gather | solution.py:97
  202.7 554.7 %all-reduce.11.cloned.1.call-start = ((), (), s32[]{:S(2)}) async-start(), calls=%async_computation.15 | async-start | bytes 8388608 | tf_op jit(solution)/shard_map/psum | solution.py:175
  673.6 228.3 %all-reduce.13.cloned.1.call-start = ((), (), s32[]{:S(2)}) async-start(), calls=%async_computation.16 | async-start | bytes 8388608 | tf_op jit(solution)/shard_map/psum | solution.py:192
  819.8 160.3 %all-reduce.15.cloned.1.call-start = ((), (), s32[]{:S(2)}) async-start(), calls=%async_computation.17 | async-start | bytes 4194304 | tf_op jit(solution)/shard_map/psum | solution.py:240
  928.4 118.4 %reduce-scatter.12.cloned.1.call-start = ((), (), s32[]{:S(2)}) async-start(), calls=%async_computation.20 | async-start | bytes 1179648 | tf_op jit(solution)/shard_map/reduce_scatter | solution.py:257
  930.5 182.7 %reduce-scatter.10.cloned.1.call-start = ((), (), s32[]{:S(2)}) async-start(), calls=%async_computation.19 | async-start | bytes 1179648 | tf_op jit(solution)/shard_map/reduce_scatter | solution.py:254
  932.6 251.1 %reduce-scatter.14.cloned.1.call-start = ((), (), s32[]{:S(2)}) async-start(), calls=%async_computation.21 | async-start | bytes 2359296 | tf_op jit(solution)/shard_map/reduce_scatter | solution.py:260
  938.1 315.9 %reduce-scatter.8.cloned.1.call-start = ((), (), s32[]{:S(2)}) async-start(), calls=%async_computation.18 | async-start | bytes 2359296 | tf_op jit(solution)/shard_map/reduce_scatter | solution.py:251
  940.9 464.9 %reduce-scatter.20.cloned.1.call-start = ((), (), s32[]{:S(2)}) async-start(), calls=%async_computation.24 | async-start | bytes 9437184 | tf_op jit(solution)/shard_map/reduce_scatter | solution.py:269
  951.8 606.1 %reduce-scatter.18.cloned.1.call-start = ((), (), s32[]{:S(2)}) async-start(), calls=%async_computation.23 | async-start | bytes 9437184 | tf_op jit(solution)/shard_map/reduce_scatter | solution.py:266
  961.9 747.5 %reduce-scatter.16.cloned.1.call-start = ((), (), s32[]{:S(2)}) async-start(), calls=%async_computation.22 | async-start | bytes 9437184 | tf_op jit(solution)/shard_map/reduce_scatter | solution.py:263
  972.4 10.6 copy-start.22
  (23 other events, 66.8 us)
Sparse Core Ops, SparseCore 0:
  10.1 42.7 all-gather.11
  55.1 38.8 all-gather.13
  96.1 48.0 all-gather.9
  146.1 49.5 all-gather.15
  200.7 83.6 all-reduce.8
  286.6 125.0 all-gather.17
  414.1 123.1 all-gather.19
  539.5 123.5 all-gather.21
  673.7 83.6 all-reduce.10
  819.9 81.9 all-reduce.12
  928.5 51.5 all-reduce.14
  983.4 63.4 reduce-scatter.11
  1050.6 62.4 reduce-scatter.9
  1116.6 67.0 reduce-scatter.13
  1187.1 66.8 reduce-scatter.7
  1257.4 148.3 reduce-scatter.19
  1409.7 148.0 reduce-scatter.17
  1561.3 148.0 reduce-scatter.15
where the time goes:
time: 1730 us; the launch traced here: 1720 us
  waiting for transfers between devices  1420 us (82%)
  matrix products  133 us (8%)
  blocking collectives  83.8 us (5%)
  other arithmetic  57.6 us (3%)
  between operations  19 us (1%)
    reduce_scatter x1, waiting for transfers between devices, per_device(): lax.psum_scatter(grad_wdown.astype(jnp.bfloat16), 'dp', scatter_dimension...  150 us
    reduce_scatter x1, waiting for transfers between devices, per_device(): lax.psum_scatter(grad_wup.astype(jnp.bfloat16), 'dp', scatter_dimension=0...  149 us
    reduce_scatter x1, waiting for transfers between devices, per_device(): lax.psum_scatter(grad_wgate.astype(jnp.bfloat16), 'dp', scatter_dimension...  149 us
    all_gather x1, waiting for transfers between devices, per_device(): lax.all_gather(w_gate, 'dp', axis=0, tiled=True)  120 us
    all_gather x1, waiting for transfers between devices, per_device(): lax.all_gather(w_up, 'dp', axis=0, tiled=True)  115 us
    all_gather x1, waiting for transfers between devices, per_device(): lax.all_gather(w_down, 'dp', axis=1, tiled=True)  113 us
    psum x1, waiting for transfers between devices, per_device(): lax.psum(jnp.dot(active, full_down, preferred_element_type=jnp.float32),...  82.6 us
    psum x1, waiting for transfers between devices, per_device(): lax.psum(dot_trans(grad_gate, full_gate) + dot_trans(grad_up, full_up), '...  81.8 us
  transfers between devices with their start and end apart: 18, of which 18 were waited for; matrix products, arithmetic and copies ran while one was open for 7% of the time, Pallas kernels for 0%

commit v1 on v0

v1 whole, which is shorter than its diff:
```python
import math

import jax
import jax.numpy as jnp
from jax import lax
from jax.sharding import PartitionSpec as P

MODEL_WIDTH = 2048
HEAD_SIZE = 256

EPS = 1e-06
THETA = 1000042.0
AXES = ("dp", "tensor")
BF = jnp.bfloat16
F32 = jnp.float32


class Net:
    def __init__(self):
        self.dp = lax.axis_size("dp")
        self.tensor = lax.axis_size("tensor")
        self.ring = self.dp // 2
        d = lax.axis_index("dp")
        t = lax.axis_index("tensor")
        self.z, self.y = d // 2, d % 2
        self.x, self.c = t // 2, t % 2

    def _perm(self, move):
        pairs = []
        for z in range(self.ring):
            for y in range(2):
                for x in range(2):
                    for c in range(2):
                        tz, ty, tx, tc = move(z, y, x, c)
                        pairs.append(
                            (
                                (z * 2 + y) * self.tensor + x * 2 + c,
                                ((tz % self.ring) * 2 + ty) * self.tensor + tx * 2 + tc,
                            )
                        )
        return pairs

    def flip_x(self, v):
        return lax.ppermute(v, AXES, self._perm(lambda z, y, x, c: (z, y, 1 - x, c)))

    def flip_y(self, v):
        return lax.ppermute(v, AXES, self._perm(lambda z, y, x, c: (z, 1 - y, x, c)))

    def flip_c(self, v):
        return lax.ppermute(v, AXES, self._perm(lambda z, y, x, c: (z, y, x, 1 - c)))

    def shift(self, v, by):
        return lax.ppermute(v, AXES, self._perm(lambda z, y, x, c: (z + by, y, x, c)))

    def swap_z(self, v, bit):
        return lax.ppermute(v, AXES, self._perm(lambda z, y, x, c: (z ^ bit, y, x, c)))

    def all_sum(self, v):
        v = v + self.flip_c(v)
        v = v + self.flip_x(v)
        return self.dp_sum(v)

    def dp_sum(self, v):
        v = v + self.flip_y(v)
        bit = 1
        while bit < self.ring:
            v = v + self.swap_z(v, bit)
            bit *= 2
        return v

    def ring_gather(self, v):
        ring, half = self.ring, v.shape[0] // 2
        pieces = [v] + [None] * (ring - 1)
        fwd = bwd = v
        for step in range(1, ring // 2):
            fwd = self.shift(fwd, 1)
            bwd = self.shift(bwd, -1)
            pieces[ring - step], pieces[step] = fwd, bwd
        lo = self.shift(fwd[:half], 1)
        hi = self.shift(bwd[half:], -1)
        pieces[ring // 2] = jnp.concatenate([lo, hi], axis=0)
        return pieces

    def ring_reduce(self, pieces):
        ring, half = self.ring, pieces[0].shape[0] // 2
        far = ring // 2
        fwd = self.shift(pieces[far][:half].astype(BF), 1)
        bwd = self.shift(pieces[far][half:].astype(BF), -1)
        for step in range(far - 1, 0, -1):
            up, down = pieces[step].astype(F32), pieces[ring - step].astype(F32)
            if step == far - 1:
                up = jnp.concatenate([up[:half] + fwd.astype(F32), up[half:]], axis=0)
                down = jnp.concatenate([down[:half], down[half:] + bwd.astype(F32)], axis=0)
            else:
                up = up + fwd.astype(F32)
                down = down + bwd.astype(F32)
            fwd = self.shift(up.astype(BF), 1)
            bwd = self.shift(down.astype(BF), -1)
        return pieces[0].astype(F32) + fwd.astype(F32) + bwd.astype(F32)

    def ring_gather_small(self, v):
        return [v] + [self.shift(v, -k) for k in range(1, self.ring)]

    def ring_reduce_small(self, pieces):
        total = pieces[0]
        for k in range(1, self.ring):
            total = total + self.shift(pieces[k], k)
        return total

    def y_order(self, mine, other, axis):
        first = jnp.where(self.y == 0, mine, other)
        second = jnp.where(self.y == 0, other, mine)
        return jnp.concatenate([first, second], axis=axis)

    def split_y(self, v, axis):
        n = v.shape[axis] // 2
        mine = lax.dynamic_slice_in_dim(v, self.y * n, n, axis)
        other = lax.dynamic_slice_in_dim(v, (1 - self.y) * n, n, axis)
        return mine, other

    def plane_gather(self, v):
        half = v.shape[0] // 2
        a = self.flip_x(v)
        b = self.flip_y(v)
        lo = self.flip_y(a[:half])
        hi = self.flip_x(b[half:])
        mine = jnp.concatenate([v, a, b, lo, hi], axis=0)
        other = self.flip_c(mine)
        return jnp.concatenate([mine, other], axis=0)

    def plane_reduce(self, v):
        rows = v.shape[0] // 2
        n = rows // 4
        half = n // 2
        got = self.flip_c(v[rows:].astype(BF))
        s = v[:rows] + got.astype(F32)
        own, a, b, dg = s[:n], s[n : 2 * n], s[2 * n : 3 * n], s[3 * n :]
        r1 = self.flip_x(dg[:half].astype(BF)).astype(F32)
        r2 = self.flip_y(dg[half:].astype(BF)).astype(F32)
        b = jnp.concatenate([b[:half] + r1, b[half:]], axis=0)
        a = jnp.concatenate([a[:half], a[half:] + r2], axis=0)
        ra = self.flip_x(a.astype(BF))
        rb = self.flip_y(b.astype(BF))
        return own + ra.astype(F32) + rb.astype(F32)


def after(value, *deps):
    return lax.optimization_barrier((value,) + deps)[0]


def tables(places, width):
    halfway = width // 2
    counter = jnp.arange(halfway, dtype=jnp.float32)
    inverse = jnp.exp(counter * (-2.0 * math.log(THETA) / width))
    angles = places.astype(jnp.float32)[..., None] * inverse
    return (jnp.cos(angles), jnp.sin(angles))


def rotate(value_rows, cos_table, sin_table):
    halfway = value_rows.shape[-1] // 2
    first_half = value_rows[..., :halfway]
    second_half = value_rows[..., halfway:]
    return jnp.concatenate(
        [
            first_half * cos_table - second_half * sin_table,
            second_half * cos_table + first_half * sin_table,
        ],
        axis=-1,
    )


def unrotate(grads_in, cos_table, sin_table):
    return rotate(grads_in, cos_table, -sin_table)


def rms_scale(value_rows):
    return lax.rsqrt(jnp.mean(value_rows * value_rows, axis=-1, keepdims=True) + EPS)


def norm_back(grad_normed, unit_rows, recip_rows, gain_full):
    scaled = grad_normed * gain_full
    gain_grad = jnp.sum(grad_normed * unit_rows, axis=0)
    grad_rows = recip_rows * (
        scaled - unit_rows * jnp.mean(scaled * unit_rows, axis=-1, keepdims=True)
    )
    return (gain_grad, grad_rows)


def dot(left, right):
    return jnp.dot(left, right, preferred_element_type=F32)


def token_dot(left, right):
    return lax.dot_general(
        left, right, (((0,), (0,)), ((), ())), preferred_element_type=jnp.float32
    )


def dot_trans(left, right):
    return lax.dot_general(
        left, right, (((1,), (1,)), ((), ())), preferred_element_type=jnp.float32
    )


def per_device(
    states,
    teacher,
    segments,
    positions,
    w_q,
    key_matrix,
    value_matrix,
    w_o,
    w_gate,
    w_up,
    w_down,
    norm1_gain,
    norm2_gain,
):
    net = Net()
    ring = net.ring
    seq, width = states.shape
    rp = w_q.shape[0]
    rows2 = 2 * rp
    tok = seq // 4
    fq, fk = w_q.shape[1], key_matrix.shape[1]
    heads_kv = fk // HEAD_SIZE
    rep = fq // fk
    hid = w_gate.shape[1] // 2

    def roll(v, back=False):
        start = net.z * rows2
        start = (width - start) if back else start
        twice = jnp.concatenate([v, v], axis=-1)
        return lax.dynamic_slice_in_dim(twice, start, width, axis=v.ndim - 1)

    gains = jnp.stack([norm1_gain, norm2_gain])
    gains = net.y_order(gains, net.flip_y(gains), axis=1)
    gains = jnp.concatenate(net.ring_gather_small(gains), axis=1).astype(F32)
    gain_one, gain_two = gains[0:1], gains[1:2]
    live = (segments > 0).astype(F32)
    count = net.dp_sum(jnp.full((8, 128), jnp.sum(live), F32))[0, 0]

    q2 = net.y_order(w_q, net.flip_y(w_q), axis=0)
    full_q = jnp.concatenate(net.ring_gather(q2), axis=0)
    kv = jnp.concatenate([key_matrix, value_matrix], axis=1)
    kv_mine = jnp.stack(net.ring_gather(kv))
    full_kv = net.y_order(kv_mine, net.flip_y(kv_mine), axis=1).reshape(width, 2 * fk)
    w_o, w_gate, w_up = after((w_o, w_gate, w_up), kv_mine, full_q)
    o_mine = jnp.stack(net.ring_gather(w_o), axis=1)
    o_other = net.flip_y(o_mine)
    full_o = jnp.stack(
        [jnp.where(net.y == 0, o_mine, o_other), jnp.where(net.y == 0, o_other, o_mine)], axis=2
    ).reshape(w_o.shape[0], width)

    def fetch_in(w):
        mine, other = net.split_y(w, 1)
        shard = net.y_order(mine, net.flip_y(other), axis=0)
        return jnp.concatenate(net.ring_gather(shard), axis=0)

    full_gate = fetch_in(w_gate)
    full_up = fetch_in(w_up)
    w_down = after(w_down, full_up)
    mine, other = net.split_y(w_down, 0)
    shard = net.y_order(mine, net.flip_y(other), axis=1)
    full_down = jnp.concatenate(net.ring_gather(shard), axis=1)

    inputs = roll(states).astype(F32)
    recip_one = rms_scale(inputs)
    unit_one = inputs * recip_one
    normed = (unit_one * gain_one).astype(BF)
    query_rows = dot(normed, full_q).reshape(seq, heads_kv, rep, HEAD_SIZE).transpose(1, 2, 0, 3)
    kv_rows = dot(normed, full_kv)
    keys = kv_rows[:, :fk].reshape(seq, heads_kv, HEAD_SIZE).transpose(1, 0, 2)
    value_rows = kv_rows[:, fk:].astype(BF).reshape(seq, heads_kv, HEAD_SIZE).transpose(1, 0, 2)
    cos_table, sin_table = tables(positions, HEAD_SIZE)
    rotated_query = rotate(query_rows, cos_table, sin_table).astype(BF)
    rotated_k = rotate(keys, cos_table, sin_table).astype(BF)
    score_scale = 1.0 / math.sqrt(HEAD_SIZE)
    key_index = jnp.arange(seq, dtype=jnp.int32)
    scores = (
        jnp.einsum("krbe,kte->krbt", rotated_query, rotated_k, preferred_element_type=F32)
        * score_scale
    )
    allowed = (segments[:, None] == segments[None, :]) & (key_index[None, :] <= key_index[:, None])
    scores = jnp.where(allowed, scores, -1e30)
    largest = jnp.max(scores, axis=-1, keepdims=True)
    exponent = jnp.exp(scores - largest)
    weights = exponent / jnp.sum(exponent, axis=-1, keepdims=True)
    weights_low = weights.astype(BF)
    attended = jnp.einsum("krbt,kte->krbe", weights_low, value_rows, preferred_element_type=F32)
    attended = attended.transpose(2, 0, 1, 3).reshape(seq, fq).astype(BF)
    partial = dot(attended, full_o).reshape(2, 2, tok, width)

    keep = lax.dynamic_index_in_dim(partial, net.c, 1, keepdims=False)
    send = lax.dynamic_index_in_dim(partial, 1 - net.c, 1, keepdims=False)
    partial = keep + net.flip_c(send.astype(BF)).astype(F32)
    keep = lax.dynamic_index_in_dim(partial, net.x, 0, keepdims=False)
    send = lax.dynamic_index_in_dim(partial, 1 - net.x, 0, keepdims=False)
    attn_sum = keep + net.flip_x(send.astype(BF)).astype(F32)

    first_token = (net.x * 2 + net.c) * tok
    my_inputs = roll(lax.dynamic_slice_in_dim(states, first_token, tok, 0)).astype(F32)
    my_teacher = roll(lax.dynamic_slice_in_dim(teacher, first_token, tok, 0)).astype(F32)
    my_live = lax.dynamic_slice_in_dim(live, first_token, tok, 0)

    hidden = my_inputs + attn_sum
    recip_two = rms_scale(hidden)
    unit_two = hidden * recip_two
    normed_two = net.plane_gather((unit_two * gain_two).astype(BF))
    gate_proj = dot(normed_two, full_gate)
    up_proj = dot(normed_two, full_up)
    sigmoid_gate = jax.nn.sigmoid(gate_proj)
    silu_gate = gate_proj * sigmoid_gate
    active = (silu_gate * up_proj).astype(BF)
    mlp_sum = net.plane_reduce(dot(active, full_down))
    output = hidden + mlp_sum
    error = (output - my_teacher) * my_live[:, None]
    factor = net.dp * seq / count
    grad_out = error * factor
    squares = jnp.sum(error * error)

    def share_tokens(v):
        def order(flag, mine, other, axis):
            return jnp.concatenate(
                [jnp.where(flag == 0, mine, other), jnp.where(flag == 0, other, mine)], axis=axis
            )

        v = order(net.x, v, net.flip_x(v), 0).reshape(2, tok, width)
        v = jnp.stack([v, net.flip_c(v)])
        v = jnp.where(net.c == 0, v, v[::-1])
        return v.transpose(1, 0, 2, 3).reshape(seq, width)

    out_states = roll(share_tokens(output.astype(BF)), back=True)

    grad_out_low = net.plane_gather(grad_out.astype(BF))
    grad_wdown = token_dot(active, grad_out_low)
    grad_active = dot_trans(grad_out_low, full_down)
    grad_gate = (
        grad_active * up_proj * sigmoid_gate * (1.0 + gate_proj * (1.0 - sigmoid_gate))
    ).astype(BF)
    grad_up = (grad_active * silu_gate).astype(BF)
    grad_wgate = token_dot(normed_two, grad_gate)
    grad_wup = token_dot(normed_two, grad_up)
    back_two = net.plane_reduce(dot_trans(grad_gate, full_gate) + dot_trans(grad_up, full_up))
    gain_two_grad, hidden_from_norm = norm_back(back_two, unit_two, recip_two, gain_two)
    grad_hidden = grad_out + hidden_from_norm
    grad_hidden_low = share_tokens(grad_hidden.astype(BF))

    grad_wo = token_dot(attended, grad_hidden_low)
    grad_attended = dot_trans(grad_hidden_low, full_o).astype(BF)
    grad_attended = grad_attended.reshape(seq, heads_kv, rep, HEAD_SIZE).transpose(1, 2, 0, 3)
    grad_weights = jnp.einsum(
        "krbe,kte->krbt", grad_attended, value_rows, preferred_element_type=F32
    )
    inner = jnp.sum(weights * grad_weights, axis=-1, keepdims=True)
    grad_scores = (weights * (grad_weights - inner)).astype(BF)
    grad_q = (
        jnp.einsum("krbt,kte->krbe", grad_scores, rotated_k, preferred_element_type=F32)
        * score_scale
    )
    grad_k = (
        jnp.einsum("krbt,krbe->kte", grad_scores, rotated_query, preferred_element_type=F32)
        * score_scale
    )
    grad_v = jnp.einsum("krbt,krbe->kte", weights_low, grad_attended, preferred_element_type=F32)
    grad_q = unrotate(grad_q, cos_table, sin_table).astype(BF)
    grad_q = grad_q.transpose(2, 0, 1, 3).reshape(seq, fq)
    grad_k = unrotate(grad_k, cos_table, sin_table).astype(BF)
    grad_k = grad_k.transpose(1, 0, 2).reshape(seq, fk)
    grad_v = grad_v.astype(BF).transpose(1, 0, 2).reshape(seq, fk)
    grad_kv = jnp.concatenate([grad_k, grad_v], axis=1)
    grad_wq = token_dot(normed, grad_q)
    grad_wkv = token_dot(normed, grad_kv)
    back_one = (dot_trans(grad_q, full_q) + dot_trans(grad_kv, full_kv)).reshape(2, 2, tok, width)
    keep = lax.dynamic_index_in_dim(back_one, net.c, 1, keepdims=False)
    send = lax.dynamic_index_in_dim(back_one, 1 - net.c, 1, keepdims=False)
    back_one = (keep + net.flip_c(send.astype(BF)).astype(F32)).astype(BF)
    back_one = back_one.astype(F32) + net.flip_x(back_one).astype(F32)

    def of_core(v):
        v = v.reshape((2, 2, tok) + v.shape[1:])
        return lax.dynamic_index_in_dim(v, net.c, 1, keepdims=False)

    unit_mine, recip_mine = of_core(unit_one), of_core(recip_one)
    scaled = back_one * gain_one
    gain_one_grad = jnp.sum(back_one * unit_mine, axis=(0, 1))
    grad_input = of_core(grad_hidden_low).astype(F32) + recip_mine * (
        scaled - unit_mine * jnp.mean(scaled * unit_mine, axis=-1, keepdims=True)
    )
    grad_input = jnp.stack([grad_input, net.flip_c(grad_input)])
    grad_input = jnp.where(net.c == 0, grad_input, grad_input[::-1])
    grad_input = roll(grad_input.transpose(1, 0, 2, 3).reshape(seq, width), back=True)

    def blocks(v, axis):
        n = v.shape[axis] // ring
        return [lax.slice_in_dim(v, k * n, (k + 1) * n, axis=axis) for k in range(ring)]

    def send_in(g):
        part = net.ring_reduce(blocks(g, 0))
        mine, other = net.split_y(part, 0)
        return net.y_order(mine, net.flip_y(other.astype(BF)).astype(F32), axis=1)

    part = net.ring_reduce(blocks(grad_wdown, 1))
    mine, other = net.split_y(part, 1)
    result_down = net.y_order(mine, net.flip_y(other.astype(BF)).astype(F32), axis=0)
    result_gate = send_in(grad_wgate)
    result_up = send_in(grad_wup)

    part = net.ring_reduce(blocks(grad_wo, 1))
    mine, other = net.split_y(part, 1)
    result_o = mine + net.flip_y(other.astype(BF)).astype(F32)

    part = net.ring_reduce(blocks(grad_wq, 0))
    mine, other = net.split_y(part, 0)
    result_q = mine + net.flip_y(other.astype(BF)).astype(F32)

    mine, other = net.split_y(grad_wkv.reshape(ring, 2, rp, 2 * fk), 1)
    part = mine + net.flip_y(other.astype(BF)).astype(F32)
    result_kv = net.ring_reduce([part[k, 0] for k in range(ring)])
    result_k, result_v = result_kv[:, :fk], result_kv[:, fk:]

    def gain_sum(v, both_x):
        v = v.reshape(ring, 2, rp)
        v = v + net.flip_c(v)
        if both_x:
            v = v + net.flip_x(v)
        mine, other = net.split_y(v, 1)
        v = (mine + net.flip_y(other))[:, 0]
        return net.ring_reduce_small([v[k] for k in range(ring)])

    result_g2 = gain_sum(gain_two_grad, True)
    result_g1 = gain_sum(gain_one_grad, False)
    squares_sum = net.all_sum(jnp.full((8, 128), squares, F32))[0, 0]
    loss_value = squares_sum / (count * width)
    return (
        out_states,
        grad_input,
        loss_value,
        result_q,
        result_k,
        result_v,
        result_o,
        result_gate,
        result_up,
        result_down,
        result_g1,
        result_g2,
    )


def solution(mesh):
    in_specs = (
        P("dp", None),
        P("dp", None),
        P("dp"),
        P("dp"),
        P("dp", "tensor"),
        P("dp", "tensor"),
        P("dp", "tensor"),
        P("tensor", "dp"),
        P("dp", "tensor"),
        P("dp", "tensor"),
        P("tensor", "dp"),
        P("dp"),
        P("dp"),
    )
    out_specs = (
        P("dp", None),
        P("dp", None),
        P(),
        P("dp", "tensor"),
        P("dp", "tensor"),
        P("dp", "tensor"),
        P("tensor", "dp"),
        P("dp", "tensor"),
        P("dp", "tensor"),
        P("tensor", "dp"),
        P("dp"),
        P("dp"),
    )
    return jax.shard_map(
        per_device, mesh=mesh, in_specs=in_specs, out_specs=out_specs, check_vma=False
    )
```

time: 1730 us -> 894 us (0.52)
  waiting for transfers between devices: 1420 us -> 486 us
  starting transfers between devices: 1.76 us -> 144 us
  blocking collectives: 83.8 us -> 0 us
  local copies, waits for them, and re-layouts: 10.1 us -> 65.8 us
  matrix products: 133 us -> 91.3 us
  other arithmetic: 57.6 us -> 90.6 us
    reduce_scatter x7 -> x0, waiting for transfers between devices: 686 us -> none  [the longest x1 150 us: per_device(): lax.psum_scatter(grad_wdown.astype(jnp.bfloat16), 'dp', scatter_dimension...]
    all_gather x7 -> x0, waiting for transfers between devices: 492 us -> none  [the longest x1 120 us: per_device(): lax.all_gather(w_gate, 'dp', axis=0, tiled=True)]
    ppermute x0 -> x112, waiting for transfers between devices: none -> 486 us  [the longest x57 384 us: shift(): lax.ppermute(v, AXES, self._perm(lambda z, y, x, c: (z + by, y, x, c)))]
    psum x4 -> x0, waiting for transfers between devices: 233 us -> none  [the longest x1 82.6 us: per_device(): lax.psum(jnp.dot(active, full_down, preferred_element_type=jnp.float32),...]
    ppermute x0 -> x112, starting transfers between devices: none -> 144 us  [the longest x57 99.2 us: shift(): lax.ppermute(v, AXES, self._perm(lambda z, y, x, c: (z + by, y, x, c)))]
    all_gather x2 -> x0, blocking collectives: 40.2 us -> none  [the longest x1 22.3 us: per_device(): lax.all_gather(norm1_gain, 'dp', axis=0, tiled=True)]
    dot_general x11 -> x9, matrix products: 49.9 us -> 26.8 us  [the longest x6 22.9 us: dot(): return jnp.dot(left, right, preferred_element_type=F32)]
    psum x1 -> x0, blocking collectives: 22 us -> none  [per_device(): lax.psum((jnp.sum(error * error), jnp.sum(live_mask)), 'dp')]
  transfers between devices with their start and end apart: 18 -> 112, of which waited for: 18 -> 62; matrix products, arithmetic and copies ran while one was open for 7% -> 15% of each run, Pallas kernels for 0% -> 0%
where the time goes in v1:
time: 894 us; the launch traced here: 883 us
  waiting for transfers between devices  486 us (54%)
  starting transfers between devices  144 us (16%)
  matrix products  91.3 us (10%)
  other arithmetic  90.6 us (10%)
  local copies, waits for them, and re-layouts  65.8 us (7%)
    ppermute x57, waiting for transfers between devices, shift(): lax.ppermute(v, AXES, self._perm(lambda z, y, x, c: (z + by, y, x, c)))  384 us
    ppermute x57, starting transfers between devices, shift(): lax.ppermute(v, AXES, self._perm(lambda z, y, x, c: (z + by, y, x, c)))  99.2 us
    ppermute x25, waiting for transfers between devices, flip_y(): lax.ppermute(v, AXES, self._perm(lambda z, y, x, c: (z, 1 - y, x, c)))  60.1 us
    dot_general x6, matrix products, dot_trans(): lax.dot_general(left, right, (((1,), (1,)), ((), ())), preferred_element_...  33.9 us
    ppermute x14, waiting for transfers between devices, flip_x(): lax.ppermute(v, AXES, self._perm(lambda z, y, x, c: (z, y, 1 - x, c)))  33.6 us
    dot_general x6, matrix products, token_dot(): lax.dot_general(left, right, (((0,), (0,)), ((), ())), preferred_element_...  27.4 us
    dot_general x6, matrix products, dot(): return jnp.dot(left, right, preferred_element_type=F32)  22.9 us
    unnamed x181, local copies, waits for them, and re-layouts  22.5 us
  transfers between devices with their start and end apart: 112, of which 62 were waited for; matrix products, arithmetic and copies ran while one was open for 15% of the time, Pallas kernels for 0%

profile of v1, /device:TPU:0, one launch (start us, length us, event | category | flops | bytes accessed | tf_op | source)
XLA Modules:
  0.0 883.5 jit_solution(8805394565025062987)
XLA Ops:
  35.4 20.1 %collective-permute-done.11 = bf16[128,512]{1,0:T(8,128)(2,1)S(1)} collective-permute-done((bf16[128,512]{1,0:T(8,128)(2,1)S(1)}, bf16[128,512]{1,0:T(8,128)(2,1)S(1)}, u32[]{:S(2)}, u32[]{:S(2)}) %collective-permute-start.11) | collective-permute-done | bytes 131104 | tf_op jit(solution)/shard_map/ppermute | solution.py:53
  113.7 13.3 %collective-permute-done.18 = bf16[512,4,256]{2,0,1:T(8,128)(2,1)} collective-permute-done((bf16[512,4,256]{2,0,1:T(8,128)(2,1)}, bf16[512,4,256]{2,0,1:T(8,128)(2,1)}, u32[]{:S(2)}, u32[]{:S(2)}) %collective-permute-start.18) | collective-permute-done | bytes 1048608 | tf_op jit(solution)/shard_map/ppermute | solution.py:47
  190.9 9.6 %collective-permute-done.22 = bf16[128,2048]{1,0:T(8,128)(2,1)S(1)} collective-permute-done((bf16[128,2048]{1,0:T(8,128)(2,1)S(1)}, bf16[128,2048]{1,0:T(8,128)(2,1)S(1)}, u32[]{:S(2)}, u32[]{:S(2)}) %collective-permute-start.22) | collective-permute-done | bytes 524320 | tf_op jit(solution)/shard_map/ppermute | solution.py:47
  211.3 18.6 %collective-permute-done.28 = bf16[512,1024]{1,0:T(8,128)(2,1)S(1)} collective-permute-done((bf16[512,1024]{1,0:T(8,128)(2,1)S(1)}, bf16[512,1024]{1,0:T(8,128)(2,1)S(1)}, u32[]{:S(2)}, u32[]{:S(2)}) %collective-permute-start.28) | collective-permute-done | bytes 1048608 | tf_op jit(solution)/shard_map/ppermute | solution.py:53
  230.5 14.3 %collective-permute-done.27 = bf16[512,1024]{1,0:T(8,128)(2,1)S(1)} collective-permute-done((bf16[512,1024]{1,0:T(8,128)(2,1)S(1)}, bf16[512,1024]{1,0:T(8,128)(2,1)S(1)}, u32[]{:S(2)}, u32[]{:S(2)}) %collective-permute-start.27) | collective-permute-done | bytes 1048608 | tf_op jit(solution)/shard_map/ppermute | solution.py:53
  252.9 25.5 %collective-permute-done.37 = bf16[1024,512]{1,0:T(8,128)(2,1)S(1)} collective-permute-done((bf16[1024,512]{1,0:T(8,128)(2,1)S(1)}, bf16[1024,512]{1,0:T(8,128)(2,1)S(1)}, u32[]{:S(2)}, u32[]{:S(2)}) %collective-permute-start.37) | collective-permute-done | bytes 1048608 | tf_op jit(solution)/shard_map/ppermute | solution.py:53
  286.1 14.8 %collective-permute-done.30 = bf16[256,1024]{1,0:T(8,128)(2,1)S(1)} collective-permute-done((bf16[256,1024]{1,0:T(8,128)(2,1)S(1)}, bf16[256,1024]{1,0:T(8,128)(2,1)S(1)}, u32[]{:S(2)}, u32[]{:S(2)}) %collective-permute-start.30) | collective-permute-done | bytes 524320 | tf_op jit(solution)/shard_map/ppermute | solution.py:53
  367.4 10.9 %collective-permute-done.51 = bf16[128,2048]{1,0:T(8,128)(2,1)} collective-permute-done((bf16[128,2048]{1,0:T(8,128)(2,1)S(1)}, bf16[128,2048]{1,0:T(8,128)(2,1)}, u32[]{:S(2)}, u32[]{:S(2)}) %collective-permute-start.51) | collective-permute-done | bytes 524320 | tf_op jit(solution)/shard_map/ppermute | solution.py:44
  434.3 10.7 %multiply_convert_fusion.1 = (bf16[1024,1024]{1,0:T(8,128)(2,1)}, bf16[1024,1024]{1,0:T(8,128)(2,1)S(1)}) fusion(f32[1024,1024]{1,0:T(8,128)} %copy-done.75, f32[1024,1024]{1,0:T(8,128)} %get-tuple-element.167, bf16[1024,2048]{1,0:T(8,128)(2,1)} %constant_dynamic-update-slice_fusion.45, bf16[1024,2048]{1,0:T(8,128)(2,1)S(1)} %copy-done.62), kind=kOutput, calls=%fused_computation.18 | convolution fusion | flops 4308598784 | bytes 20971520 | tf_op jit(solution)/shard_map/dot_general | solution.py:200
  446.3 9.0 %fusion.132 = f32[1024,2048]{1,0:T(8,128)} fusion(bf16[1024,1024]{1,0:T(8,128)(2,1)S(1)} %get-tuple-element.67, bf16[2048,1024]{1,0:T(8,128)(2,1)} %copy-done.64), kind=kOutput, calls=%fused_computation.365 | convolution fusion | flops 4294967296 | bytes 14680064 | tf_op jit(solution)/shard_map/dot_general | solution.py:200
  455.3 8.6 fusion.128
  471.9 10.2 %convolution_add_fusion = f32[1024,2048]{1,0:T(8,128)} fusion(f32[1024,2048]{1,0:T(8,128)} %fusion.132, bf16[1024,1024]{1,0:T(8,128)(2,1)S(1)} %copy-done.73, bf16[2048,1024]{1,0:T(8,128)(2,1)} %copy-done.65), kind=kOutput, calls=%fused_computation.23 | convolution fusion | flops 4297064448 | bytes 23068672 | tf_op jit(solution)/shard_map/dot_general | solution.py:200
  494.7 8.5 collective-permute-done.86
  503.1 10.2 %collective-permute-done.88 = bf16[256,1024]{1,0:T(8,128)(2,1)S(1)} collective-permute-done((bf16[256,1024]{1,0:T(8,128)(2,1)S(1)}, bf16[256,1024]{1,0:T(8,128)(2,1)S(1)}, u32[]{:S(2)}, u32[]{:S(2)}) %collective-permute-start.88) | collective-permute-done | bytes 524320 | tf_op jit(solution)/shard_map/ppermute | solution.py:53
  515.7 10.0 %collective-permute-done.96 = bf16[512,512]{1,0:T(8,128)(2,1)S(1)} collective-permute-done((bf16[512,512]{1,0:T(8,128)(2,1)S(1)}, bf16[512,512]{1,0:T(8,128)(2,1)S(1)}, u32[]{:S(2)}, u32[]{:S(2)}) %collective-permute-start.96) | collective-permute-done | bytes 524320 | tf_op jit(solution)/shard_map/ppermute | solution.py:53
  525.7 10.1 %collective-permute-done.98 = bf16[512,512]{1,0:T(8,128)(2,1)S(1)} collective-permute-done((bf16[512,512]{1,0:T(8,128)(2,1)S(1)}, bf16[512,512]{1,0:T(8,128)(2,1)S(1)}, u32[]{:S(2)}, u32[]{:S(2)}) %collective-permute-start.98) | collective-permute-done | bytes 524320 | tf_op jit(solution)/shard_map/ppermute | solution.py:53
  548.2 10.1 %collective-permute-done.93 = bf16[256,1024]{1,0:T(8,128)(2,1)S(1)} collective-permute-done((bf16[256,1024]{1,0:T(8,128)(2,1)S(1)}, bf16[256,1024]{1,0:T(8,128)(2,1)S(1)}, u32[]{:S(2)}, u32[]{:S(2)}) %collective-permute-start.93) | collective-permute-done | bytes 524320 | tf_op jit(solution)/shard_map/ppermute | solution.py:53
  564.3 17.6 %collective-permute-done.87 = bf16[512,1024]{1,0:T(8,128)(2,1)S(1)} collective-permute-done((bf16[512,1024]{1,0:T(8,128)(2,1)S(1)}, bf16[512,1024]{1,0:T(8,128)(2,1)S(1)}, u32[]{:S(2)}, u32[]{:S(2)}) %collective-permute-start.87) | collective-permute-done | bytes 1048608 | tf_op jit(solution)/shard_map/ppermute | solution.py:53
  581.9 21.3 %collective-permute-done.89 = bf16[512,1024]{1,0:T(8,128)(2,1)S(1)} collective-permute-done((bf16[512,1024]{1,0:T(8,128)(2,1)S(1)}, bf16[512,1024]{1,0:T(8,128)(2,1)S(1)}, u32[]{:S(2)}, u32[]{:S(2)}) %collective-permute-start.89) | collective-permute-done | bytes 1048608 | tf_op jit(solution)/shard_map/ppermute | solution.py:53
  607.8 64.1 %collective-permute-done.92 = bf16[512,1024]{1,0:T(8,128)(2,1)S(1)} collective-permute-done((bf16[512,1024]{1,0:T(8,128)(2,1)}, bf16[512,1024]{1,0:T(8,128)(2,1)S(1)}, u32[]{:S(2)}, u32[]{:S(2)}) %collective-permute-start.92) | collective-permute-done | bytes 1048608 | tf_op jit(solution)/shard_map/ppermute | solution.py:53
  672.2 20.3 %collective-permute-done.94 = bf16[512,1024]{1,0:T(8,128)(2,1)} collective-permute-done((bf16[512,1024]{1,0:T(8,128)(2,1)}, bf16[512,1024]{1,0:T(8,128)(2,1)}, u32[]{:S(2)}, u32[]{:S(2)}) %collective-permute-start.94) | collective-permute-done | bytes 1048608 | tf_op jit(solution)/shard_map/ppermute | solution.py:53
  801.8 10.4 %collective-permute-done.82 = bf16[512,512]{1,0:T(8,128)(2,1)S(1)} collective-permute-done((bf16[512,512]{1,0:T(8,128)(2,1)S(1)}, bf16[512,512]{1,0:T(8,128)(2,1)S(1)}, u32[]{:S(2)}, u32[]{:S(2)}) %collective-permute-start.82) | collective-permute-done | bytes 524320 | tf_op jit(solution)/shard_map/ppermute | solution.py:53
  812.2 13.1 %collective-permute-start.74 = (bf16[512,512]{1,0:T(8,128)(2,1)S(1)}, bf16[512,512]{1,0:T(8,128)(2,1)S(1)}, u32[]{:S(2)}, u32[]{:S(2)}) collective-permute-start(bf16[512,512]{1,0:T(8,128)(2,1)S(1)} %pad_maximum_fusion.29), channel_id=1, source_target_pairs={{0,24},{1,25},{2,26},{3,27},{4,28},{5,29},{6,30},{7,31},{8,0},{9,1... | collective-permute-start | bytes 1572872 | tf_op jit(solution)/shard_map/ppermute | solution.py:53
  834.8 8.4 collective-permute-done.74
  (602 shorter events, 507.8 us)
Async XLA Ops:
  77.5 66.6 %collective-permute-start.26 = (bf16[256,1024]{1,0:T(8,128)(2,1)}, bf16[256,1024]{1,0:T(8,128)(2,1)}, u32[]{:S(2)}, u32[]{:S(2)}) collective-permute-start(bf16[256,1024]{1,0:T(8,128)(2,1)} %constant_dynamic-slice_fusion.8), channel_id=1, source_target_pairs={{0,4},{1,5},{2,6},{3,7},{4,0},{5,1},{6,2},{7,3},{8,12},{9,13},{10,... | collective-permute-start | bytes 1572872 | tf_op jit(solution)/shard_map/ppermute | solution.py:47
  111.4 39.7 %collective-permute-start.32 = (bf16[512,1024]{1,0:T(8,128)(2,1)}, bf16[512,1024]{1,0:T(8,128)(2,1)}, u32[]{:S(2)}, u32[]{:S(2)}) collective-permute-start(bf16[512,1024]{1,0:T(8,128)(2,1)} %pad_maximum_fusion.11), channel_id=1, source_target_pairs={{0,24},{1,25},{2,26},{3,27},{4,28},{5,29},{6,30},{7,31},{8,0},{9,1... | collective-permute-start | bytes 3145736 | tf_op jit(solution)/shard_map/ppermute | solution.py:53
  178.8 66.0 %collective-permute-start.27 = (bf16[512,1024]{1,0:T(8,128)(2,1)S(1)}, bf16[512,1024]{1,0:T(8,128)(2,1)S(1)}, u32[]{:S(2)}, u32[]{:S(2)}) collective-permute-start(bf16[512,1024]{1,0:T(8,128)(2,1)S(1)} %pad_maximum_fusion.10), channel_id=1, source_target_pairs={{0,24},{1,25},{2,26},{3,27},{4,28},{5,29},{6,30},{7,31},{8,0},{9,1... | collective-permute-start | bytes 3145736 | tf_op jit(solution)/shard_map/ppermute | solution.py:53
  181.8 48.1 %collective-permute-start.28 = (bf16[512,1024]{1,0:T(8,128)(2,1)S(1)}, bf16[512,1024]{1,0:T(8,128)(2,1)S(1)}, u32[]{:S(2)}, u32[]{:S(2)}) collective-permute-start(bf16[512,1024]{1,0:T(8,128)(2,1)S(1)} %pad_maximum_fusion.10), channel_id=1, source_target_pairs={{0,8},{1,9},{2,10},{3,11},{4,12},{5,13},{6,14},{7,15},{8,16},{9,17... | collective-permute-start | bytes 3145736 | tf_op jit(solution)/shard_map/ppermute | solution.py:53
  207.1 108.7 %collective-permute-start.25 = (bf16[512,2048]{1,0:T(8,128)(2,1)S(1)}, bf16[512,2048]{1,0:T(8,128)(2,1)S(1)}, u32[]{:S(2)}, u32[]{:S(2)}) collective-permute-start(bf16[512,2048]{1,0:T(8,128)(2,1)S(1)} %get-tuple-element.147), channel_id=1, source_target_pairs={{0,1},{1,0},{2,3},{3,2},{4,5},{5,4},{6,7},{7,6},{8,9},{9,8},{10,11... | collective-permute-start | bytes 6291464 | tf_op jit(solution)/shard_map/ppermute | solution.py:50
  207.4 44.9 %collective-permute-start.38 = (bf16[1024,512]{1,0:T(8,128)(2,1)S(1)}, bf16[1024,512]{1,0:T(8,128)(2,1)S(1)}, u32[]{:S(2)}, u32[]{:S(2)}) collective-permute-start(bf16[1024,512]{1,0:T(8,128)(2,1)S(1)} %pad_maximum_fusion.12), channel_id=1, source_target_pairs={{0,8},{1,9},{2,10},{3,11},{4,12},{5,13},{6,14},{7,15},{8,16},{9,17... | collective-permute-start | bytes 3145736 | tf_op jit(solution)/shard_map/ppermute | solution.py:53
  208.4 70.0 %collective-permute-start.37 = (bf16[1024,512]{1,0:T(8,128)(2,1)S(1)}, bf16[1024,512]{1,0:T(8,128)(2,1)S(1)}, u32[]{:S(2)}, u32[]{:S(2)}) collective-permute-start(bf16[1024,512]{1,0:T(8,128)(2,1)S(1)} %pad_maximum_fusion.12), channel_id=1, source_target_pairs={{0,24},{1,25},{2,26},{3,27},{4,28},{5,29},{6,30},{7,31},{8,0},{9,1... | collective-permute-start | bytes 3145736 | tf_op jit(solution)/shard_map/ppermute | solution.py:53
  230.0 56.1 %collective-permute-start.29 = (bf16[256,1024]{1,0:T(8,128)(2,1)S(1)}, bf16[256,1024]{1,0:T(8,128)(2,1)S(1)}, u32[]{:S(2)}, u32[]{:S(2)}) collective-permute-start(bf16[256,1024]{1,0:T(8,128)(2,1)S(1)} %slice.549), channel_id=1, source_target_pairs={{0,8},{1,9},{2,10},{3,11},{4,12},{5,13},{6,14},{7,15},{8,16},{9,17... | collective-permute-start | bytes 1572872 | tf_op jit(solution)/shard_map/ppermute | solution.py:53
  244.9 56.0 %collective-permute-start.30 = (bf16[256,1024]{1,0:T(8,128)(2,1)S(1)}, bf16[256,1024]{1,0:T(8,128)(2,1)S(1)}, u32[]{:S(2)}, u32[]{:S(2)}) collective-permute-start(bf16[256,1024]{1,0:T(8,128)(2,1)S(1)} %slice.550), channel_id=1, source_target_pairs={{0,24},{1,25},{2,26},{3,27},{4,28},{5,29},{6,30},{7,31},{8,0},{9,1... | collective-permute-start | bytes 1572872 | tf_op jit(solution)/shard_map/ppermute | solution.py:53
  252.3 56.2 %collective-permute-start.39 = (bf16[512,512]{1,0:T(8,128)(2,1)S(1)}, bf16[512,512]{1,0:T(8,128)(2,1)S(1)}, u32[]{:S(2)}, u32[]{:S(2)}) collective-permute-start(bf16[512,512]{1,0:T(8,128)(2,1)S(1)} %slice.553), channel_id=1, source_target_pairs={{0,8},{1,9},{2,10},{3,11},{4,12},{5,13},{6,14},{7,15},{8,16},{9,17... | collective-permute-start | bytes 1572872 | tf_op jit(solution)/shard_map/ppermute | solution.py:53
  278.5 36.9 %collective-permute-start.40 = (bf16[512,512]{1,0:T(8,128)(2,1)S(1)}, bf16[512,512]{1,0:T(8,128)(2,1)S(1)}, u32[]{:S(2)}, u32[]{:S(2)}) collective-permute-start(bf16[512,512]{1,0:T(8,128)(2,1)S(1)} %slice.554), channel_id=1, source_target_pairs={{0,24},{1,25},{2,26},{3,27},{4,28},{5,29},{6,30},{7,31},{8,0},{9,1... | collective-permute-start | bytes 1572872 | tf_op jit(solution)/shard_map/ppermute | solution.py:53
  484.7 121.8 %collective-permute-start.56 = (bf16[512,2048]{1,0:T(8,128)(2,1)S(1)}, bf16[512,2048]{1,0:T(8,128)(2,1)S(1)}, u32[]{:S(2)}, u32[]{:S(2)}) collective-permute-start(bf16[512,2048]{1,0:T(8,128)(2,1)S(1)} %slice.775), channel_id=1, source_target_pairs={{0,1},{1,0},{2,3},{3,2},{4,5},{5,4},{6,7},{7,6},{8,9},{9,8},{10,11... | collective-permute-start | bytes 6291464 | tf_op jit(solution)/shard_map/ppermute | solution.py:50
  490.6 45.2 %collective-permute-start.98 = (bf16[512,512]{1,0:T(8,128)(2,1)S(1)}, bf16[512,512]{1,0:T(8,128)(2,1)S(1)}, u32[]{:S(2)}, u32[]{:S(2)}) collective-permute-start(bf16[512,512]{1,0:T(8,128)(2,1)S(1)} %get-tuple-element.70), channel_id=1, source_target_pairs={{0,24},{1,25},{2,26},{3,27},{4,28},{5,29},{6,30},{7,31},{8,0},{9,1... | collective-permute-start | bytes 1572872 | tf_op jit(solution)/shard_map/ppermute | solution.py:53
  503.1 45.0 %collective-permute-start.91 = (bf16[256,1024]{1,0:T(8,128)(2,1)S(1)}, bf16[256,1024]{1,0:T(8,128)(2,1)S(1)}, u32[]{:S(2)}, u32[]{:S(2)}) collective-permute-start(bf16[256,1024]{1,0:T(8,128)(2,1)S(1)} %get-tuple-element.73), channel_id=1, source_target_pairs={{0,8},{1,9},{2,10},{3,11},{4,12},{5,13},{6,14},{7,15},{8,16},{9,17... | collective-permute-start | bytes 1572872 | tf_op jit(solution)/shard_map/ppermute | solution.py:53
  513.3 44.9 %collective-permute-start.93 = (bf16[256,1024]{1,0:T(8,128)(2,1)S(1)}, bf16[256,1024]{1,0:T(8,128)(2,1)S(1)}, u32[]{:S(2)}, u32[]{:S(2)}) collective-permute-start(bf16[256,1024]{1,0:T(8,128)(2,1)S(1)} %get-tuple-element.74), channel_id=1, source_target_pairs={{0,24},{1,25},{2,26},{3,27},{4,28},{5,29},{6,30},{7,31},{8,0},{9,1... | collective-permute-start | bytes 1572872 | tf_op jit(solution)/shard_map/ppermute | solution.py:53
  525.7 56.3 %collective-permute-start.87 = (bf16[512,1024]{1,0:T(8,128)(2,1)S(1)}, bf16[512,1024]{1,0:T(8,128)(2,1)S(1)}, u32[]{:S(2)}, u32[]{:S(2)}) collective-permute-start(bf16[512,1024]{1,0:T(8,128)(2,1)S(1)} %pad_maximum_fusion.15), channel_id=1, source_target_pairs={{0,8},{1,9},{2,10},{3,11},{4,12},{5,13},{6,14},{7,15},{8,16},{9,17... | collective-permute-start | bytes 3145736 | tf_op jit(solution)/shard_map/ppermute | solution.py:53
  535.8 67.4 %collective-permute-start.89 = (bf16[512,1024]{1,0:T(8,128)(2,1)S(1)}, bf16[512,1024]{1,0:T(8,128)(2,1)S(1)}, u32[]{:S(2)}, u32[]{:S(2)}) collective-permute-start(bf16[512,1024]{1,0:T(8,128)(2,1)S(1)} %pad_maximum_fusion.16), channel_id=1, source_target_pairs={{0,24},{1,25},{2,26},{3,27},{4,28},{5,29},{6,30},{7,31},{8,0},{9,1... | collective-permute-start | bytes 3145736 | tf_op jit(solution)/shard_map/ppermute | solution.py:53
  548.2 153.7 %collective-permute-start.97 = (bf16[1024,512]{1,0:T(8,128)(2,1)}, bf16[1024,512]{1,0:T(8,128)(2,1)}, u32[]{:S(2)}, u32[]{:S(2)}) collective-permute-start(bf16[1024,512]{1,0:T(8,128)(2,1)} %pad_maximum_fusion.19), channel_id=1, source_target_pairs={{0,8},{1,9},{2,10},{3,11},{4,12},{5,13},{6,14},{7,15},{8,16},{9,17... | collective-permute-start | bytes 3145736 | tf_op jit(solution)/shard_map/ppermute | solution.py:53
  558.3 144.0 %collective-permute-start.99 = (bf16[1024,512]{1,0:T(8,128)(2,1)}, bf16[1024,512]{1,0:T(8,128)(2,1)}, u32[]{:S(2)}, u32[]{:S(2)}) collective-permute-start(bf16[1024,512]{1,0:T(8,128)(2,1)} %pad_maximum_fusion.20), channel_id=1, source_target_pairs={{0,24},{1,25},{2,26},{3,27},{4,28},{5,29},{6,30},{7,31},{8,0},{9,1... | collective-permute-start | bytes 3145736 | tf_op jit(solution)/shard_map/ppermute | solution.py:53
  581.9 90.0 %collective-permute-start.92 = (bf16[512,1024]{1,0:T(8,128)(2,1)}, bf16[512,1024]{1,0:T(8,128)(2,1)S(1)}, u32[]{:S(2)}, u32[]{:S(2)}) collective-permute-start(bf16[512,1024]{1,0:T(8,128)(2,1)} %pad_maximum_fusion.17), channel_id=1, source_target_pairs={{0,8},{1,9},{2,10},{3,11},{4,12},{5,13},{6,14},{7,15},{8,16},{9,17... | collective-permute-start | bytes 3145736 | tf_op jit(solution)/shard_map/ppermute | solution.py:53
  603.2 89.3 %collective-permute-start.94 = (bf16[512,1024]{1,0:T(8,128)(2,1)}, bf16[512,1024]{1,0:T(8,128)(2,1)}, u32[]{:S(2)}, u32[]{:S(2)}) collective-permute-start(bf16[512,1024]{1,0:T(8,128)(2,1)} %pad_maximum_fusion.18), channel_id=1, source_target_pairs={{0,24},{1,25},{2,26},{3,27},{4,28},{5,29},{6,30},{7,31},{8,0},{9,1... | collective-permute-start | bytes 3145736 | tf_op jit(solution)/shard_map/ppermute | solution.py:53
  606.5 100.5 %collective-permute-start.90 = (bf16[256,1024]{1,0:T(8,128)(2,1)}, bf16[256,1024]{1,0:T(8,128)(2,1)}, u32[]{:S(2)}, u32[]{:S(2)}) collective-permute-start(bf16[256,1024]{1,0:T(8,128)(2,1)} %dynamic-slice_convert_fusion.4), channel_id=1, source_target_pairs={{0,4},{1,5},{2,6},{3,7},{4,0},{5,1},{6,2},{7,3},{8,12},{9,13},{10,... | collective-permute-start | bytes 1572872 | tf_op jit(solution)/shard_map/ppermute | solution.py:47
  770.1 55.5 %collective-permute-start.63 = (bf16[2,128,2048]{2,1,0:T(8,128)(2,1)S(1)}, bf16[2,128,2048]{2,1,0:T(8,128)(2,1)S(1)}, u32[]{:S(2)}, u32[]{:S(2)}) collective-permute-start(bf16[2,128,2048]{2,1,0:T(8,128)(2,1)S(1)} %fusion.24), channel_id=1, source_target_pairs={{0,1},{1,0},{2,3},{3,2},{4,5},{5,4},{6,7},{7,6},{8,9},{9,8},{10,11... | collective-permute-start | bytes 3145736 | tf_op jit(solution)/shard_map/ppermute | solution.py:50
  795.3 49.1 %collective-permute-start.76 = (bf16[4,1,256,512]{3,2,1,0:T(8,128)(2,1)S(1)}, bf16[4,1,256,512]{3,2,1,0:T(8,128)(2,1)S(1)}, u32[]{:S(2)}, u32[]{:S(2)}) collective-permute-start(bf16[4,1,256,512]{3,2,1,0:T(8,128)(2,1)S(1)} %dynamic-slice_convert_fusion), channel_id=1, source_target_pairs={{0,4},{1,5},{2,6},{3,7},{4,0},{5,1},{6,2},{7,3},{8,12},{9,13},{10,... | collective-permute-start | bytes 3145736 | tf_op jit(solution)/shard_map/ppermute | solution.py:47
  (168 other events, 2859.9 us)

commit v2 on v0

v2 whole, which is shorter than its diff:
```python
import functools
import math

import jax
import jax.numpy as jnp
from jax import lax
from jax.experimental import pallas as pl
from jax.experimental.pallas import tpu as pltpu
from jax.sharding import PartitionSpec as P

HEAD_SIZE = 256

EPS = 1e-06
THETA = 1000042.0
AXES = ("dp", "tensor")
BF = jnp.bfloat16
F32 = jnp.float32
EXTRA = 16
LIMIT = 56 * 1024 * 1024


class Net:
    def __init__(self):
        self.dp = lax.axis_size("dp")
        self.tensor = lax.axis_size("tensor")
        self.bits = self.dp.bit_length() - 1
        self.far = self.dp // 4
        self.d = lax.axis_index("dp")
        t = lax.axis_index("tensor")
        self.y, self.l, self.f = self.d % 2, (self.d // 2) % 2, self.d // 4
        self.x, self.c = t // 2, t % 2
        self.far_groups = [[4 * f + low for f in range(self.far)] for low in range(4)]

    def flip(self, v, dp_mask, tensor_mask=0):
        pairs = []
        for d in range(self.dp):
            for t in range(self.tensor):
                there = (d ^ dp_mask) * self.tensor + (t ^ tensor_mask)
                pairs.append((d * self.tensor + t, there))
        return lax.ppermute(v, AXES, pairs)

    def flip_y(self, v):
        return self.flip(v, 1)

    def flip_l(self, v):
        return self.flip(v, 2)

    def flip_x(self, v):
        return self.flip(v, 0, 2)

    def flip_c(self, v):
        return self.flip(v, 0, 1)

    def dp_sum(self, v):
        for bit in range(self.bits):
            v = v + self.flip(v, 1 << bit)
        return v

    def far_gather(self, v):
        pieces = [v]
        bit = 4
        while bit < self.dp:
            sent = pieces[0] if len(pieces) == 1 else jnp.stack(pieces)
            got = self.flip(sent, bit)
            pieces = pieces + ([got] if len(pieces) == 1 else [got[k] for k in range(len(pieces))])
            bit *= 2
        return pieces

    def absolute(self, pieces, axis):
        if self.far == 2:
            return in_order(self.f, *pieces, axis)
        stack = jnp.stack(pieces)
        return jnp.concatenate(
            [
                lax.dynamic_index_in_dim(stack, jnp.bitwise_xor(self.f, n), 0, keepdims=False)
                for n in range(self.far)
            ],
            axis=axis,
        )

    def far_reduce(self, pieces, *deps):
        bit = self.dp // 2
        while bit >= 4:
            n = len(pieces) // 2
            sent = pieces[n:]
            got = self.flip(sent[0] if n == 1 else jnp.stack(sent), bit)
            got = after(got, *deps) if deps else got
            got = [got] if n == 1 else [got[k] for k in range(n)]
            pieces = [
                p.astype(F32) + g.astype(F32) if n == 1 else (p.astype(F32) + g.astype(F32)).astype(BF)
                for p, g in zip(pieces[:n], got)
            ]
            bit //= 2
        return pieces[0]

    def cube_gather(self, v):
        parts = [v[a:b] for a, b in part_rows(v.shape[0])]
        for step in range(2):
            got = [self.cube_flip(n, step, part) for n, part in enumerate(parts)]
            parts = [jnp.concatenate(pair, axis=0) for pair in zip(parts, got)]
        last = [self.cube_flip(n, 2, part) for n, part in enumerate(parts)]
        return parts, last

    def cube_flip(self, part, step, v):
        return (self.flip_l, self.flip_y, self.flip_x)[(part + step) % 3](v)

    def cube_reduce(self, near, last):
        got = [self.cube_flip(n, 2, v.astype(BF)) for n, v in enumerate(last)]
        parts = [a.astype(F32) + b.astype(F32) for a, b in zip(near, got)]
        for step in (1, 0):
            half = [v.shape[0] // 2 for v in parts]
            got = [
                self.cube_flip(n, step, v[h:].astype(BF)) for n, (v, h) in enumerate(zip(parts, half))
            ]
            parts = [v[:h] + g.astype(F32) for v, h, g in zip(parts, half, got)]
        return jnp.concatenate(parts, axis=0)


def part_rows(n):
    one = -(-n // 48) * 16
    return [(0, one), (one, 2 * one), (2 * one, n)]


def split_parts(v, n):
    out, at = [], 0
    for a, b in part_rows(n):
        out.append(v[at : at + 4 * (b - a)])
        at += 4 * (b - a)
    return out


def in_order(flag, mine, other, axis):
    first = jnp.where(flag == 0, mine, other)
    second = jnp.where(flag == 0, other, mine)
    return jnp.concatenate([first, second], axis=axis)


def halves(flag, v, axis):
    n = v.shape[axis] // 2
    mine = lax.dynamic_slice_in_dim(v, flag * n, n, axis)
    other = lax.dynamic_slice_in_dim(v, (1 - flag) * n, n, axis)
    return mine, other


def after(value, *deps):
    return lax.optimization_barrier((value,) + deps)[0]


def pin(*values):
    return lax.optimization_barrier(values)


def nt(left, right):
    return lax.dot_general(left, right, (((1,), (1,)), ((), ())), preferred_element_type=F32)


def tn(left, right):
    return lax.dot_general(left, right, (((0,), (0,)), ((), ())), preferred_element_type=F32)


def dot(left, right):
    return jnp.dot(left, right, preferred_element_type=F32)


def spin(v, cos, sin):
    half = v.shape[-1] // 2
    a, b = v[:, :half], v[:, half:]
    return jnp.concatenate([a * cos - b * sin, b * cos + a * sin], axis=-1)


def attend_kernel(far, *refs):
    me, states, cos_ref, sin_ref, seg_col, seg_row, *weights = refs[:10]
    n1_ref, qr_ref, kr_ref, v_ref, p_ref, o_ref = refs[10:]
    seq, width = states.shape
    rp = width // (4 * far)
    fq, fk = qr_ref.shape[1], kr_ref.shape[1]
    tile = min(128, seq)
    scale = 1.0 / math.sqrt(HEAD_SIZE)
    d = me[0]

    @pl.loop(0, seq // tile)
    def _(number):
        rows = pl.ds(pl.multiple_of(number * tile, tile), tile)
        xf = states[rows, :].astype(F32)
        recip = lax.rsqrt(jnp.mean(xf * xf, axis=-1, keepdims=True) + EPS)
        total = None
        for j in range(2):
            for i in range(2):
                for k in range(far):
                    at = jnp.bitwise_xor(d, 4 * k + 2 * i + j)
                    if rp % 128 == 0:
                        block = states[rows, pl.ds(pl.multiple_of(at * rp, 128), rp)].astype(F32)
                    else:
                        first = pl.multiple_of((at // 2) * (2 * rp), 128)
                        block = states[rows, pl.ds(first, 2 * rp)].astype(F32)
                        block = jnp.where(at % 2 == 0, block[:, :rp], block[:, rp:])
                    w = weights[2 * j + i]
                    gain = w[k, rp : rp + EXTRA, :rp][:1].astype(F32)
                    normed = (block * recip * gain).astype(BF)
                    place = ((j * 2 + i) * far + k) * rp
                    n1_ref[rows, place : place + rp] = normed
                    part = dot(normed, w[k, :rp, :])
                    total = part if total is None else total + part
        cos, sin = cos_ref[rows, :], sin_ref[rows, :]
        for head in range(fq // HEAD_SIZE):
            block = slice(head * HEAD_SIZE, (head + 1) * HEAD_SIZE)
            qr_ref[rows, block] = spin(total[:, block], cos, sin).astype(BF)
        for head in range(fk // HEAD_SIZE):
            block = slice(head * HEAD_SIZE, (head + 1) * HEAD_SIZE)
            at = fq + head * HEAD_SIZE
            kr_ref[rows, block] = spin(total[:, at : at + HEAD_SIZE], cos, sin).astype(BF)
        v_ref[rows, :] = total[:, fq + fk :].astype(BF)

    rep = fq // fk
    for i in range(seq // tile):
        rows, keys = slice(i * tile, (i + 1) * tile), slice(0, (i + 1) * tile)
        shape = (tile, (i + 1) * tile)
        behind = lax.broadcasted_iota(jnp.int32, shape, 1) <= (
            lax.broadcasted_iota(jnp.int32, shape, 0) + i * tile
        )
        allowed = (seg_col[rows, :] == seg_row[:, keys]) & behind
        for head in range(fq // HEAD_SIZE):
            block = slice(head * HEAD_SIZE, (head + 1) * HEAD_SIZE)
            k = head // rep
            kblock = slice(k * HEAD_SIZE, (k + 1) * HEAD_SIZE)
            s = nt(qr_ref[rows, block], kr_ref[keys, kblock]) * scale
            s = jnp.where(allowed, s, -1e30)
            e = jnp.exp(s - jnp.max(s, axis=-1, keepdims=True))
            p = (e / jnp.sum(e, axis=-1, keepdims=True)).astype(BF)
            p_ref[head, rows, keys] = p
            o_ref[rows, block] = dot(p, v_ref[keys, kblock]).astype(BF)


def attend(me, states, cos, sin, segments, weights, fq, fk, far):
    seq, width = states.shape
    shapes = [
        jax.ShapeDtypeStruct((seq, width), BF),
        jax.ShapeDtypeStruct((seq, fq), BF),
        jax.ShapeDtypeStruct((seq, fk), BF),
        jax.ShapeDtypeStruct((seq, fk), BF),
        jax.ShapeDtypeStruct((fq // HEAD_SIZE, seq, seq), BF),
        jax.ShapeDtypeStruct((seq, fq), BF),
    ]
    vmem = pl.BlockSpec(memory_space=pltpu.VMEM)
    flops = 2 * seq * width * (fq + 2 * fk) + 4 * seq * seq * fq
    return pl.pallas_call(
        functools.partial(attend_kernel, far),
        out_shape=shapes,
        in_specs=[pl.BlockSpec(memory_space=pltpu.SMEM)] + [vmem] * 9,
        out_specs=[vmem] * 6,
        compiler_params=pltpu.CompilerParams(vmem_limit_bytes=LIMIT),
        cost_estimate=pl.CostEstimate(
            flops=flops, bytes_accessed=12 << 20, transcendentals=seq * seq * 2
        ),
        name="attend",
    )(me, states, cos, sin, segments[:, None], segments[None, :], *weights)


def attend_back_kernel(far, *refs):
    me, dh, w_o, qr_ref, kr_ref, v_ref, p_ref, cos_ref, sin_ref, *weights = refs[:13]
    d_ref, send_ref, keep_ref = refs[13:16]
    do_ref, dk_ref, dv_ref = refs[16:]
    seq, width = dh.shape
    rp = width // (4 * far)
    fq, fk = qr_ref.shape[1], kr_ref.shape[1]
    tile = min(128, seq)
    scale = 1.0 / math.sqrt(HEAD_SIZE)
    rep = fq // fk

    @pl.loop(0, seq // tile)
    def _(i):
        rows = pl.ds(pl.multiple_of(i * tile, tile), tile)
        do_ref[rows, :] = nt(dh[rows, :], w_o[...]).astype(BF)

    dk_ref[...] = jnp.zeros_like(dk_ref)
    dv_ref[...] = jnp.zeros_like(dv_ref)
    for i in range(seq // tile):
        rows, keys = slice(i * tile, (i + 1) * tile), slice(0, (i + 1) * tile)
        cos, sin = cos_ref[rows, :], -sin_ref[rows, :]
        for head in range(fq // HEAD_SIZE):
            block = slice(head * HEAD_SIZE, (head + 1) * HEAD_SIZE)
            k = head // rep
            kblock = slice(k * HEAD_SIZE, (k + 1) * HEAD_SIZE)
            do = do_ref[rows, block]
            pb = p_ref[head, rows, keys]
            p = pb.astype(F32)
            dp = nt(do, v_ref[keys, kblock])
            inner = jnp.sum(p * dp, axis=-1, keepdims=True)
            ds = (p * (dp - inner)).astype(BF)
            dq = dot(ds, kr_ref[keys, kblock]) * scale
            d_ref[rows, block] = spin(dq, cos, sin).astype(BF)
            dk_ref[keys, kblock] += tn(ds, qr_ref[rows, block])
            dv_ref[keys, kblock] += tn(pb, do)
    for head in range(fk // HEAD_SIZE):
        block = slice(head * HEAD_SIZE, (head + 1) * HEAD_SIZE)
        at = fq + head * HEAD_SIZE
        d_ref[:, at : at + HEAD_SIZE] = spin(
            dk_ref[:, block] * scale, cos_ref[...], -sin_ref[...]
        ).astype(BF)
    d_ref[:, fq + fk :] = dv_ref[...].astype(BF)

    tok = seq // 4
    mine, d = me[1], me[0]
    for side in range(2):
        out = slice(side * tok, (side + 1) * tok)
        for ref, which in ((send_ref, 1 - mine), (keep_ref, mine)):
            rows = pl.ds(pl.multiple_of((side * 2 + which) * tok, tok), tok)
            grad = d_ref[rows, :]
            for i in range(2):
                for k in range(far):
                    values = [
                        nt(grad, weights[2 * j + i][k, :rp, :]).astype(BF) for j in range(2)
                    ]
                    at = jnp.bitwise_xor(d, 4 * k + 2 * i)
                    if rp % 128 == 0:
                        for j in range(2):
                            place = pl.multiple_of(jnp.bitwise_xor(at, j) * rp, 128)
                            ref[out, pl.ds(place, rp)] = values[j]
                    else:
                        place = pl.multiple_of((at // 2) * (2 * rp), 128)
                        pair = [jnp.concatenate(v, axis=-1) for v in (values, values[::-1])]
                        ref[out, pl.ds(place, 2 * rp)] = jnp.where(at % 2 == 0, *pair)


def attend_back(me, dh, w_o, qr, kr, v, p, cos, sin, weights, far):
    seq, width = dh.shape
    fq, fk = qr.shape[1], kr.shape[1]
    vmem = pl.BlockSpec(memory_space=pltpu.VMEM)
    flops = 2 * seq * width * (fq + fq + 2 * fk) + 10 * seq * seq * fq
    return pl.pallas_call(
        functools.partial(attend_back_kernel, far),
        out_shape=[
            jax.ShapeDtypeStruct((seq, fq + 2 * fk), BF),
            jax.ShapeDtypeStruct((seq // 2, width), BF),
            jax.ShapeDtypeStruct((seq // 2, width), BF),
        ],
        in_specs=[pl.BlockSpec(memory_space=pltpu.SMEM)] + [vmem] * 12,
        out_specs=[vmem] * 3,
        scratch_shapes=[
            pltpu.VMEM((seq, fq), BF),
            pltpu.VMEM((seq, fk), F32),
            pltpu.VMEM((seq, fk), F32),
        ],
        compiler_params=pltpu.CompilerParams(vmem_limit_bytes=LIMIT),
        cost_estimate=pl.CostEstimate(flops=flops, bytes_accessed=16 << 20, transcendentals=0),
        name="attend_back",
    )(me, dh, w_o, qr, kr, v, p, cos, sin, *weights)


def tables(places, width):
    halfway = width // 2
    counter = jnp.arange(halfway, dtype=jnp.float32)
    inverse = jnp.exp(counter * (-2.0 * math.log(THETA) / width))
    angles = places.astype(jnp.float32)[..., None] * inverse
    return (jnp.cos(angles), jnp.sin(angles))


def rms_scale(value_rows):
    return lax.rsqrt(jnp.mean(value_rows * value_rows, axis=-1, keepdims=True) + EPS)


def norm_back(grad_normed, unit_rows, recip_rows, gain_full):
    scaled = grad_normed * gain_full
    gain_grad = jnp.sum(grad_normed * unit_rows, axis=0)
    grad_rows = recip_rows * (
        scaled - unit_rows * jnp.mean(scaled * unit_rows, axis=-1, keepdims=True)
    )
    return (gain_grad, grad_rows)


def per_device(
    states,
    teacher,
    segments,
    positions,
    w_q,
    key_matrix,
    value_matrix,
    w_o,
    w_gate,
    w_up,
    w_down,
    norm1_gain,
    norm2_gain,
):
    net = Net()
    far = net.far
    seq, width = states.shape
    rp = w_q.shape[0]
    tok = seq // 4
    fq, fk = w_q.shape[1], key_matrix.shape[1]
    fqkv = fq + 2 * fk
    sub = w_gate.shape[1] // 4

    def blocks_at(a, n, places, axis):
        return jnp.concatenate(
            [lax.dynamic_slice_in_dim(a, at * n, n, axis) for at in places], axis=axis
        )

    def add(a, b):
        return (a.astype(F32) + b.astype(F32)).astype(BF)

    live = (segments > 0).astype(F32)
    alive = jnp.sum(live)
    high = jnp.floor(alive / 256.0)
    low = alive - high * 256.0
    rider = jnp.concatenate([norm1_gain, norm2_gain, jnp.zeros((fqkv - 2 * rp,), BF)])
    rider = jnp.stack([rider, jnp.pad(jnp.stack([high, low]).astype(BF), (0, fqkv - 2))])
    rider = jnp.pad(rider, ((0, EXTRA - 2), (0, 0)))
    qkv = jnp.concatenate(
        [jnp.concatenate([w_q, key_matrix, value_matrix], axis=1), rider], axis=0
    )
    qkv_own = jnp.stack(net.far_gather(qkv))

    def swap_y(w, axis):
        mine, other = [blocks_at(w, sub, [y, 2 + y], axis) for y in (net.y, 1 - net.y)]
        return in_order(net.y, mine, net.flip_y(other), 1 - axis)

    def swap_l(w, axis, *deps):
        mine, other = halves(net.l, w, axis)
        return in_order(net.l, mine, net.flip_l(after(other, *deps)), 1 - axis)

    def gather(w, axis):
        return lax.all_gather(
            w, "dp", axis=axis, axis_index_groups=net.far_groups, tiled=True
        )

    o_pair = in_order(net.y, w_o, net.flip_y(w_o), 1)
    gate = gather(swap_l(swap_y(w_gate, 1), 1), 0)
    up, down = swap_y(w_up, 1), swap_y(w_down, 0)

    qkv_l, qkv_y = net.flip_l(qkv_own), net.flip_y(qkv_own)
    o_far = net.absolute(net.far_gather(after(o_pair, qkv_own)), 1)
    qkv_all = (qkv_own, qkv_l, qkv_y, net.flip_y(qkv_l))
    o_l = net.flip_l(after(o_far, qkv_l))
    up = gather(swap_l(up, 1, qkv_l), 0)
    down = gather(swap_l(down, 0, qkv_all[3]), 1)
    parts = []
    for n in range(far):
        block = slice(n * 2 * rp, (n + 1) * 2 * rp)
        parts.append(in_order(net.l, o_far[:, block], o_l[:, block], 1))
    full_o = jnp.concatenate(parts, axis=1)

    me = jnp.stack([net.d, net.c]).astype(jnp.int32)
    cos_table, sin_table = tables(positions, HEAD_SIZE)
    normed, qr, kr, v, p, attended = attend(
        me, states, cos_table, sin_table, segments, qkv_all, fq, fk, far
    )
    rider = [w[k, rp : rp + 2] for w in qkv_all for k in range(far)]
    count = sum(e[1, 0].astype(F32) * 256.0 + e[1, 1].astype(F32) for e in rider)

    def gains(at):
        def piece(j, i, k):
            return qkv_all[2 * j + i][k, rp, at : at + rp].astype(F32)

        parts = []
        for k in range(far):
            pairs = [in_order(net.y, piece(0, i, k), piece(1, i, k), 0) for i in range(2)]
            parts.append(in_order(net.l, *pairs, 0))
        return net.absolute(parts, 0)[None, :]

    gain_one, gain_two = gains(0), gains(rp)

    def rows_of_core(a, which):
        return blocks_at(a, tok, [which, 2 + which], 0)

    send = net.flip_c(dot(rows_of_core(attended, 1 - net.c), full_o).astype(BF))
    keep = dot(rows_of_core(attended, net.c), full_o)
    keep, send = halves(net.x, keep + send.astype(F32), 0)
    attn_sum = keep + net.flip_x(send.astype(BF)).astype(F32)

    first_token = (net.x * 2 + net.c) * tok
    my_inputs = lax.dynamic_slice_in_dim(states, first_token, tok, 0).astype(F32)
    my_teacher = lax.dynamic_slice_in_dim(teacher, first_token, tok, 0).astype(F32)
    my_live = lax.dynamic_slice_in_dim(live, first_token, tok, 0)

    full_gate = jnp.concatenate([gate, net.flip_c(gate)], axis=1)
    full_up = jnp.concatenate([up, net.flip_c(up)], axis=1)
    full_down = jnp.concatenate([down, net.flip_c(down)], axis=0)
    hidden = my_inputs + attn_sum
    recip_two = rms_scale(hidden)
    unit_two = hidden * recip_two
    near, last = net.cube_gather((unit_two * gain_two).astype(BF))
    n2_near, n2_last = jnp.concatenate(near, axis=0), jnp.concatenate(last, axis=0)

    def act(n2):
        gate, up = dot(n2, full_gate), dot(n2, full_up)
        sig = jax.nn.sigmoid(gate)
        silu = gate * sig
        return (silu * up).astype(BF), up * sig * (1.0 + gate * (1.0 - sig)), silu

    act_near, by_gate_near, by_up_near = act(n2_near)
    act_last, by_gate_last, by_up_last = act(after(n2_last, act_near))
    y_last = dot(act_last, full_down).astype(BF)
    y_near = dot(after(act_near, y_last), full_down)
    mlp_sum = net.cube_reduce(split_parts(y_near, tok), split_parts(y_last, tok))
    output = hidden + mlp_sum
    error = (output - my_teacher) * my_live[:, None]
    factor = net.dp * seq / count
    grad_out = error * factor
    squares = jnp.sum(error * error)

    def share_tokens(a):
        a = in_order(net.x, a, net.flip_x(a), 0)
        b = net.flip_c(a)
        return jnp.concatenate(
            [in_order(net.c, a[:tok], b[:tok], 0), in_order(net.c, a[tok:], b[tok:], 0)], axis=0
        )

    near, last = net.cube_gather(grad_out.astype(BF))
    dy_all = jnp.concatenate(near + last, axis=0)
    act_all = jnp.concatenate([act_near, act_last], axis=0)
    n2_all = jnp.concatenate([n2_near, n2_last], axis=0)

    def sum_back(mine, other, axis):
        return lax.psum_scatter(
            add(mine, net.flip_c(other)),
            "dp",
            scatter_dimension=axis,
            axis_index_groups=net.far_groups,
            tiled=True,
        ).astype(F32)

    down_other = tn(act_all[:, sub:], dy_all).astype(BF)
    down_mine = tn(act_all[:, :sub], dy_all).astype(BF)
    down_sum = sum_back(down_mine, down_other, 1)
    grad_active = nt(after(dy_all, down_mine), full_down)
    dg_all = (grad_active * jnp.concatenate([by_gate_near, by_gate_last], axis=0)).astype(BF)
    du_all = (grad_active * jnp.concatenate([by_up_near, by_up_last], axis=0)).astype(BF)
    dn_all = nt(dg_all, full_gate) + nt(du_all, full_up)
    dn_near, dn_last = dn_all[: 4 * tok], dn_all[4 * tok :].astype(BF)
    n2_all, dg_late, du_late = after((n2_all, dg_all, du_all), dn_last)
    gate_other = tn(n2_all, dg_late[:, sub:]).astype(BF)
    gate_mine = tn(n2_all, dg_late[:, :sub]).astype(BF)
    gate_sum = sum_back(gate_mine, gate_other, 0)
    up_other = tn(n2_all, du_late[:, sub:]).astype(BF)
    up_mine = tn(n2_all, du_late[:, :sub]).astype(BF)
    up_sum = sum_back(up_mine, up_other, 0)

    back_two = net.cube_reduce(split_parts(dn_near, tok), split_parts(dn_last, tok))
    gain_two_grad, hidden_from_norm = norm_back(back_two, unit_two, recip_two, gain_two)
    grad_hidden = grad_out + hidden_from_norm
    grad_hidden_low = share_tokens(grad_hidden.astype(BF))
    out_states = share_tokens(after(output.astype(BF), grad_hidden_low))

    grad_qkv, send, keep = attend_back(
        me, grad_hidden_low, full_o, qr, kr, v, p, cos_table, sin_table, qkv_all, far
    )
    back_one = (keep.astype(F32) + net.flip_c(send).astype(F32)).astype(BF)
    back_got = net.flip_x(back_one)
    dh_low, att, n1, g_qkv = after((grad_hidden_low, attended, normed, grad_qkv), send)
    grad_wqkv = tn(n1, g_qkv).astype(BF)
    grad_wo = tn(att, dh_low).astype(BF)

    half, quarter = width // 2, width // 4
    gq, gkv = grad_wqkv[:, :fq], grad_wqkv[:, fq:]
    gkv = [gkv[n * quarter : (n + 1) * quarter] for n in range(4)]
    q_got = net.flip_y(gq[half:])
    kv_got = net.flip_l(jnp.concatenate([gkv[1], gkv[3]], axis=0))
    q_got, kv_got, back_got = pin(q_got, kv_got, back_got)
    gq = add(gq[:half], q_got)
    gkv = add(jnp.concatenate([gkv[0], gkv[2]], axis=0), kv_got)
    q_got = net.flip_l(gq[quarter:])
    kv_got = net.flip_y(gkv[quarter:])
    gqkv = jnp.concatenate([add(gq[:quarter], q_got), add(gkv[:quarter], kv_got)], axis=1)

    other = blocks_at(grad_wo, rp, [2 * n + 1 - net.y for n in range(2 * far)], 1)
    go = add(
        blocks_at(grad_wo, rp, [2 * n + net.y for n in range(2 * far)], 1), net.flip_y(other)
    )
    other = blocks_at(go, rp, [2 * n + 1 - net.l for n in range(far)], 1)
    go = add(blocks_at(go, rp, [2 * n + net.l for n in range(far)], 1), net.flip_l(other))

    def far_blocks(a):
        n = a.shape[0] // far
        return [a[k * n : (k + 1) * n] for k in range(far)]

    go = [
        lax.dynamic_slice_in_dim(go, jnp.bitwise_xor(net.f, k) * rp, rp, 1) for k in range(far)
    ]
    result_qkv = net.far_reduce(far_blocks(gqkv)).astype(F32)
    result_o = net.far_reduce(go).astype(F32)
    result_q = result_qkv[:, :fq]
    result_k, result_v = result_qkv[:, fq : fq + fk], result_qkv[:, fq + fk :]

    def exchange(total, axis):
        cross = 1 - axis
        mine, other = halves(net.l, total, axis)
        got = net.flip_l(other.astype(BF)).astype(F32)
        mine, other = halves(net.y, in_order(net.l, mine, got, cross), axis)
        got = net.flip_y(other.astype(BF)).astype(F32)
        parts = []
        for n in range(2):
            cut = functools.partial(
                lax.slice_in_dim, start_index=n * sub, limit_index=(n + 1) * sub, axis=cross
            )
            parts.append(in_order(net.y, cut(mine), cut(got), cross))
        return jnp.concatenate(parts, axis=cross)

    result_down = exchange(after(down_sum, send), 1)
    result_gate = exchange(after(gate_sum, back_got), 0)
    result_up = exchange(after(up_sum, back_got), 0)

    back_one = back_one.astype(F32) + back_got.astype(F32)
    xf = rows_of_core(states, net.c).astype(F32)
    recip_mine = rms_scale(xf)
    gain_one_grad, from_norm = norm_back(back_one, xf * recip_mine, recip_mine, gain_one)
    grad_input = rows_of_core(grad_hidden_low, net.c).astype(F32) + from_norm
    grad_other = net.flip_c(grad_input)
    grad_input = jnp.concatenate(
        [
            in_order(net.c, grad_input[:tok], grad_other[:tok], 0),
            in_order(net.c, grad_input[tok:], grad_other[tok:], 0),
        ],
        axis=0,
    )

    small = jnp.concatenate([0.5 * gain_one_grad, gain_two_grad, jnp.full((128,), squares, F32)])
    small = small.reshape(-1, 128)
    small = small + net.flip_c(small)
    small = small + net.flip_x(small)
    small = net.dp_sum(small).reshape(-1)
    result_g1 = lax.dynamic_slice_in_dim(small[:width], net.d * rp, rp)
    result_g2 = lax.dynamic_slice_in_dim(small[width : 2 * width], net.d * rp, rp)
    loss_value = small[2 * width] / (count * width)
    return (
        out_states,
        grad_input,
        loss_value,
        result_q,
        result_k,
        result_v,
        result_o,
        result_gate,
        result_up,
        result_down,
        result_g1,
        result_g2,
    )


def solution(mesh):
    in_specs = (
        P("dp", None),
        P("dp", None),
        P("dp"),
        P("dp"),
        P("dp", "tensor"),
        P("dp", "tensor"),
        P("dp", "tensor"),
        P("tensor", "dp"),
        P("dp", "tensor"),
        P("dp", "tensor"),
        P("tensor", "dp"),
        P("dp"),
        P("dp"),
    )
    out_specs = (
        P("dp", None),
        P("dp", None),
        P(),
        P("dp", "tensor"),
        P("dp", "tensor"),
        P("dp", "tensor"),
        P("tensor", "dp"),
        P("dp", "tensor"),
        P("dp", "tensor"),
        P("tensor", "dp"),
        P("dp"),
        P("dp"),
    )
    return jax.shard_map(
        per_device, mesh=mesh, in_specs=in_specs, out_specs=out_specs, check_vma=False
    )
```

time: 1730 us -> 753 us (0.44)
  waiting for transfers between devices: 1420 us -> 370 us
  starting transfers between devices: 1.76 us -> 96.9 us
  blocking collectives: 83.8 us -> 0 us
  local copies, waits for them, and re-layouts: 10.1 us -> 52.8 us
  matrix products: 133 us -> 92.4 us
  Pallas kernels: 0 us -> 27.9 us
    reduce_scatter x7 -> x3, waiting for transfers between devices: 686 us -> 0.02 us  [sum_back(): lax.psum_scatter(add(mine, net.flip_c(other)), 'dp', scatter_dimension=ax...]
    all_gather x7 -> x3, waiting for transfers between devices: 492 us -> 63.1 us  [gather(): lax.all_gather(w, 'dp', axis=axis, axis_index_groups=net.far_groups, tile...]
    ppermute x0 -> x83, waiting for transfers between devices: none -> 306 us  [flip(): return lax.ppermute(v, AXES, pairs)]
    psum x4 -> x0, waiting for transfers between devices: 233 us -> none  [the longest x1 82.6 us: per_device(): lax.psum(jnp.dot(active, full_down, preferred_element_type=jnp.float32),...]
    ppermute x0 -> x83, starting transfers between devices: none -> 96.3 us  [flip(): return lax.ppermute(v, AXES, pairs)]
    dot_general x27 -> x19, matrix products: 133 us -> 92.4 us  [the longest x8 33.3 us: tn(): lax.dot_general(left, right, (((0,), (0,)), ((), ())), preferred_element_...]
    all_gather x2 -> x0, blocking collectives: 40.2 us -> none  [the longest x1 22.3 us: per_device(): lax.all_gather(norm1_gain, 'dp', axis=0, tiled=True)]
    pallas_call x0 -> x2, Pallas kernels: none -> 27.9 us  [the longest x1 17.4 us: attend_back(): pl.pallas_call(functools.partial(attend_back_kernel, far), out_shape=[jax...]
  transfers between devices with their start and end apart: 18 -> 89, of which waited for: 18 -> 48; matrix products, arithmetic and copies ran while one was open for 7% -> 24% of each run, Pallas kernels for 0% -> 4%
where the time goes in v2:
time: 753 us; the launch traced here: 744 us
  waiting for transfers between devices  370 us (49%)
  starting transfers between devices  96.9 us (13%)
  matrix products  92.4 us (12%)
  other arithmetic  74.7 us (10%)
  local copies, waits for them, and re-layouts  52.8 us (7%)
  between operations  29.7 us (4%)
  Pallas kernels  27.9 us (4%)
    ppermute x83, waiting for transfers between devices, flip(): return lax.ppermute(v, AXES, pairs)  306 us
    ppermute x83, starting transfers between devices, flip(): return lax.ppermute(v, AXES, pairs)  96.3 us
    all_gather x3, waiting for transfers between devices, gather(): lax.all_gather(w, 'dp', axis=axis, axis_index_groups=net.far_groups, tile...  63.1 us
    dot_general x8, matrix products, tn(): lax.dot_general(left, right, (((0,), (0,)), ((), ())), preferred_element_...  33.3 us
    dot_general x8, matrix products, dot(): return jnp.dot(left, right, preferred_element_type=F32)  30 us
    dot_general x3, matrix products, nt(): lax.dot_general(left, right, (((1,), (1,)), ((), ())), preferred_element_...  29 us
    unnamed x108, local copies, waits for them, and re-layouts  24.7 us
    pallas_call x1, Pallas kernels, attend_back(): pl.pallas_call(functools.partial(attend_back_kernel, far), out_shape=[jax...  17.4 us
  transfers between devices with their start and end apart: 89, of which 48 were waited for; matrix products, arithmetic and copies ran while one was open for 24% of the time, Pallas kernels for 4%

profile of v2, /device:TPU:0, one launch (start us, length us, event | category | flops | bytes accessed | tf_op | source)
XLA Modules:
  0.0 744.0 jit_solution(7444688122113236248)
XLA Ops:
  29.9 10.3 %collective-permute-done.18 = bf16[256,1024]{1,0:T(8,128)(2,1)} collective-permute-done((bf16[256,1024]{1,0:T(8,128)(2,1)}, bf16[256,1024]{1,0:T(8,128)(2,1)}, u32[]{:S(2)}, u32[]{:S(2)}) %collective-permute-start.18) | collective-permute-done | bytes 524320 | tf_op jit(solution)/shard_map/ppermute | solution.py:40
  60.7 27.6 %collective-permute-done.5 = bf16[512,512]{1,0:T(8,128)(2,1)S(1)} collective-permute-done((bf16[512,512]{1,0:T(8,128)(2,1)S(1)}, bf16[512,512]{1,0:T(8,128)(2,1)S(1)}, u32[]{:S(2)}, u32[]{:S(2)}) %collective-permute-start.5) | collective-permute-done | bytes 524320 | tf_op jit(solution)/shard_map/ppermute | solution.py:40
  103.3 28.9 %collective-permute-done.6 = bf16[512,1024]{1,0:T(8,128)(2,1)} collective-permute-done((bf16[512,1024]{1,0:T(8,128)(2,1)}, bf16[512,1024]{1,0:T(8,128)(2,1)}, u32[]{:S(2)}, u32[]{:S(2)}) %collective-permute-start.6) | collective-permute-done | bytes 1048608 | tf_op jit(solution)/shard_map/ppermute | solution.py:40
  134.9 10.5 %attend.1 = (bf16[512,2048]{1,0:T(8,128)(2,1)}, bf16[512,512]{1,0:T(8,128)(2,1)}, bf16[512,256]{1,0:T(8,128)(2,1)}, bf16[512,256]{1,0:T(8,128)(2,1)}, bf16[2,512...) custom-call(s32[2]{0:T(128)} %pad_add_fusion.refs_0_, bf16[512,2048]{1,0:T(8,128)(2,1)} %refs_1_.1, ...), custom_call_target="tpu_custom_call" | custom-call | flops 2684354560 | bytes 12582912 | tf_op jit(solution)/shard_map/attend/pallas_call | solution.py:246
  180.8 32.5 %all-gather.6.cloned.1.call-done = bf16[2048,512]{1,0:T(8,128)(2,1)} async-done(((bf16[1024,512]{1,0:T(8,128)(2,1)}), bf16[2048,512]{1,0:T(8,128)(2,1)}) %all-gather.6.cloned.1.call-update) | async-done | bytes 2097168 | tf_op jit(solution)/shard_map/all_gather | solution.py:424
  240.5 30.5 %all-gather.8.cloned.1.call-done = bf16[512,2048]{1,0:T(8,128)(2,1)} async-done(((bf16[512,1024]{1,0:T(8,128)(2,1)}), bf16[512,2048]{1,0:T(8,128)(2,1)}) %all-gather.8.cloned.1.call-update) | async-done | bytes 2097168 | tf_op jit(solution)/shard_map/all_gather | solution.py:424
  296.2 7.9 %add_multiply_fusion.1 = (f32[512,1024]{1,0:T(8,128)}, bf16[512,1024]{1,0:T(8,128)(2,1)S(1)}, f32[512,1024]{1,0:T(8,128)}) fusion(f32[512,1024]{1,0:T(8,128)S(1)} %fusion.84, bf16[512,2048]{1,0:T(8,128)(2,1)} %get-tuple-element.239, bf16[2048,1024]{1,0:T(8,128)(2,1)} %constant_dynamic-update-slice_fusion.9), kind=kOutput, calls=%fused_computation.58 | convolution fusion | flops 2153250816 | bytes 13631488 | tf_op jit(solution)/shard_map/dot_general | solution.py:162
  306.7 7.2 add_multiply_fusion
  331.9 10.9 %collective-permute-done.34 = bf16[64,2048]{1,0:T(8,128)(2,1)S(1)} collective-permute-done((bf16[64,2048]{1,0:T(8,128)(2,1)S(1)}, bf16[64,2048]{1,0:T(8,128)(2,1)S(1)}, u32[]{:S(2)}, u32[]{:S(2)}) %collective-permute-start.34) | collective-permute-done | bytes 262176 | tf_op jit(solution)/shard_map/ppermute | solution.py:40
  377.0 7.3 collective-permute-done.39
  411.4 10.1 %fusion = (bf16[1024,1024]{1,0:T(8,128)(2,1)}, bf16[1024,1024]{1,0:T(8,128)(2,1)}) fusion(f32[512,1024]{1,0:T(8,128)} %get-tuple-element.96, f32[512,1024]{1,0:T(8,128)} %get-tuple-element.94, f32[512,1024]{1,0:T(8,128)} %get-tuple-element.139, f32[512,1024]{1,0:T(8,128)} %get-tuple-element.138, bf16[1024,2048]{1,0:T(8,128)(2,1)} %copy-done.25, ...), kind=kOutput, calls=%fused_computation.1 | convolution fusion | flops 4301258752 | bytes 20971520 | tf_op jit(solution)/shard_map/dot_general | solution.py:154
  421.5 8.6 %fusion.87 = f32[1024,2048]{1,0:T(8,128)} fusion(bf16[1024,1024]{1,0:T(8,128)(2,1)} %get-tuple-element.69, bf16[2048,1024]{1,0:T(8,128)(2,1)S(1)} %constant_dynamic-update-slice_fusion.11), kind=kOutput, calls=%fused_computation.431 | convolution fusion | flops 4294967296 | bytes 14680064 | tf_op jit(solution)/shard_map/dot_general | solution.py:154
  430.1 10.4 %fusion.83 = (bf16[1024,2048]{1,0:T(8,128)(2,1)S(1)}, f32[1024,2048]{1,0:T(8,128)}) fusion(f32[1024,2048]{1,0:T(8,128)} %fusion.87, bf16[1024,1024]{1,0:T(8,128)(2,1)S(1)} %copy-done.39, bf16[2048,1024]{1,0:T(8,128)(2,1)} %constant_dynamic-update-slice_fusion.9), kind=kOutput, calls=%fused_computation.427 | convolution fusion | flops 4299161600 | bytes 27262976 | tf_op jit(solution)/shard_map/dot_general | solution.py:154
  463.9 18.3 %collective-permute-done.52 = bf16[64,2048]{1,0:T(8,128)(2,1)S(1)} collective-permute-done((bf16[64,2048]{1,0:T(8,128)(2,1)S(1)}, bf16[64,2048]{1,0:T(8,128)(2,1)S(1)}, u32[]{:S(2)}, u32[]{:S(2)}) %collective-permute-start.52) | collective-permute-done | bytes 262176 | tf_op jit(solution)/shard_map/ppermute | solution.py:40
  515.8 10.5 %collective-permute-done.54 = bf16[128,2048]{1,0:T(8,128)(2,1)S(1)} collective-permute-done((bf16[128,2048]{1,0:T(8,128)(2,1)S(1)}, bf16[128,2048]{1,0:T(8,128)(2,1)S(1)}, u32[]{:S(2)}, u32[]{:S(2)}) %collective-permute-start.54) | collective-permute-done | bytes 524320 | tf_op jit(solution)/shard_map/ppermute | solution.py:40
  536.2 17.4 %attend_back.1 = (bf16[512,1024]{1,0:T(8,128)(2,1)}, bf16[256,2048]{1,0:T(8,128)(2,1)}, bf16[256,2048]{1,0:T(8,128)(2,1)}) custom-call(s32[2]{0:T(128)} %pad_add_fusion.refs_0_, bf16[512,2048]{1,0:T(8,128)(2,1)} %pad_maximum_fusion.3.refs_1_, bf16[512,2048]{1,0:T(8,128)(2,1)} %copy-done, bf16[512,512]{1,0:T(8,128)(2,1)} %get-tuple-element.51.refs_3_, ...), custom_call_target="tpu_custom_call" | custom-call | flops 4563402752 | bytes 16777216 | tf_op jit(solution)/shard_map/attend_back/pallas_call | solution.py:330
  564.4 8.3 %collective-permute-done.56 = bf16[128,2048]{1,0:T(8,128)(2,1)S(1)} collective-permute-done((bf16[128,2048]{1,0:T(8,128)(2,1)S(1)}, bf16[128,2048]{1,0:T(8,128)(2,1)S(1)}, u32[]{:S(2)}, u32[]{:S(2)}) %collective-permute-start.56) | collective-permute-done | bytes 524320 | tf_op jit(solution)/shard_map/ppermute | solution.py:40
  573.0 34.6 %collective-permute-done.71 = bf16[512,1024]{1,0:T(8,128)(2,1)S(1)} collective-permute-done((bf16[512,1024]{1,0:T(8,128)(2,1)S(1)}, bf16[512,1024]{1,0:T(8,128)(2,1)S(1)}, u32[]{:S(2)}, u32[]{:S(2)}) %collective-permute-start.71) | collective-permute-done | bytes 1048608 | tf_op jit(solution)/shard_map/ppermute | solution.py:40
  610.2 19.8 %collective-permute-done.72 = bf16[512,512]{1,0:T(8,128)(2,1)S(1)} collective-permute-done((bf16[512,512]{1,0:T(8,128)(2,1)S(1)}, bf16[512,512]{1,0:T(8,128)(2,1)S(1)}, u32[]{:S(2)}, u32[]{:S(2)}) %collective-permute-start.72) | collective-permute-done | bytes 524320 | tf_op jit(solution)/shard_map/ppermute | solution.py:40
  643.8 8.5 %collective-permute-done.65 = f32[33,128]{1,0:T(8,128)S(1)} collective-permute-done((f32[33,128]{1,0:T(8,128)S(1)}, f32[33,128]{1,0:T(8,128)S(1)}, u32[]{:S(2)}, u32[]{:S(2)}) %collective-permute-start.65) | collective-permute-done | bytes 16928 | tf_op jit(solution)/shard_map/ppermute | solution.py:40
  666.5 9.1 %collective-permute-start.81 = (bf16[512,512]{1,0:T(8,128)(2,1)}, bf16[512,512]{1,0:T(8,128)(2,1)}, u32[]{:S(2)}, u32[]{:S(2)}) collective-permute-start(bf16[512,512]{1,0:T(8,128)(2,1)} %dynamic-slice_convert_fusion), channel_id=1, source_target_pairs={{0,8},{1,9},{2,10},{3,11},{4,12},{5,13},{6,14},{7,15},{8,0},{9,1},... | collective-permute-start | bytes 1572872 | tf_op jit(solution)/shard_map/ppermute | solution.py:40
  675.6 7.7 %collective-permute-done.70 = bf16[256,1024]{1,0:T(8,128)(2,1)} collective-permute-done((bf16[256,1024]{1,0:T(8,128)(2,1)}, bf16[256,1024]{1,0:T(8,128)(2,1)}, u32[]{:S(2)}, u32[]{:S(2)}) %collective-permute-start.70) | collective-permute-done | bytes 524320 | tf_op jit(solution)/shard_map/ppermute | solution.py:40
  697.4 9.5 %collective-permute-done.78 = bf16[512,512]{1,0:T(8,128)(2,1)S(1)} collective-permute-done((bf16[512,512]{1,0:T(8,128)(2,1)S(1)}, bf16[512,512]{1,0:T(8,128)(2,1)S(1)}, u32[]{:S(2)}, u32[]{:S(2)}) %collective-permute-start.78) | collective-permute-done | bytes 524320 | tf_op jit(solution)/shard_map/ppermute | solution.py:40
  709.0 7.4 collective-permute-done.75
  (484 shorter events, 360.5 us)
Async XLA Ops:
  7.2 157.4 %all-gather.4.cloned.1.call-start = ((), (), s32[]{:S(2)}) async-start(), calls=%async_computation.3 | async-start | bytes 3145728 | tf_op jit(solution)/shard_map/all_gather | solution.py:424
  41.8 51.7 %collective-permute-start.16 = (bf16[512,512]{1,0:T(8,128)(2,1)S(1)}, bf16[512,512]{1,0:T(8,128)(2,1)S(1)}, u32[]{:S(2)}, u32[]{:S(2)}) collective-permute-start(bf16[512,512]{1,0:T(8,128)(2,1)S(1)} %fusion.35), channel_id=1, source_target_pairs={{0,8},{1,9},{2,10},{3,11},{4,12},{5,13},{6,14},{7,15},{8,0},{9,1},... | collective-permute-start | bytes 1572872 | tf_op jit(solution)/shard_map/ppermute | solution.py:40
  49.5 44.0 %collective-permute-start.1 = (bf16[2,272,1024]{2,1,0:T(8,128)(2,1)}, bf16[2,272,1024]{2,1,0:T(8,128)(2,1)S(1)}, u32[]{:S(2)}, u32[]{:S(2)}) collective-permute-start(bf16[2,272,1024]{2,1,0:T(8,128)(2,1)} %pad_maximum_fusion.8.refs_6_.refs_9_), channel_id=1, source_target_pairs={{0,8},{1,9},{2,10},{3,11},{4,12},{5,13},{6,14},{7,15},{8,0},{9,1},... | collective-permute-start | bytes 3342344 | tf_op jit(solution)/shard_map/ppermute | solution.py:40
  56.6 41.9 %collective-permute-start.2 = (bf16[2,272,1024]{2,1,0:T(8,128)(2,1)}, bf16[2,272,1024]{2,1,0:T(8,128)(2,1)}, u32[]{:S(2)}, u32[]{:S(2)}) collective-permute-start(bf16[2,272,1024]{2,1,0:T(8,128)(2,1)} %pad_maximum_fusion.8.refs_6_.refs_9_), channel_id=1, source_target_pairs={{0,4},{1,5},{2,6},{3,7},{4,0},{5,1},{6,2},{7,3},{8,12},{9,13},{10,... | collective-permute-start | bytes 3342344 | tf_op jit(solution)/shard_map/ppermute | solution.py:40
  93.5 38.7 %collective-permute-start.6 = (bf16[512,1024]{1,0:T(8,128)(2,1)}, bf16[512,1024]{1,0:T(8,128)(2,1)}, u32[]{:S(2)}, u32[]{:S(2)}) collective-permute-start(bf16[512,1024]{1,0:T(8,128)(2,1)} %pad_maximum_fusion.11), channel_id=1, source_target_pairs={{0,8},{1,9},{2,10},{3,11},{4,12},{5,13},{6,14},{7,15},{8,0},{9,1},... | collective-permute-start | bytes 3145736 | tf_op jit(solution)/shard_map/ppermute | solution.py:40
  95.6 117.8 %all-gather.6.cloned.1.call-start = ((), (), s32[]{:S(2)}) async-start(), calls=%async_computation.4 | async-start | bytes 3145728 | tf_op jit(solution)/shard_map/all_gather | solution.py:424
  95.7 57.0 %collective-permute-start.19 = (bf16[512,512]{1,0:T(8,128)(2,1)}, bf16[512,512]{1,0:T(8,128)(2,1)S(1)}, u32[]{:S(2)}, u32[]{:S(2)}) collective-permute-start(bf16[512,512]{1,0:T(8,128)(2,1)} %fusion.33), channel_id=1, source_target_pairs={{0,8},{1,9},{2,10},{3,11},{4,12},{5,13},{6,14},{7,15},{8,0},{9,1},... | collective-permute-start | bytes 1572872 | tf_op jit(solution)/shard_map/ppermute | solution.py:40
  97.0 36.9 %collective-permute-start.3 = (bf16[2,272,1024]{2,1,0:T(8,128)(2,1)}, bf16[2,272,1024]{2,1,0:T(8,128)(2,1)S(1)}, u32[]{:S(2)}, u32[]{:S(2)}) collective-permute-start(bf16[2,272,1024]{2,1,0:T(8,128)(2,1)} %copy-done.36), channel_id=1, source_target_pairs={{0,4},{1,5},{2,6},{3,7},{4,0},{5,1},{6,2},{7,3},{8,12},{9,13},{10,... | collective-permute-start | bytes 3342344 | tf_op jit(solution)/shard_map/ppermute | solution.py:40
  154.0 117.0 %all-gather.8.cloned.1.call-start = ((), (), s32[]{:S(2)}) async-start(), calls=%async_computation.5 | async-start | bytes 3145728 | tf_op jit(solution)/shard_map/all_gather | solution.py:424
  164.6 72.8 %collective-permute-start.17 = (bf16[2048,512]{1,0:T(8,128)(2,1)}, bf16[2048,512]{1,0:T(8,128)(2,1)}, u32[]{:S(2)}, u32[]{:S(2)}) collective-permute-start(bf16[2048,512]{1,0:T(8,128)(2,1)} %all-gather.4.cloned.1.call-done), channel_id=1, source_target_pairs={{0,1},{1,0},{2,3},{3,2},{4,5},{5,4},{6,7},{7,6},{8,9},{9,8},{10,11... | collective-permute-start | bytes 6291464 | tf_op jit(solution)/shard_map/ppermute | solution.py:40
  180.6 483.3 %reduce-scatter.8.cloned.1.call-start = ((), (), s32[]{:S(2)}) async-start(), calls=%async_computation.8 | async-start | bytes 3145728 | tf_op jit(solution)/shard_map/reduce_scatter | solution.py:516
  213.4 77.0 %collective-permute-start.20 = (bf16[2048,512]{1,0:T(8,128)(2,1)}, bf16[2048,512]{1,0:T(8,128)(2,1)}, u32[]{:S(2)}, u32[]{:S(2)}) collective-permute-start(bf16[2048,512]{1,0:T(8,128)(2,1)} %all-gather.6.cloned.1.call-done), channel_id=1, source_target_pairs={{0,1},{1,0},{2,3},{3,2},{4,5},{5,4},{6,7},{7,6},{8,9},{9,8},{10,11... | collective-permute-start | bytes 6291464 | tf_op jit(solution)/shard_map/ppermute | solution.py:40
  226.0 78.1 %collective-permute-start.21 = (bf16[192,2048]{1,0:T(8,128)(2,1)}, bf16[192,2048]{1,0:T(8,128)(2,1)S(1)}, u32[]{:S(2)}, u32[]{:S(2)}) collective-permute-start(bf16[192,2048]{1,0:T(8,128)(2,1)} %pad_maximum_fusion.21), channel_id=1, source_target_pairs={{0,2},{1,3},{2,0},{3,1},{4,6},{5,7},{6,4},{7,5},{8,10},{9,11},{10,... | collective-permute-start | bytes 2359304 | tf_op jit(solution)/shard_map/ppermute | solution.py:40
  271.0 42.9 %collective-permute-start.26 = (bf16[512,2048]{1,0:T(8,128)(2,1)}, bf16[512,2048]{1,0:T(8,128)(2,1)S(1)}, u32[]{:S(2)}, u32[]{:S(2)}) collective-permute-start(bf16[512,2048]{1,0:T(8,128)(2,1)} %all-gather.8.cloned.1.call-done), channel_id=1, source_target_pairs={{0,1},{1,0},{2,3},{3,2},{4,5},{5,4},{6,7},{7,6},{8,9},{9,8},{10,11... | collective-permute-start | bytes 6291464 | tf_op jit(solution)/shard_map/ppermute | solution.py:40
  444.1 38.3 %collective-permute-start.45 = (bf16[192,2048]{1,0:T(8,128)(2,1)}, bf16[192,2048]{1,0:T(8,128)(2,1)}, u32[]{:S(2)}, u32[]{:S(2)}) collective-permute-start(bf16[192,2048]{1,0:T(8,128)(2,1)} %get-tuple-element.90), channel_id=1, source_target_pairs={{0,2},{1,3},{2,0},{3,1},{4,6},{5,7},{6,4},{7,5},{8,10},{9,11},{10,... | collective-permute-start | bytes 2359304 | tf_op jit(solution)/shard_map/ppermute | solution.py:40
  455.4 230.8 %reduce-scatter.6.cloned.1.call-start = ((), (), s32[]{:S(2)}) async-start(), calls=%async_computation.7 | async-start | bytes 3145728 | tf_op jit(solution)/shard_map/reduce_scatter | solution.py:516
  463.4 64.1 %collective-permute-start.74 = (bf16[2048,512]{1,0:T(8,128)(2,1)}, bf16[2048,512]{1,0:T(8,128)(2,1)}, u32[]{:S(2)}, u32[]{:S(2)}) collective-permute-start(bf16[2048,512]{1,0:T(8,128)(2,1)} %convolution_convert_fusion.4), channel_id=1, source_target_pairs={{0,1},{1,0},{2,3},{3,2},{4,5},{5,4},{6,7},{7,6},{8,9},{9,8},{10,11... | collective-permute-start | bytes 6291464 | tf_op jit(solution)/shard_map/ppermute | solution.py:40
  505.7 183.3 %reduce-scatter.4.cloned.1.call-start = ((), (), s32[]{:S(2)}) async-start(), calls=%async_computation.6 | async-start | bytes 3145728 | tf_op jit(solution)/shard_map/reduce_scatter | solution.py:516
  553.6 54.6 %collective-permute-start.58 = (bf16[256,2048]{1,0:T(8,128)(2,1)}, bf16[256,2048]{1,0:T(8,128)(2,1)S(1)}, u32[]{:S(2)}, u32[]{:S(2)}) collective-permute-start(bf16[256,2048]{1,0:T(8,128)(2,1)} %get-tuple-element.56), channel_id=1, source_target_pairs={{0,1},{1,0},{2,3},{3,2},{4,5},{5,4},{6,7},{7,6},{8,9},{9,8},{10,11... | collective-permute-start | bytes 3145736 | tf_op jit(solution)/shard_map/ppermute | solution.py:40
  560.3 71.6 %collective-permute-start.59 = (bf16[1024,512]{1,0:T(8,128)(2,1)S(1)}, bf16[1024,512]{1,0:T(8,128)(2,1)S(1)}, u32[]{:S(2)}, u32[]{:S(2)}) collective-permute-start(bf16[1024,512]{1,0:T(8,128)(2,1)S(1)} %slice.631), channel_id=1, source_target_pairs={{0,4},{1,5},{2,6},{3,7},{4,0},{5,1},{6,2},{7,3},{8,12},{9,13},{10,... | collective-permute-start | bytes 3145736 | tf_op jit(solution)/shard_map/ppermute | solution.py:40
  563.5 44.1 %collective-permute-start.71 = (bf16[512,1024]{1,0:T(8,128)(2,1)S(1)}, bf16[512,1024]{1,0:T(8,128)(2,1)S(1)}, u32[]{:S(2)}, u32[]{:S(2)}) collective-permute-start(bf16[512,1024]{1,0:T(8,128)(2,1)S(1)} %pad_maximum_fusion.20), channel_id=1, source_target_pairs={{0,4},{1,5},{2,6},{3,7},{4,0},{5,1},{6,2},{7,3},{8,12},{9,13},{10,... | collective-permute-start | bytes 3145736 | tf_op jit(solution)/shard_map/ppermute | solution.py:40
  564.2 67.7 %collective-permute-start.60 = (bf16[1024,512]{1,0:T(8,128)(2,1)S(1)}, bf16[1024,512]{1,0:T(8,128)(2,1)S(1)}, u32[]{:S(2)}, u32[]{:S(2)}) collective-permute-start(bf16[1024,512]{1,0:T(8,128)(2,1)S(1)} %pad_maximum_fusion.19), channel_id=1, source_target_pairs={{0,8},{1,9},{2,10},{3,11},{4,12},{5,13},{6,14},{7,15},{8,0},{9,1},... | collective-permute-start | bytes 3145736 | tf_op jit(solution)/shard_map/ppermute | solution.py:40
  572.9 57.3 %collective-permute-start.57 = (bf16[256,2048]{1,0:T(8,128)(2,1)S(1)}, bf16[256,2048]{1,0:T(8,128)(2,1)S(1)}, u32[]{:S(2)}, u32[]{:S(2)}) collective-permute-start(bf16[256,2048]{1,0:T(8,128)(2,1)S(1)} %pad_maximum_fusion.17), channel_id=1, source_target_pairs={{0,1},{1,0},{2,3},{3,2},{4,5},{5,4},{6,7},{7,6},{8,9},{9,8},{10,11... | collective-permute-start | bytes 3145736 | tf_op jit(solution)/shard_map/ppermute | solution.py:40
  661.3 57.5 %collective-permute-start.62 = (f32[256,2048]{1,0:T(8,128)S(1)}, f32[256,2048]{1,0:T(8,128)}, u32[]{:S(2)}, u32[]{:S(2)}) collective-permute-start(f32[256,2048]{1,0:T(8,128)S(1)} %fusion.8), channel_id=1, source_target_pairs={{0,1},{1,0},{2,3},{3,2},{4,5},{5,4},{6,7},{7,6},{8,9},{9,8},{10,11... | collective-permute-start | bytes 6291464 | tf_op jit(solution)/shard_map/ppermute | solution.py:40
  (106 other events, 1446.4 us)
Sparse Core Ops, SparseCore 0:
  95.7 56.7 all-gather.3
  154.6 58.6 all-gather.5
  215.5 55.4 all-gather.7
  455.5 52.2 reduce-scatter.7
  510.0 54.1 reduce-scatter.5
  566.9 54.3 reduce-scatter.3

commit v3 on v2

--- a/solution.py
+++ b/solution.py
@@ -29,6 +29,7 @@
         t = lax.axis_index("tensor")
         self.y, self.l, self.f = self.d % 2, (self.d // 2) % 2, self.d // 4
         self.x, self.c = t // 2, t % 2
+        self.near_groups = [[4 * f + low for low in range(4)] for f in range(self.far)]
         self.far_groups = [[4 * f + low for f in range(self.far)] for low in range(4)]
 
     def flip(self, v, dp_mask, tensor_mask=0):
@@ -410,42 +411,45 @@
     qkv = jnp.concatenate(
         [jnp.concatenate([w_q, key_matrix, value_matrix], axis=1), rider], axis=0
     )
-    qkv_own = jnp.stack(net.far_gather(qkv))
-
-    def swap_y(w, axis):
-        mine, other = [blocks_at(w, sub, [y, 2 + y], axis) for y in (net.y, 1 - net.y)]
-        return in_order(net.y, mine, net.flip_y(other), 1 - axis)
-
-    def swap_l(w, axis, *deps):
-        mine, other = halves(net.l, w, axis)
-        return in_order(net.l, mine, net.flip_l(after(other, *deps)), 1 - axis)
+
+    def exchange(w, split, concat):
+        return lax.all_to_all(
+            w, "dp", split, concat, axis_index_groups=net.near_groups, tiled=True
+        )
 
     def gather(w, axis):
         return lax.all_gather(
             w, "dp", axis=axis, axis_index_groups=net.far_groups, tiled=True
         )
 
+    w_gate, w_up, w_down = after((w_gate, w_up, w_down), qkv)
     o_pair = in_order(net.y, w_o, net.flip_y(w_o), 1)
-    gate = gather(swap_l(swap_y(w_gate, 1), 1), 0)
-    up, down = swap_y(w_up, 1), swap_y(w_down, 0)
-
+    qkv_own = jnp.stack(net.far_gather(qkv))
+    gate = exchange(w_gate, 1, 0)
+    up = exchange(after(w_up, gate), 1, 0)
+    down = exchange(after(w_down, up), 0, 1)
+    gate = gather(gate, 0)
     qkv_l, qkv_y = net.flip_l(qkv_own), net.flip_y(qkv_own)
-    o_far = net.absolute(net.far_gather(after(o_pair, qkv_own)), 1)
-    qkv_all = (qkv_own, qkv_l, qkv_y, net.flip_y(qkv_l))
-    o_l = net.flip_l(after(o_far, qkv_l))
-    up = gather(swap_l(up, 1, qkv_l), 0)
-    down = gather(swap_l(down, 0, qkv_all[3]), 1)
+    o_far = net.far_gather(after(o_pair, qkv_own))
+    o_far = net.absolute([after(o, qkv_l, qkv_y) for o in o_far], 1)
+    o_l = net.flip_l(o_far)
+    qkv_ly, up = pin(net.flip_y(qkv_l), up)
+    up = gather(up, 0)
+    qkv_ly, gate = pin(qkv_ly, gate)
+    qkv_all = (qkv_own, qkv_l, qkv_y, qkv_ly)
+
+    me = jnp.stack([net.d, net.c]).astype(jnp.int32)
+    cos_table, sin_table = tables(positions, HEAD_SIZE)
+    normed, qr, kr, v, p, attended = attend(
+        me, states, cos_table, sin_table, segments, qkv_all, fq, fk, far
+    )
+    o_l = after(o_l, attended)
     parts = []
     for n in range(far):
         block = slice(n * 2 * rp, (n + 1) * 2 * rp)
         parts.append(in_order(net.l, o_far[:, block], o_l[:, block], 1))
     full_o = jnp.concatenate(parts, axis=1)
 
-    me = jnp.stack([net.d, net.c]).astype(jnp.int32)
-    cos_table, sin_table = tables(positions, HEAD_SIZE)
-    normed, qr, kr, v, p, attended = attend(
-        me, states, cos_table, sin_table, segments, qkv_all, fq, fk, far
-    )
     rider = [w[k, rp : rp + 2] for w in qkv_all for k in range(far)]
     count = sum(e[1, 0].astype(F32) * 256.0 + e[1, 1].astype(F32) for e in rider)
 
@@ -474,23 +478,28 @@
     my_teacher = lax.dynamic_slice_in_dim(teacher, first_token, tok, 0).astype(F32)
     my_live = lax.dynamic_slice_in_dim(live, first_token, tok, 0)
 
+    attn_sum, down = pin(attn_sum, down)
+    down = gather(down, 1)
     full_gate = jnp.concatenate([gate, net.flip_c(gate)], axis=1)
-    full_up = jnp.concatenate([up, net.flip_c(up)], axis=1)
-    full_down = jnp.concatenate([down, net.flip_c(down)], axis=0)
     hidden = my_inputs + attn_sum
     recip_two = rms_scale(hidden)
     unit_two = hidden * recip_two
     near, last = net.cube_gather((unit_two * gain_two).astype(BF))
+    up = after(up, *near)
+    full_up = jnp.concatenate([up, net.flip_c(up)], axis=1)
     n2_near, n2_last = jnp.concatenate(near, axis=0), jnp.concatenate(last, axis=0)
 
     def act(n2):
         gate, up = dot(n2, full_gate), dot(n2, full_up)
         sig = jax.nn.sigmoid(gate)
         silu = gate * sig
-        return (silu * up).astype(BF), up * sig * (1.0 + gate * (1.0 - sig)), silu
+        by_gate = (up * sig * (1.0 + gate * (1.0 - sig))).astype(BF)
+        return (silu * up).astype(BF), by_gate, silu.astype(BF)
 
     act_near, by_gate_near, by_up_near = act(n2_near)
     act_last, by_gate_last, by_up_last = act(after(n2_last, act_near))
+    down = after(down, act_last)
+    full_down = jnp.concatenate([down, net.flip_c(down)], axis=0)
     y_last = dot(act_last, full_down).astype(BF)
     y_near = dot(after(act_near, y_last), full_down)
     mlp_sum = net.cube_reduce(split_parts(y_near, tok), split_parts(y_last, tok))
@@ -512,30 +521,28 @@
     act_all = jnp.concatenate([act_near, act_last], axis=0)
     n2_all = jnp.concatenate([n2_near, n2_last], axis=0)
 
-    def sum_back(mine, other, axis):
+    def sum_back(total, axis):
         return lax.psum_scatter(
-            add(mine, net.flip_c(other)),
-            "dp",
-            scatter_dimension=axis,
-            axis_index_groups=net.far_groups,
-            tiled=True,
-        ).astype(F32)
+            total, "dp", scatter_dimension=axis, axis_index_groups=net.far_groups, tiled=True
+        )
 
     down_other = tn(act_all[:, sub:], dy_all).astype(BF)
     down_mine = tn(act_all[:, :sub], dy_all).astype(BF)
-    down_sum = sum_back(down_mine, down_other, 1)
+    down_got = net.flip_c(down_other)
     grad_active = nt(after(dy_all, down_mine), full_down)
     dg_all = (grad_active * jnp.concatenate([by_gate_near, by_gate_last], axis=0)).astype(BF)
     du_all = (grad_active * jnp.concatenate([by_up_near, by_up_last], axis=0)).astype(BF)
+    dg_all, du_all, down_sum = pin(dg_all, du_all, add(down_mine, down_got))
+    down_sum = sum_back(down_sum, 1)
     dn_all = nt(dg_all, full_gate) + nt(du_all, full_up)
     dn_near, dn_last = dn_all[: 4 * tok], dn_all[4 * tok :].astype(BF)
     n2_all, dg_late, du_late = after((n2_all, dg_all, du_all), dn_last)
     gate_other = tn(n2_all, dg_late[:, sub:]).astype(BF)
     gate_mine = tn(n2_all, dg_late[:, :sub]).astype(BF)
-    gate_sum = sum_back(gate_mine, gate_other, 0)
+    gate_sum = sum_back(add(gate_mine, net.flip_c(gate_other)), 0)
     up_other = tn(n2_all, du_late[:, sub:]).astype(BF)
     up_mine = tn(n2_all, du_late[:, :sub]).astype(BF)
-    up_sum = sum_back(up_mine, up_other, 0)
+    up_sum = sum_back(add(up_mine, net.flip_c(up_other)), 0)
 
     back_two = net.cube_reduce(split_parts(dn_near, tok), split_parts(dn_last, tok))
     gain_two_grad, hidden_from_norm = norm_back(back_two, unit_two, recip_two, gain_two)
@@ -557,11 +564,13 @@
     gkv = [gkv[n * quarter : (n + 1) * quarter] for n in range(4)]
     q_got = net.flip_y(gq[half:])
     kv_got = net.flip_l(jnp.concatenate([gkv[1], gkv[3]], axis=0))
+    q_got, gate_sum = pin(q_got, gate_sum)
     q_got, kv_got, back_got = pin(q_got, kv_got, back_got)
     gq = add(gq[:half], q_got)
     gkv = add(jnp.concatenate([gkv[0], gkv[2]], axis=0), kv_got)
     q_got = net.flip_l(gq[quarter:])
     kv_got = net.flip_y(gkv[quarter:])
+    q_got, kv_got, up_sum = pin(q_got, kv_got, up_sum)
     gqkv = jnp.concatenate([add(gq[:quarter], q_got), add(gkv[:quarter], kv_got)], axis=1)
 
     other = blocks_at(grad_wo, rp, [2 * n + 1 - net.y for n in range(2 * far)], 1)
@@ -583,23 +592,9 @@
     result_q = result_qkv[:, :fq]
     result_k, result_v = result_qkv[:, fq : fq + fk], result_qkv[:, fq + fk :]
 
-    def exchange(total, axis):
-        cross = 1 - axis
-        mine, other = halves(net.l, total, axis)
-        got = net.flip_l(other.astype(BF)).astype(F32)
-        mine, other = halves(net.y, in_order(net.l, mine, got, cross), axis)
-        got = net.flip_y(other.astype(BF)).astype(F32)
-        parts = []
-        for n in range(2):
-            cut = functools.partial(
-                lax.slice_in_dim, start_index=n * sub, limit_index=(n + 1) * sub, axis=cross
-            )
-            parts.append(in_order(net.y, cut(mine), cut(got), cross))
-        return jnp.concatenate(parts, axis=cross)
-
-    result_down = exchange(after(down_sum, send), 1)
-    result_gate = exchange(after(gate_sum, back_got), 0)
-    result_up = exchange(after(up_sum, back_got), 0)
+    result_down = exchange(after(down_sum, send), 1, 0).astype(F32)
+    result_gate = exchange(after(gate_sum, back_got), 0, 1).astype(F32)
+    result_up = exchange(after(up_sum, far_blocks(gqkv)[0]), 0, 1).astype(F32)
 
     back_one = back_one.astype(F32) + back_got.astype(F32)
     xf = rows_of_core(states, net.c).astype(F32)

time: 753 us -> 729 us (0.968)
  matrix products: 92.4 us -> 72.4 us
  waiting for transfers between devices: 370 us -> 356 us
  other arithmetic: 74.7 us -> 61.7 us
  local copies, waits for them, and re-layouts: 52.8 us -> 63.9 us
  starting transfers between devices: 96.9 us -> 108 us
    all_gather x3, waiting for transfers between devices: 63.1 us -> 6.87 us  [gather(): lax.all_gather(w, 'dp', axis=axis, axis_index_groups=net.far_groups, tile...]
    ppermute x83 -> x71, waiting for transfers between devices: 306 us -> 339 us  [flip(): return lax.ppermute(v, AXES, pairs)]
    all_to_all x0 -> x6, starting transfers between devices: none -> 29 us  [exchange(): lax.all_to_all(w, 'dp', split, concat, axis_index_groups=net.near_groups,...]
    ppermute x83 -> x71, starting transfers between devices: 96.3 us -> 79 us  [flip(): return lax.ppermute(v, AXES, pairs)]
    all_to_all x0 -> x6, waiting for transfers between devices: none -> 10.8 us  [exchange(): lax.all_to_all(w, 'dp', split, concat, axis_index_groups=net.near_groups,...]
    dot_general x8, matrix products: 30 us -> 21.4 us  [dot(): return jnp.dot(left, right, preferred_element_type=F32)]
    unnamed x108 -> x158, local copies, waits for them, and re-layouts: 24.7 us -> 21.1 us
  transfers between devices with their start and end apart: 89 -> 83, of which waited for: 48 -> 42; matrix products, arithmetic and copies ran while one was open for 24% -> 21% of each run, Pallas kernels for 4% -> 4%
where the time goes in v3:
time: 729 us; the launch traced here: 720 us
  waiting for transfers between devices  356 us (49%)
  starting transfers between devices  108 us (15%)
  matrix products  72.4 us (10%)
  local copies, waits for them, and re-layouts  63.9 us (9%)
  other arithmetic  61.7 us (8%)
  between operations  29.4 us (4%)
  Pallas kernels  27.8 us (4%)
    ppermute x71, waiting for transfers between devices, flip(): return lax.ppermute(v, AXES, pairs)  339 us
    ppermute x71, starting transfers between devices, flip(): return lax.ppermute(v, AXES, pairs)  79 us
    all_to_all x6, starting transfers between devices, exchange(): lax.all_to_all(w, 'dp', split, concat, axis_index_groups=net.near_groups,...  29 us
    dot_general x8, matrix products, tn(): lax.dot_general(left, right, (((0,), (0,)), ((), ())), preferred_element_...  28.9 us
    dot_general x3, matrix products, nt(): lax.dot_general(left, right, (((1,), (1,)), ((), ())), preferred_element_...  22.2 us
    dot_general x8, matrix products, dot(): return jnp.dot(left, right, preferred_element_type=F32)  21.4 us
    unnamed x158, local copies, waits for them, and re-layouts  21.1 us
    pallas_call x1, Pallas kernels, attend_back(): pl.pallas_call(functools.partial(attend_back_kernel, far), out_shape=[jax...  17.4 us
  transfers between devices with their start and end apart: 83, of which 42 were waited for; matrix products, arithmetic and copies ran while one was open for 21% of the time, Pallas kernels for 4%

profile of v3, /device:TPU:0, one launch (start us, length us, event | category | flops | bytes accessed | tf_op | source)
XLA Modules:
  0.0 720.2 jit_solution(13205066781791693472)
XLA Ops:
  23.1 18.8 %collective-permute-done = bf16[272,1024]{1,0:T(8,128)(2,1)S(1)} collective-permute-done((bf16[272,1024]{1,0:T(8,128)(2,1)S(1)}, bf16[272,1024]{1,0:T(8,128)(2,1)S(1)}, u32[]{:S(2)}, u32[]{:S(2)}) %collective-permute-start) | collective-permute-done | bytes 557088 | tf_op jit(solution)/shard_map/ppermute | solution.py:41
  58.9 49.4 %collective-permute-done.5 = bf16[512,512]{1,0:T(8,128)(2,1)S(1)} collective-permute-done((bf16[512,512]{1,0:T(8,128)(2,1)S(1)}, bf16[512,512]{1,0:T(8,128)(2,1)S(1)}, u32[]{:S(2)}, u32[]{:S(2)}) %collective-permute-start.5) | collective-permute-done | bytes 524320 | tf_op jit(solution)/shard_map/ppermute | solution.py:41
  121.0 8.0 %collective-permute-done.3.refs_9_.refs_12_ = bf16[2,272,1024]{2,1,0:T(8,128)(2,1)} collective-permute-done((bf16[2,272,1024]{2,1,0:T(8,128)(2,1)}, bf16[2,272,1024]{2,1,0:T(8,128)(2,1)}, u32[]{:S(2)}, u32[]{:S(2)}) %collective-permute-start.3) | collective-permute-done | bytes 1114144 | tf_op jit(solution)/shard_map/ppermute | solution.py:41
  129.0 10.4 %attend.1 = (bf16[512,2048]{1,0:T(8,128)(2,1)}, bf16[512,512]{1,0:T(8,128)(2,1)}, bf16[512,256]{1,0:T(8,128)(2,1)}, bf16[512,256]{1,0:T(8,128)(2,1)}, bf16[2,512...) custom-call(s32[2]{0:T(128)} %pad_add_fusion.refs_0_, bf16[512,2048]{1,0:T(8,128)(2,1)} %refs_1_.1, ...), custom_call_target="tpu_custom_call" | custom-call | flops 2684354560 | bytes 12582912 | tf_op jit(solution)/shard_map/attend/pallas_call | solution.py:247
  142.4 7.9 %all-to-all-start.2 = ((bf16[4,512,256]{2,1,0:T(8,128)(2,1)}), bf16[4,512,256]{2,1,0:T(8,128)(2,1)}, u32[]{:S(2)}, u32[]{:S(2)}) async-start(bf16[4,512,256]{2,1,0:T(8,128)(2,1)} %bitcast.14), calls=%async_computation.2 | async-start | bytes 2097152 | tf_op jit(solution)/shard_map/all_to_all | solution.py:416
  157.9 8.1 %all-to-all-done.2 = bf16[4,512,256]{2,1,0:T(8,128)(2,1)} async-done(((bf16[4,512,256]{2,1,0:T(8,128)(2,1)}), bf16[4,512,256]{2,1,0:T(8,128)(2,1)}, u32[]{:S(2)}, u32[]{:S(2)}) %all-to-all-start.2) | async-done | bytes 1048608 | tf_op jit(solution)/shard_map/all_to_all | solution.py:416
  182.1 8.5 %collective-permute-done.10 = bf16[96,2048]{1,0:T(8,128)(2,1)S(1)} collective-permute-done((bf16[96,2048]{1,0:T(8,128)(2,1)S(1)}, bf16[96,2048]{1,0:T(8,128)(2,1)S(1)}, u32[]{:S(2)}, u32[]{:S(2)}) %collective-permute-start.10) | collective-permute-done | bytes 393248 | tf_op jit(solution)/shard_map/ppermute | solution.py:41
  216.0 23.4 %collective-permute-done.14 = bf16[64,2048]{1,0:T(8,128)(2,1)S(1)} collective-permute-done((bf16[64,2048]{1,0:T(8,128)(2,1)S(1)}, bf16[64,2048]{1,0:T(8,128)(2,1)S(1)}, u32[]{:S(2)}, u32[]{:S(2)}) %collective-permute-start.14) | collective-permute-done | bytes 262176 | tf_op jit(solution)/shard_map/ppermute | solution.py:41
  250.9 13.1 %collective-permute-done.17 = bf16[192,2048]{1,0:T(8,128)(2,1)S(1)} collective-permute-done((bf16[192,2048]{1,0:T(8,128)(2,1)}, bf16[192,2048]{1,0:T(8,128)(2,1)S(1)}, u32[]{:S(2)}, u32[]{:S(2)}) %collective-permute-start.17) | collective-permute-done | bytes 786464 | tf_op jit(solution)/shard_map/ppermute | solution.py:41
  263.9 11.9 %collective-permute-done.18 = bf16[192,2048]{1,0:T(8,128)(2,1)S(1)} collective-permute-done((bf16[192,2048]{1,0:T(8,128)(2,1)}, bf16[192,2048]{1,0:T(8,128)(2,1)S(1)}, u32[]{:S(2)}, u32[]{:S(2)}) %collective-permute-start.18) | collective-permute-done | bytes 786464 | tf_op jit(solution)/shard_map/ppermute | solution.py:41
  293.4 6.9 all-gather.8.cloned.1.call-done
  323.7 9.0 %collective-permute-done.27 = bf16[128,2048]{1,0:T(8,128)(2,1)S(1)} collective-permute-done((bf16[128,2048]{1,0:T(8,128)(2,1)S(1)}, bf16[128,2048]{1,0:T(8,128)(2,1)S(1)}, u32[]{:S(2)}, u32[]{:S(2)}) %collective-permute-start.27) | collective-permute-done | bytes 524320 | tf_op jit(solution)/shard_map/ppermute | solution.py:41
  336.9 9.4 %collective-permute-done.28 = bf16[64,2048]{1,0:T(8,128)(2,1)S(1)} collective-permute-done((bf16[64,2048]{1,0:T(8,128)(2,1)S(1)}, bf16[64,2048]{1,0:T(8,128)(2,1)S(1)}, u32[]{:S(2)}, u32[]{:S(2)}) %collective-permute-start.28) | collective-permute-done | bytes 262176 | tf_op jit(solution)/shard_map/ppermute | solution.py:41
  428.6 7.1 fusion.76
  435.8 8.4 %fusion.72 = (bf16[1024,2048]{1,0:T(8,128)(2,1)S(1)}, f32[1024,2048]{1,0:T(8,128)}) fusion(f32[1024,2048]{1,0:T(8,128)S(1)} %fusion.76, bf16[1024,1024]{1,0:T(8,128)(2,1)} %get-tuple-element.98, bf16[2048,1024]{1,0:T(8,128)(2,1)S(1)} %copy-done.31), kind=kOutput, calls=%fused_computation.332 | convolution fusion | flops 4299161600 | bytes 27262976 | tf_op jit(solution)/shard_map/dot_general | solution.py:155
  467.5 26.9 %collective-permute-done.47 = bf16[64,2048]{1,0:T(8,128)(2,1)S(1)} collective-permute-done((bf16[64,2048]{1,0:T(8,128)(2,1)S(1)}, bf16[64,2048]{1,0:T(8,128)(2,1)S(1)}, u32[]{:S(2)}, u32[]{:S(2)}) %collective-permute-start.47) | collective-permute-done | bytes 262176 | tf_op jit(solution)/shard_map/ppermute | solution.py:41
  500.7 7.2 %collective-permute-done.44 = bf16[96,2048]{1,0:T(8,128)(2,1)S(1)} collective-permute-done((bf16[96,2048]{1,0:T(8,128)(2,1)S(1)}, bf16[96,2048]{1,0:T(8,128)(2,1)S(1)}, u32[]{:S(2)}, u32[]{:S(2)}) %collective-permute-start.44) | collective-permute-done | bytes 393248 | tf_op jit(solution)/shard_map/ppermute | solution.py:41
  520.6 8.1 %collective-permute-done.49 = bf16[128,2048]{1,0:T(8,128)(2,1)S(1)} collective-permute-done((bf16[128,2048]{1,0:T(8,128)(2,1)S(1)}, bf16[128,2048]{1,0:T(8,128)(2,1)S(1)}, u32[]{:S(2)}, u32[]{:S(2)}) %collective-permute-start.49) | collective-permute-done | bytes 524320 | tf_op jit(solution)/shard_map/ppermute | solution.py:41
  530.0 6.9 add_convert_fusion
  538.6 17.4 %attend_back.1 = (bf16[512,1024]{1,0:T(8,128)(2,1)}, bf16[256,2048]{1,0:T(8,128)(2,1)}, bf16[256,2048]{1,0:T(8,128)(2,1)}) custom-call(s32[2]{0:T(128)} %pad_add_fusion.refs_0_, bf16[512,2048]{1,0:T(8,128)(2,1)} %pad_maximum_fusion.3.refs_1_, bf16[512,2048]{1,0:T(8,128)(2,1)} %copy-done, bf16[512,512]{1,0:T(8,128)(2,1)} %get-tuple-element.87.refs_3_, ...), custom_call_target="tpu_custom_call" | custom-call | flops 4563402752 | bytes 16777216 | tf_op jit(solution)/shard_map/attend_back/pallas_call | solution.py:331
  573.1 11.2 %collective-permute-done.68 = bf16[512,1024]{1,0:T(8,128)(2,1)S(1)} collective-permute-done((bf16[512,1024]{1,0:T(8,128)(2,1)S(1)}, bf16[512,1024]{1,0:T(8,128)(2,1)S(1)}, u32[]{:S(2)}, u32[]{:S(2)}) %collective-permute-start.68) | collective-permute-done | bytes 1048608 | tf_op jit(solution)/shard_map/ppermute | solution.py:41
  596.9 31.5 %collective-permute-done.69 = bf16[512,512]{1,0:T(8,128)(2,1)} collective-permute-done((bf16[512,512]{1,0:T(8,128)(2,1)}, bf16[512,512]{1,0:T(8,128)(2,1)}, u32[]{:S(2)}, u32[]{:S(2)}) %collective-permute-start.69) | collective-permute-done | bytes 524320 | tf_op jit(solution)/shard_map/ppermute | solution.py:41
  643.2 11.7 %collective-permute-done.64 = bf16[512,512]{1,0:T(8,128)(2,1)} collective-permute-done((bf16[512,512]{1,0:T(8,128)(2,1)S(1)}, bf16[512,512]{1,0:T(8,128)(2,1)}, u32[]{:S(2)}, u32[]{:S(2)}) %collective-permute-start.64) | collective-permute-done | bytes 524320 | tf_op jit(solution)/shard_map/ppermute | solution.py:41
  668.6 15.4 %collective-permute-done.62 = f32[33,128]{1,0:T(8,128)S(1)} collective-permute-done((f32[33,128]{1,0:T(8,128)S(1)}, f32[33,128]{1,0:T(8,128)S(1)}, u32[]{:S(2)}, u32[]{:S(2)}) %collective-permute-start.62) | collective-permute-done | bytes 16928 | tf_op jit(solution)/shard_map/ppermute | solution.py:41
  (493 shorter events, 354.1 us)
Async XLA Ops:
  18.5 110.5 %all-gather.4.cloned.1.call-start = ((), (), s32[]{:S(2)}) async-start(), calls=%async_computation.9 | async-start | bytes 3145728 | tf_op jit(solution)/shard_map/all_gather | solution.py:421
  43.2 65.1 %collective-permute-start.2 = (bf16[2,272,1024]{2,1,0:T(8,128)(2,1)}, bf16[2,272,1024]{2,1,0:T(8,128)(2,1)}, u32[]{:S(2)}, u32[]{:S(2)}) collective-permute-start(bf16[2,272,1024]{2,1,0:T(8,128)(2,1)} %pad_maximum_fusion.5.refs_6_.refs_9_), channel_id=1, source_target_pairs={{0,4},{1,5},{2,6},{3,7},{4,0},{5,1},{6,2},{7,3},{8,12},{9,13},{10,... | collective-permute-start | bytes 3342344 | tf_op jit(solution)/shard_map/ppermute | solution.py:41
  44.9 63.4 %collective-permute-start.1 = (bf16[2,272,1024]{2,1,0:T(8,128)(2,1)}, bf16[2,272,1024]{2,1,0:T(8,128)(2,1)}, u32[]{:S(2)}, u32[]{:S(2)}) collective-permute-start(bf16[2,272,1024]{2,1,0:T(8,128)(2,1)} %pad_maximum_fusion.5.refs_6_.refs_9_), channel_id=1, source_target_pairs={{0,8},{1,9},{2,10},{3,11},{4,12},{5,13},{6,14},{7,15},{8,0},{9,1},... | collective-permute-start | bytes 3342344 | tf_op jit(solution)/shard_map/ppermute | solution.py:41
  50.8 57.5 %collective-permute-start.5 = (bf16[512,512]{1,0:T(8,128)(2,1)S(1)}, bf16[512,512]{1,0:T(8,128)(2,1)S(1)}, u32[]{:S(2)}, u32[]{:S(2)}) collective-permute-start(bf16[512,512]{1,0:T(8,128)(2,1)S(1)} %pad_maximum_fusion.21), channel_id=1, source_target_pairs={{0,16},{1,17},{2,18},{3,19},{4,20},{5,21},{6,22},{7,23},{8,24},{9,... | collective-permute-start | bytes 1572872 | tf_op jit(solution)/shard_map/ppermute | solution.py:41
  55.3 64.3 %all-to-all-start.1 = ((bf16[256,4,512]{0,2,1:T(8,128)(2,1)}), bf16[256,4,512]{0,2,1:T(8,128)(2,1)S(1)}, u32[]{:S(2)}, u32[]{:S(2)}) async-start(bf16[256,4,512]{0,2,1:T(8,128)(2,1)} %bitcast.11), calls=%async_computation.1 | async-start | bytes 2097152 | tf_op jit(solution)/shard_map/all_to_all | solution.py:416
  150.3 90.0 %all-gather.6.cloned.1.call-start = ((), (), s32[]{:S(2)}) async-start(), calls=%async_computation.10 | async-start | bytes 3145728 | tf_op jit(solution)/shard_map/all_gather | solution.py:421
  181.3 118.9 %all-gather.8.cloned.1.call-start = ((), (), s32[]{:S(2)}) async-start(), calls=%async_computation.11 | async-start | bytes 3145728 | tf_op jit(solution)/shard_map/all_gather | solution.py:421
  181.4 63.8 %collective-permute-start.15 = (bf16[2048,512]{1,0:T(8,128)(2,1)}, bf16[2048,512]{1,0:T(8,128)(2,1)}, u32[]{:S(2)}, u32[]{:S(2)}) collective-permute-start(bf16[2048,512]{1,0:T(8,128)(2,1)} %all-gather.4.cloned.1.call-done), channel_id=1, source_target_pairs={{0,1},{1,0},{2,3},{3,2},{4,5},{5,4},{6,7},{7,6},{8,9},{9,8},{10,11... | collective-permute-start | bytes 6291464 | tf_op jit(solution)/shard_map/ppermute | solution.py:41
  243.5 346.6 %reduce-scatter.8.cloned.1.call-start = ((), (), s32[]{:S(2)}) async-start(), calls=%async_computation.14 | async-start | bytes 3145728 | tf_op jit(solution)/shard_map/reduce_scatter | solution.py:525
  446.0 185.7 %reduce-scatter.4.cloned.1.call-start = ((), (), s32[]{:S(2)}) async-start(), calls=%async_computation.12 | async-start | bytes 3145728 | tf_op jit(solution)/shard_map/reduce_scatter | solution.py:525
  447.8 46.9 %collective-permute-start.40 = (bf16[192,2048]{1,0:T(8,128)(2,1)}, bf16[192,2048]{1,0:T(8,128)(2,1)S(1)}, u32[]{:S(2)}, u32[]{:S(2)}) collective-permute-start(bf16[192,2048]{1,0:T(8,128)(2,1)} %get-tuple-element.134), channel_id=1, source_target_pairs={{0,2},{1,3},{2,0},{3,1},{4,6},{5,7},{6,4},{7,5},{8,10},{9,11},{10,... | collective-permute-start | bytes 2359304 | tf_op jit(solution)/shard_map/ppermute | solution.py:41
  449.6 45.1 %collective-permute-start.43 = (bf16[192,2048]{1,0:T(8,128)(2,1)S(1)}, bf16[192,2048]{1,0:T(8,128)(2,1)S(1)}, u32[]{:S(2)}, u32[]{:S(2)}) collective-permute-start(bf16[192,2048]{1,0:T(8,128)(2,1)S(1)} %get-tuple-element.135), channel_id=1, source_target_pairs={{0,8},{1,9},{2,10},{3,11},{4,12},{5,13},{6,14},{7,15},{8,0},{9,1},... | collective-permute-start | bytes 2359304 | tf_op jit(solution)/shard_map/ppermute | solution.py:41
  467.0 62.9 %collective-permute-start.66 = (bf16[2048,512]{1,0:T(8,128)(2,1)}, bf16[2048,512]{1,0:T(8,128)(2,1)}, u32[]{:S(2)}, u32[]{:S(2)}) collective-permute-start(bf16[2048,512]{1,0:T(8,128)(2,1)} %convolution_convert_fusion.1), channel_id=1, source_target_pairs={{0,1},{1,0},{2,3},{3,2},{4,5},{5,4},{6,7},{7,6},{8,9},{9,8},{10,11... | collective-permute-start | bytes 6291464 | tf_op jit(solution)/shard_map/ppermute | solution.py:41
  467.0 43.6 %collective-permute-start.55 = (bf16[2048,512]{1,0:T(8,128)(2,1)S(1)}, bf16[2048,512]{1,0:T(8,128)(2,1)S(1)}, u32[]{:S(2)}, u32[]{:S(2)}) collective-permute-start(bf16[2048,512]{1,0:T(8,128)(2,1)S(1)} %convolution_convert_fusion.3), channel_id=1, source_target_pairs={{0,1},{1,0},{2,3},{3,2},{4,5},{5,4},{6,7},{7,6},{8,9},{9,8},{10,11... | collective-permute-start | bytes 6291464 | tf_op jit(solution)/shard_map/ppermute | solution.py:41
  514.5 140.7 %reduce-scatter.6.cloned.1.call-start = ((), (), s32[]{:S(2)}) async-start(), calls=%async_computation.13 | async-start | bytes 3145728 | tf_op jit(solution)/shard_map/reduce_scatter | solution.py:525
  565.8 65.9 %collective-permute-start.54 = (bf16[1024,512]{1,0:T(8,128)(2,1)}, bf16[1024,512]{1,0:T(8,128)(2,1)}, u32[]{:S(2)}, u32[]{:S(2)}) collective-permute-start(bf16[1024,512]{1,0:T(8,128)(2,1)} %slice.578), channel_id=1, source_target_pairs={{0,4},{1,5},{2,6},{3,7},{4,0},{5,1},{6,2},{7,3},{8,12},{9,13},{10,... | collective-permute-start | bytes 3145736 | tf_op jit(solution)/shard_map/ppermute | solution.py:41
  568.3 63.4 %collective-permute-start.56 = (bf16[1024,512]{1,0:T(8,128)(2,1)}, bf16[1024,512]{1,0:T(8,128)(2,1)}, u32[]{:S(2)}, u32[]{:S(2)}) collective-permute-start(bf16[1024,512]{1,0:T(8,128)(2,1)} %pad_maximum_fusion.13), channel_id=1, source_target_pairs={{0,8},{1,9},{2,10},{3,11},{4,12},{5,13},{6,14},{7,15},{8,0},{9,1},... | collective-permute-start | bytes 3145736 | tf_op jit(solution)/shard_map/ppermute | solution.py:41
  571.4 60.3 %collective-permute-start.57 = (bf16[256,2048]{1,0:T(8,128)(2,1)S(1)}, bf16[256,2048]{1,0:T(8,128)(2,1)S(1)}, u32[]{:S(2)}, u32[]{:S(2)}) collective-permute-start(bf16[256,2048]{1,0:T(8,128)(2,1)S(1)} %add_convert_fusion.6), channel_id=1, source_target_pairs={{0,2},{1,3},{2,0},{3,1},{4,6},{5,7},{6,4},{7,5},{8,10},{9,11},{10,... | collective-permute-start | bytes 3145736 | tf_op jit(solution)/shard_map/ppermute | solution.py:41
  586.4 42.0 %collective-permute-start.69 = (bf16[512,512]{1,0:T(8,128)(2,1)}, bf16[512,512]{1,0:T(8,128)(2,1)}, u32[]{:S(2)}, u32[]{:S(2)}) collective-permute-start(bf16[512,512]{1,0:T(8,128)(2,1)} %pad_maximum_fusion.24), channel_id=1, source_target_pairs={{0,8},{1,9},{2,10},{3,11},{4,12},{5,13},{6,14},{7,15},{8,0},{9,1},... | collective-permute-start | bytes 1572872 | tf_op jit(solution)/shard_map/ppermute | solution.py:41
  590.1 73.5 %collective-permute-start.52 = (bf16[256,2048]{1,0:T(8,128)(2,1)}, bf16[256,2048]{1,0:T(8,128)(2,1)}, u32[]{:S(2)}, u32[]{:S(2)}) collective-permute-start(bf16[256,2048]{1,0:T(8,128)(2,1)} %pad_maximum_fusion.11), channel_id=1, source_target_pairs={{0,1},{1,0},{2,3},{3,2},{4,5},{5,4},{6,7},{7,6},{8,9},{9,8},{10,11... | collective-permute-start | bytes 3145736 | tf_op jit(solution)/shard_map/ppermute | solution.py:41
  592.4 64.2 %all-to-all-start.5 = ((bf16[512,4,256]{2,0,1:T(8,128)(2,1)}), bf16[512,4,256]{2,0,1:T(8,128)(2,1)}, u32[]{:S(2)}, u32[]{:S(2)}) async-start(bf16[512,4,256]{2,0,1:T(8,128)(2,1)} %bitcast.110), calls=%async_computation.8 | async-start | bytes 2097152 | tf_op jit(solution)/shard_map/all_to_all | solution.py:416
  630.5 56.5 %collective-permute-start.70 = (bf16[512,256]{1,0:T(8,128)(2,1)S(1)}, bf16[512,256]{1,0:T(8,128)(2,1)}, u32[]{:S(2)}, u32[]{:S(2)}) collective-permute-start(bf16[512,256]{1,0:T(8,128)(2,1)S(1)} %constant_dynamic-slice_fusion), channel_id=1, source_target_pairs={{0,16},{1,17},{2,18},{3,19},{4,20},{5,21},{6,22},{7,23},{8,24},{9,... | collective-permute-start | bytes 786440 | tf_op jit(solution)/shard_map/ppermute | solution.py:41
  643.2 62.2 %collective-permute-start.58 = (f32[256,2048]{1,0:T(8,128)S(1)}, f32[256,2048]{1,0:T(8,128)}, u32[]{:S(2)}, u32[]{:S(2)}) collective-permute-start(f32[256,2048]{1,0:T(8,128)S(1)} %fusion.6), channel_id=1, source_target_pairs={{0,1},{1,0},{2,3},{3,2},{4,5},{5,4},{6,7},{7,6},{8,9},{9,8},{10,11... | collective-permute-start | bytes 6291464 | tf_op jit(solution)/shard_map/ppermute | solution.py:41
  656.6 36.1 %all-to-all-start.3 = ((bf16[4,256,512]{2,1,0:T(8,128)(2,1)}), bf16[4,256,512]{2,1,0:T(8,128)(2,1)}, u32[]{:S(2)}, u32[]{:S(2)}) async-start(bf16[4,256,512]{2,1,0:T(8,128)(2,1)} %bitcast.119), calls=%async_computation.5 | async-start | bytes 2097152 | tf_op jit(solution)/shard_map/all_to_all | solution.py:416
  (125 other events, 1644.6 us)
Sparse Core Ops, SparseCore 0:
  50.8 69.6 all-gather.3
  181.4 56.8 all-gather.5
  243.6 56.6 all-gather.7
  446.1 54.6 reduce-scatter.7
  514.6 53.6 reduce-scatter.3
  570.4 53.2 reduce-scatter.5

commit v4 on v3

--- a/solution.py
+++ b/solution.py
@@ -103,7 +103,8 @@
         return parts, last
 
     def cube_flip(self, part, step, v):
-        return (self.flip_l, self.flip_y, self.flip_x)[(part + step) % 3](v)
+        orders = ((self.flip_l, self.flip_x, self.flip_y), (self.flip_y, self.flip_l, self.flip_x))
+        return orders[part][step](v)
 
     def cube_reduce(self, near, last):
         got = [self.cube_flip(n, 2, v.astype(BF)) for n, v in enumerate(last)]
@@ -118,8 +119,7 @@
 
 
 def part_rows(n):
-    one = -(-n // 48) * 16
-    return [(0, one), (one, 2 * one), (2 * one, n)]
+    return [(0, n // 2), (n // 2, n)]
 
 
 def split_parts(v, n):
@@ -431,7 +431,7 @@
     gate = gather(gate, 0)
     qkv_l, qkv_y = net.flip_l(qkv_own), net.flip_y(qkv_own)
     o_far = net.far_gather(after(o_pair, qkv_own))
-    o_far = net.absolute([after(o, qkv_l, qkv_y) for o in o_far], 1)
+    o_far = net.absolute(o_far, 1)
     o_l = net.flip_l(o_far)
     qkv_ly, up = pin(net.flip_y(qkv_l), up)
     up = gather(up, 0)
@@ -480,6 +480,7 @@
 
     attn_sum, down = pin(attn_sum, down)
     down = gather(down, 1)
+    gate = after(gate, attn_sum)
     full_gate = jnp.concatenate([gate, net.flip_c(gate)], axis=1)
     hidden = my_inputs + attn_sum
     recip_two = rms_scale(hidden)
@@ -534,7 +535,9 @@
     du_all = (grad_active * jnp.concatenate([by_up_near, by_up_last], axis=0)).astype(BF)
     dg_all, du_all, down_sum = pin(dg_all, du_all, add(down_mine, down_got))
     down_sum = sum_back(down_sum, 1)
-    dn_all = nt(dg_all, full_gate) + nt(du_all, full_up)
+    dn_all = nt(
+        jnp.concatenate([dg_all, du_all], axis=1), jnp.concatenate([full_gate, full_up], axis=1)
+    )
     dn_near, dn_last = dn_all[: 4 * tok], dn_all[4 * tok :].astype(BF)
     n2_all, dg_late, du_late = after((n2_all, dg_all, du_all), dn_last)
     gate_other = tn(n2_all, dg_late[:, sub:]).astype(BF)

time: 729 us -> 676 us (0.927)
  waiting for transfers between devices: 356 us -> 320 us
  starting transfers between devices: 108 us -> 97 us
    ppermute x71 -> x59, waiting for transfers between devices: 339 us -> 308 us  [flip(): return lax.ppermute(v, AXES, pairs)]
    ppermute x71 -> x59, starting transfers between devices: 79 us -> 71 us  [flip(): return lax.ppermute(v, AXES, pairs)]
    unnamed x158 -> x143, local copies, waits for them, and re-layouts: 21.1 us -> 26.1 us
    dot_general x3 -> x2, matrix products: 22.2 us -> 21.7 us  [nt(): lax.dot_general(left, right, (((1,), (1,)), ((), ())), preferred_element_...]
  transfers between devices with their start and end apart: 83 -> 71, of which waited for: 42 -> 33; matrix products, arithmetic and copies ran while one was open for 21% -> 24% of each run, Pallas kernels for 4% -> 4%
where the time goes in v4:
time: 676 us; the launch traced here: 667 us
  waiting for transfers between devices  320 us (47%)
  starting transfers between devices  97 us (14%)
  matrix products  69.1 us (10%)
  local copies, waits for them, and re-layouts  66.6 us (10%)
  other arithmetic  57.7 us (9%)
  between operations  29.5 us (4%)
  Pallas kernels  27.6 us (4%)
    ppermute x59, waiting for transfers between devices, flip(): return lax.ppermute(v, AXES, pairs)  308 us
    ppermute x59, starting transfers between devices, flip(): return lax.ppermute(v, AXES, pairs)  71 us
    unnamed x143, local copies, waits for them, and re-layouts  26.1 us
    dot_general x8, matrix products, tn(): lax.dot_general(left, right, (((0,), (0,)), ((), ())), preferred_element_...  25.6 us
    all_to_all x6, starting transfers between devices, exchange(): lax.all_to_all(w, 'dp', split, concat, axis_index_groups=net.near_groups,...  25.3 us
    dot_general x8, matrix products, dot(): return jnp.dot(left, right, preferred_element_type=F32)  21.8 us
    dot_general x2, matrix products, nt(): lax.dot_general(left, right, (((1,), (1,)), ((), ())), preferred_element_...  21.7 us
    pallas_call x1, Pallas kernels, attend_back(): pl.pallas_call(functools.partial(attend_back_kernel, far), out_shape=[jax...  17.2 us
  transfers between devices with their start and end apart: 71, of which 33 were waited for; matrix products, arithmetic and copies ran while one was open for 24% of the time, Pallas kernels for 4%

profile of v4, /device:TPU:0, one launch (start us, length us, event | category | flops | bytes accessed | tf_op | source)
XLA Modules:
  0.0 667.2 jit_solution(2640755560198846979)
XLA Ops:
  23.1 18.8 %collective-permute-done = bf16[272,1024]{1,0:T(8,128)(2,1)S(1)} collective-permute-done((bf16[272,1024]{1,0:T(8,128)(2,1)S(1)}, bf16[272,1024]{1,0:T(8,128)(2,1)S(1)}, u32[]{:S(2)}, u32[]{:S(2)}) %collective-permute-start) | collective-permute-done | bytes 557088 | tf_op jit(solution)/shard_map/ppermute | solution.py:41
  59.4 36.5 %collective-permute-done.1.refs_7_.refs_10_ = bf16[2,272,1024]{2,1,0:T(8,128)(2,1)} collective-permute-done((bf16[2,272,1024]{2,1,0:T(8,128)(2,1)}, bf16[2,272,1024]{2,1,0:T(8,128)(2,1)}, u32[]{:S(2)}, u32[]{:S(2)}) %collective-permute-start.1) | collective-permute-done | bytes 1114144 | tf_op jit(solution)/shard_map/ppermute | solution.py:41
  97.3 9.4 %collective-permute-done.5 = bf16[512,512]{1,0:T(8,128)(2,1)S(1)} collective-permute-done((bf16[512,512]{1,0:T(8,128)(2,1)S(1)}, bf16[512,512]{1,0:T(8,128)(2,1)S(1)}, u32[]{:S(2)}, u32[]{:S(2)}) %collective-permute-start.5) | collective-permute-done | bytes 524320 | tf_op jit(solution)/shard_map/ppermute | solution.py:41
  123.2 10.4 %attend.1 = (bf16[512,2048]{1,0:T(8,128)(2,1)}, bf16[512,512]{1,0:T(8,128)(2,1)}, bf16[512,256]{1,0:T(8,128)(2,1)}, bf16[512,256]{1,0:T(8,128)(2,1)}, bf16[2,512...) custom-call(s32[2]{0:T(128)} %pad_add_fusion.refs_0_, bf16[512,2048]{1,0:T(8,128)(2,1)} %refs_1_.1, ...), custom_call_target="tpu_custom_call" | custom-call | flops 2684354560 | bytes 12582912 | tf_op jit(solution)/shard_map/attend/pallas_call | solution.py:247
  152.0 8.0 %all-to-all-done.2 = bf16[4,512,256]{2,1,0:T(8,128)(2,1)} async-done(((bf16[4,512,256]{2,1,0:T(8,128)(2,1)}), bf16[4,512,256]{2,1,0:T(8,128)(2,1)}, u32[]{:S(2)}, u32[]{:S(2)}) %all-to-all-start.2) | async-done | bytes 1048608 | tf_op jit(solution)/shard_map/all_to_all | solution.py:416
  169.1 11.8 %collective-permute-done.9 = bf16[64,2048]{1,0:T(8,128)(2,1)S(1)} collective-permute-done((bf16[64,2048]{1,0:T(8,128)(2,1)S(1)}, bf16[64,2048]{1,0:T(8,128)(2,1)S(1)}, u32[]{:S(2)}, u32[]{:S(2)}) %collective-permute-start.9) | collective-permute-done | bytes 262176 | tf_op jit(solution)/shard_map/ppermute | solution.py:41
  183.2 10.1 %collective-permute-done.10 = bf16[128,2048]{1,0:T(8,128)(2,1)S(1)} collective-permute-done((bf16[128,2048]{1,0:T(8,128)(2,1)S(1)}, bf16[128,2048]{1,0:T(8,128)(2,1)S(1)}, u32[]{:S(2)}, u32[]{:S(2)}) %collective-permute-start.10) | collective-permute-done | bytes 524320 | tf_op jit(solution)/shard_map/ppermute | solution.py:41
  209.8 7.8 %collective-permute-done.12 = bf16[128,2048]{1,0:T(8,128)(2,1)S(1)} collective-permute-done((bf16[128,2048]{1,0:T(8,128)(2,1)S(1)}, bf16[128,2048]{1,0:T(8,128)(2,1)S(1)}, u32[]{:S(2)}, u32[]{:S(2)}) %collective-permute-start.12) | collective-permute-done | bytes 524320 | tf_op jit(solution)/shard_map/ppermute | solution.py:41
  230.3 17.6 %collective-permute-done.16 = bf16[256,2048]{1,0:T(8,128)(2,1)S(1)} collective-permute-done((bf16[256,2048]{1,0:T(8,128)(2,1)}, bf16[256,2048]{1,0:T(8,128)(2,1)S(1)}, u32[]{:S(2)}, u32[]{:S(2)}) %collective-permute-start.16) | collective-permute-done | bytes 1048608 | tf_op jit(solution)/shard_map/ppermute | solution.py:41
  282.9 16.7 %collective-permute-done.18 = bf16[256,2048]{1,0:T(8,128)(2,1)S(1)} collective-permute-done((bf16[256,2048]{1,0:T(8,128)(2,1)S(1)}, bf16[256,2048]{1,0:T(8,128)(2,1)S(1)}, u32[]{:S(2)}, u32[]{:S(2)}) %collective-permute-start.18) | collective-permute-done | bytes 1048608 | tf_op jit(solution)/shard_map/ppermute | solution.py:41
  315.8 6.4 collective-permute-done.19
  342.4 7.2 %collective-permute-done.25 = bf16[128,2048]{1,0:T(8,128)(2,1)S(1)} collective-permute-done((bf16[128,2048]{1,0:T(8,128)(2,1)S(1)}, bf16[128,2048]{1,0:T(8,128)(2,1)S(1)}, u32[]{:S(2)}, u32[]{:S(2)}) %collective-permute-start.25) | collective-permute-done | bytes 524320 | tf_op jit(solution)/shard_map/ppermute | solution.py:41
  352.1 17.4 %collective-permute-done.28 = bf16[256,2048]{1,0:T(8,128)(2,1)S(1)} collective-permute-done((bf16[256,2048]{1,0:T(8,128)(2,1)S(1)}, bf16[256,2048]{1,0:T(8,128)(2,1)S(1)}, u32[]{:S(2)}, u32[]{:S(2)}) %collective-permute-start.28) | collective-permute-done | bytes 1048608 | tf_op jit(solution)/shard_map/ppermute | solution.py:41
  376.5 6.2 multiply_convert_fusion
  385.1 15.4 %fusion.80 = (bf16[1024,2048]{1,0:T(8,128)(2,1)}, f32[1024,2048]{1,0:T(8,128)}) fusion(bf16[2048,512]{1,0:T(8,128)(2,1)} %copy-done.28, bf16[2048,512]{1,0:T(8,128)(2,1)} %all-gather.6.cloned.1.call-done, bf16[2048,512]{1,0:T(8,128)(2,1)} %collective-permute-done.13, bf16[2048,512]{1,0:T(8,128)(2,1)} %all-gather.4.cloned.1.call-done, ...), kind=kOutput, calls=%fused_computation.316 | convolution fusion | flops 8633974784 | bytes 25165824 | tf_op jit(solution)/shard_map/dot_general | solution.py:155
  408.8 19.2 %collective-permute-done.31 = bf16[256,2048]{1,0:T(8,128)(2,1)S(1)} collective-permute-done((bf16[256,2048]{1,0:T(8,128)(2,1)S(1)}, bf16[256,2048]{1,0:T(8,128)(2,1)S(1)}, u32[]{:S(2)}, u32[]{:S(2)}) %collective-permute-start.31) | collective-permute-done | bytes 1048608 | tf_op jit(solution)/shard_map/ppermute | solution.py:41
  435.9 12.8 %collective-permute-done.35 = bf16[128,2048]{1,0:T(8,128)(2,1)S(1)} collective-permute-done((bf16[128,2048]{1,0:T(8,128)(2,1)S(1)}, bf16[128,2048]{1,0:T(8,128)(2,1)S(1)}, u32[]{:S(2)}, u32[]{:S(2)}) %collective-permute-start.35) | collective-permute-done | bytes 524320 | tf_op jit(solution)/shard_map/ppermute | solution.py:41
  466.4 9.4 %collective-permute-done.37 = bf16[128,2048]{1,0:T(8,128)(2,1)S(1)} collective-permute-done((bf16[128,2048]{1,0:T(8,128)(2,1)S(1)}, bf16[128,2048]{1,0:T(8,128)(2,1)S(1)}, u32[]{:S(2)}, u32[]{:S(2)}) %collective-permute-start.37) | collective-permute-done | bytes 524320 | tf_op jit(solution)/shard_map/ppermute | solution.py:41
  477.0 6.9 %add_convert_fusion = bf16[2048,512]{1,0:T(8,128)(2,1)} fusion(bf16[2048,512]{1,0:T(8,128)(2,1)} %collective-permute-done.54, bf16[1024,2048]{1,0:T(8,128)(2,1)} %copy-done.47, bf16[1024,1024]{1,0:T(8,128)(2,1)} %get-tuple-element.101), kind=kOutput, calls=%fused_computation.12 | convolution fusion | flops 2152726528 | bytes 9437184 | tf_op jit(solution)/shard_map/dot_general | solution.py:159
  485.7 17.2 %attend_back.1 = (bf16[512,1024]{1,0:T(8,128)(2,1)}, bf16[256,2048]{1,0:T(8,128)(2,1)}, bf16[256,2048]{1,0:T(8,128)(2,1)}) custom-call(s32[2]{0:T(128)} %pad_add_fusion.refs_0_, bf16[512,2048]{1,0:T(8,128)(2,1)} %pad_maximum_fusion.3.refs_1_, bf16[512,2048]{1,0:T(8,128)(2,1)} %copy-done, bf16[512,512]{1,0:T(8,128)(2,1)} %get-tuple-element.85.refs_3_, ...), custom_call_target="tpu_custom_call" | custom-call | flops 4563402752 | bytes 16777216 | tf_op jit(solution)/shard_map/attend_back/pallas_call | solution.py:331
  517.8 13.4 %collective-permute-done.56 = bf16[512,1024]{1,0:T(8,128)(2,1)S(1)} collective-permute-done((bf16[512,1024]{1,0:T(8,128)(2,1)S(1)}, bf16[512,1024]{1,0:T(8,128)(2,1)S(1)}, u32[]{:S(2)}, u32[]{:S(2)}) %collective-permute-start.56) | collective-permute-done | bytes 1048608 | tf_op jit(solution)/shard_map/ppermute | solution.py:41
  542.6 32.4 %collective-permute-done.57 = bf16[512,512]{1,0:T(8,128)(2,1)} collective-permute-done((bf16[512,512]{1,0:T(8,128)(2,1)}, bf16[512,512]{1,0:T(8,128)(2,1)}, u32[]{:S(2)}, u32[]{:S(2)}) %collective-permute-start.57) | collective-permute-done | bytes 524320 | tf_op jit(solution)/shard_map/ppermute | solution.py:41
  591.2 10.4 %collective-permute-done.52 = bf16[512,512]{1,0:T(8,128)(2,1)} collective-permute-done((bf16[512,512]{1,0:T(8,128)(2,1)S(1)}, bf16[512,512]{1,0:T(8,128)(2,1)}, u32[]{:S(2)}, u32[]{:S(2)}) %collective-permute-start.52) | collective-permute-done | bytes 524320 | tf_op jit(solution)/shard_map/ppermute | solution.py:41
  615.9 15.4 %collective-permute-done.50 = f32[33,128]{1,0:T(8,128)S(1)} collective-permute-done((f32[33,128]{1,0:T(8,128)S(1)}, f32[33,128]{1,0:T(8,128)S(1)}, u32[]{:S(2)}, u32[]{:S(2)}) %collective-permute-start.50) | collective-permute-done | bytes 16928 | tf_op jit(solution)/shard_map/ppermute | solution.py:41
  (437 shorter events, 300.8 us)
Async XLA Ops:
  13.2 34.6 %all-to-all-start = ((bf16[256,4,512]{0,2,1:T(8,128)(2,1)}), bf16[256,4,512]{0,2,1:T(8,128)(2,1)S(1)}, u32[]{:S(2)}, u32[]{:S(2)}) async-start(bf16[256,4,512]{0,2,1:T(8,128)(2,1)} %bitcast.8), calls=%async_computation | async-start | bytes 2097152 | tf_op jit(solution)/shard_map/all_to_all | solution.py:416
  18.5 104.7 %all-gather.4.cloned.1.call-start = ((), (), s32[]{:S(2)}) async-start(), calls=%async_computation.9 | async-start | bytes 3145728 | tf_op jit(solution)/shard_map/all_gather | solution.py:421
  43.1 52.8 %collective-permute-start.1 = (bf16[2,272,1024]{2,1,0:T(8,128)(2,1)}, bf16[2,272,1024]{2,1,0:T(8,128)(2,1)}, u32[]{:S(2)}, u32[]{:S(2)}) collective-permute-start(bf16[2,272,1024]{2,1,0:T(8,128)(2,1)} %pad_maximum_fusion.5.refs_6_.refs_9_), channel_id=1, source_target_pairs={{0,8},{1,9},{2,10},{3,11},{4,12},{5,13},{6,14},{7,15},{8,0},{9,1},... | collective-permute-start | bytes 3342344 | tf_op jit(solution)/shard_map/ppermute | solution.py:41
  49.3 57.5 %collective-permute-start.5 = (bf16[512,512]{1,0:T(8,128)(2,1)S(1)}, bf16[512,512]{1,0:T(8,128)(2,1)S(1)}, u32[]{:S(2)}, u32[]{:S(2)}) collective-permute-start(bf16[512,512]{1,0:T(8,128)(2,1)S(1)} %pad_maximum_fusion.21), channel_id=1, source_target_pairs={{0,16},{1,17},{2,18},{3,19},{4,20},{5,21},{6,22},{7,23},{8,24},{9,... | collective-permute-start | bytes 1572872 | tf_op jit(solution)/shard_map/ppermute | solution.py:41
  53.8 64.3 %all-to-all-start.1 = ((bf16[256,4,512]{0,2,1:T(8,128)(2,1)}), bf16[256,4,512]{0,2,1:T(8,128)(2,1)S(1)}, u32[]{:S(2)}, u32[]{:S(2)}) async-start(bf16[256,4,512]{0,2,1:T(8,128)(2,1)} %bitcast.11), calls=%async_computation.1 | async-start | bytes 2097152 | tf_op jit(solution)/shard_map/all_to_all | solution.py:416
  57.4 65.8 %collective-permute-start.2 = (bf16[2,272,1024]{2,1,0:T(8,128)(2,1)}, bf16[2,272,1024]{2,1,0:T(8,128)(2,1)}, u32[]{:S(2)}, u32[]{:S(2)}) collective-permute-start(bf16[2,272,1024]{2,1,0:T(8,128)(2,1)} %pad_maximum_fusion.5.refs_6_.refs_9_), channel_id=1, source_target_pairs={{0,4},{1,5},{2,6},{3,7},{4,0},{5,1},{6,2},{7,3},{8,12},{9,13},{10,... | collective-permute-start | bytes 3342344 | tf_op jit(solution)/shard_map/ppermute | solution.py:41
  108.0 31.0 %collective-permute-start.6 = (bf16[512,1024]{1,0:T(8,128)(2,1)}, bf16[512,1024]{1,0:T(8,128)(2,1)S(1)}, u32[]{:S(2)}, u32[]{:S(2)}) collective-permute-start(bf16[512,1024]{1,0:T(8,128)(2,1)} %pad_maximum_fusion.8), channel_id=1, source_target_pairs={{0,8},{1,9},{2,10},{3,11},{4,12},{5,13},{6,14},{7,15},{8,0},{9,1},... | collective-permute-start | bytes 3145736 | tf_op jit(solution)/shard_map/ppermute | solution.py:41
  145.4 75.1 %all-gather.6.cloned.1.call-start = ((), (), s32[]{:S(2)}) async-start(), calls=%async_computation.10 | async-start | bytes 3145728 | tf_op jit(solution)/shard_map/all_gather | solution.py:421
  146.2 118.9 %all-gather.8.cloned.1.call-start = ((), (), s32[]{:S(2)}) async-start(), calls=%async_computation.11 | async-start | bytes 3145728 | tf_op jit(solution)/shard_map/all_gather | solution.py:421
  196.5 30.1 %collective-permute-start.13 = (bf16[2048,512]{1,0:T(8,128)(2,1)}, bf16[2048,512]{1,0:T(8,128)(2,1)}, u32[]{:S(2)}, u32[]{:S(2)}) collective-permute-start(bf16[2048,512]{1,0:T(8,128)(2,1)} %all-gather.4.cloned.1.call-done), channel_id=1, source_target_pairs={{0,1},{1,0},{2,3},{3,2},{4,5},{5,4},{6,7},{7,6},{8,9},{9,8},{10,11... | collective-permute-start | bytes 6291464 | tf_op jit(solution)/shard_map/ppermute | solution.py:41
  196.5 339.3 %reduce-scatter.8.cloned.1.call-start = ((), (), s32[]{:S(2)}) async-start(), calls=%async_computation.14 | async-start | bytes 3145728 | tf_op jit(solution)/shard_map/reduce_scatter | solution.py:526
  385.1 192.8 %reduce-scatter.4.cloned.1.call-start = ((), (), s32[]{:S(2)}) async-start(), calls=%async_computation.12 | async-start | bytes 3145728 | tf_op jit(solution)/shard_map/reduce_scatter | solution.py:526
  408.7 44.2 %collective-permute-start.43 = (bf16[2048,512]{1,0:T(8,128)(2,1)S(1)}, bf16[2048,512]{1,0:T(8,128)(2,1)S(1)}, u32[]{:S(2)}, u32[]{:S(2)}) collective-permute-start(bf16[2048,512]{1,0:T(8,128)(2,1)S(1)} %convolution_convert_fusion.3), channel_id=1, source_target_pairs={{0,1},{1,0},{2,3},{3,2},{4,5},{5,4},{6,7},{7,6},{8,9},{9,8},{10,11... | collective-permute-start | bytes 6291464 | tf_op jit(solution)/shard_map/ppermute | solution.py:41
  435.9 41.1 %collective-permute-start.54 = (bf16[2048,512]{1,0:T(8,128)(2,1)}, bf16[2048,512]{1,0:T(8,128)(2,1)}, u32[]{:S(2)}, u32[]{:S(2)}) collective-permute-start(bf16[2048,512]{1,0:T(8,128)(2,1)} %convolution_convert_fusion.1), channel_id=1, source_target_pairs={{0,1},{1,0},{2,3},{3,2},{4,5},{5,4},{6,7},{7,6},{8,9},{9,8},{10,11... | collective-permute-start | bytes 6291464 | tf_op jit(solution)/shard_map/ppermute | solution.py:41
  456.8 146.2 %reduce-scatter.6.cloned.1.call-start = ((), (), s32[]{:S(2)}) async-start(), calls=%async_computation.13 | async-start | bytes 3145728 | tf_op jit(solution)/shard_map/reduce_scatter | solution.py:526
  513.4 64.4 %collective-permute-start.42 = (bf16[1024,512]{1,0:T(8,128)(2,1)}, bf16[1024,512]{1,0:T(8,128)(2,1)}, u32[]{:S(2)}, u32[]{:S(2)}) collective-permute-start(bf16[1024,512]{1,0:T(8,128)(2,1)} %slice.502), channel_id=1, source_target_pairs={{0,4},{1,5},{2,6},{3,7},{4,0},{5,1},{6,2},{7,3},{8,12},{9,13},{10,... | collective-permute-start | bytes 3145736 | tf_op jit(solution)/shard_map/ppermute | solution.py:41
  514.9 62.9 %collective-permute-start.44 = (bf16[1024,512]{1,0:T(8,128)(2,1)}, bf16[1024,512]{1,0:T(8,128)(2,1)}, u32[]{:S(2)}, u32[]{:S(2)}) collective-permute-start(bf16[1024,512]{1,0:T(8,128)(2,1)} %pad_maximum_fusion.17), channel_id=1, source_target_pairs={{0,8},{1,9},{2,10},{3,11},{4,12},{5,13},{6,14},{7,15},{8,0},{9,1},... | collective-permute-start | bytes 3145736 | tf_op jit(solution)/shard_map/ppermute | solution.py:41
  517.2 60.7 %collective-permute-start.45 = (bf16[256,2048]{1,0:T(8,128)(2,1)S(1)}, bf16[256,2048]{1,0:T(8,128)(2,1)S(1)}, u32[]{:S(2)}, u32[]{:S(2)}) collective-permute-start(bf16[256,2048]{1,0:T(8,128)(2,1)S(1)} %add_convert_fusion.6), channel_id=1, source_target_pairs={{0,2},{1,3},{2,0},{3,1},{4,6},{5,7},{6,4},{7,5},{8,10},{9,11},{10,... | collective-permute-start | bytes 3145736 | tf_op jit(solution)/shard_map/ppermute | solution.py:41
  533.2 41.9 %collective-permute-start.57 = (bf16[512,512]{1,0:T(8,128)(2,1)}, bf16[512,512]{1,0:T(8,128)(2,1)}, u32[]{:S(2)}, u32[]{:S(2)}) collective-permute-start(bf16[512,512]{1,0:T(8,128)(2,1)} %pad_maximum_fusion.26), channel_id=1, source_target_pairs={{0,8},{1,9},{2,10},{3,11},{4,12},{5,13},{6,14},{7,15},{8,0},{9,1},... | collective-permute-start | bytes 1572872 | tf_op jit(solution)/shard_map/ppermute | solution.py:41
  535.8 75.1 %collective-permute-start.40 = (bf16[256,2048]{1,0:T(8,128)(2,1)}, bf16[256,2048]{1,0:T(8,128)(2,1)}, u32[]{:S(2)}, u32[]{:S(2)}) collective-permute-start(bf16[256,2048]{1,0:T(8,128)(2,1)} %pad_maximum_fusion.15), channel_id=1, source_target_pairs={{0,1},{1,0},{2,3},{3,2},{4,5},{5,4},{6,7},{7,6},{8,9},{9,8},{10,11... | collective-permute-start | bytes 3145736 | tf_op jit(solution)/shard_map/ppermute | solution.py:41
  538.1 66.3 %all-to-all-start.5 = ((bf16[512,4,256]{2,0,1:T(8,128)(2,1)}), bf16[512,4,256]{2,0,1:T(8,128)(2,1)}, u32[]{:S(2)}, u32[]{:S(2)}) async-start(bf16[512,4,256]{2,0,1:T(8,128)(2,1)} %bitcast.106), calls=%async_computation.8 | async-start | bytes 2097152 | tf_op jit(solution)/shard_map/all_to_all | solution.py:416
  577.1 56.9 %collective-permute-start.58 = (bf16[512,256]{1,0:T(8,128)(2,1)S(1)}, bf16[512,256]{1,0:T(8,128)(2,1)}, u32[]{:S(2)}, u32[]{:S(2)}) collective-permute-start(bf16[512,256]{1,0:T(8,128)(2,1)S(1)} %constant_dynamic-slice_fusion), channel_id=1, source_target_pairs={{0,16},{1,17},{2,18},{3,19},{4,20},{5,21},{6,22},{7,23},{8,24},{9,... | collective-permute-start | bytes 786440 | tf_op jit(solution)/shard_map/ppermute | solution.py:41
  591.2 61.3 %collective-permute-start.46 = (f32[256,2048]{1,0:T(8,128)S(1)}, f32[256,2048]{1,0:T(8,128)}, u32[]{:S(2)}, u32[]{:S(2)}) collective-permute-start(f32[256,2048]{1,0:T(8,128)S(1)} %fusion.17), channel_id=1, source_target_pairs={{0,1},{1,0},{2,3},{3,2},{4,5},{5,4},{6,7},{7,6},{8,9},{9,8},{10,11... | collective-permute-start | bytes 6291464 | tf_op jit(solution)/shard_map/ppermute | solution.py:41
  604.4 35.3 %all-to-all-start.3 = ((bf16[4,256,512]{2,1,0:T(8,128)(2,1)}), bf16[4,256,512]{2,1,0:T(8,128)(2,1)}, u32[]{:S(2)}, u32[]{:S(2)}) async-start(bf16[4,256,512]{2,1,0:T(8,128)(2,1)} %bitcast.117), calls=%async_computation.5 | async-start | bytes 2097152 | tf_op jit(solution)/shard_map/all_to_all | solution.py:416
  (109 other events, 1465.4 us)
Sparse Core Ops, SparseCore 0:
  49.3 69.9 all-gather.3
  148.3 58.3 all-gather.5
  208.2 55.5 all-gather.7
  385.2 53.7 reduce-scatter.7
  457.0 53.8 reduce-scatter.3
  513.6 53.2 reduce-scatter.5

commit v5 on v4

--- a/solution.py
+++ b/solution.py
@@ -435,7 +435,6 @@
     o_l = net.flip_l(o_far)
     qkv_ly, up = pin(net.flip_y(qkv_l), up)
     up = gather(up, 0)
-    qkv_ly, gate = pin(qkv_ly, gate)
     qkv_all = (qkv_own, qkv_l, qkv_y, qkv_ly)
 
     me = jnp.stack([net.d, net.c]).astype(jnp.int32)
@@ -502,7 +501,7 @@
     down = after(down, act_last)
     full_down = jnp.concatenate([down, net.flip_c(down)], axis=0)
     y_last = dot(act_last, full_down).astype(BF)
-    y_near = dot(after(act_near, y_last), full_down)
+    y_near = dot(after(act_near, y_last), full_down).astype(BF)
     mlp_sum = net.cube_reduce(split_parts(y_near, tok), split_parts(y_last, tok))
     output = hidden + mlp_sum
     error = (output - my_teacher) * my_live[:, None]
@@ -538,7 +537,8 @@
     dn_all = nt(
         jnp.concatenate([dg_all, du_all], axis=1), jnp.concatenate([full_gate, full_up], axis=1)
     )
-    dn_near, dn_last = dn_all[: 4 * tok], dn_all[4 * tok :].astype(BF)
+    dn_all = dn_all.astype(BF)
+    dn_near, dn_last = dn_all[: 4 * tok], dn_all[4 * tok :]
     n2_all, dg_late, du_late = after((n2_all, dg_all, du_all), dn_last)
     gate_other = tn(n2_all, dg_late[:, sub:]).astype(BF)
     gate_mine = tn(n2_all, dg_late[:, :sub]).astype(BF)

time: 676 us -> 674 us (level)
  waiting for transfers between devices: 320 us -> 328 us
    ppermute x59, waiting for transfers between devices: 308 us -> 323 us  [flip(): return lax.ppermute(v, AXES, pairs)]
    all_to_all x6, waiting for transfers between devices: 11.3 us -> 3.67 us  [exchange(): lax.all_to_all(w, 'dp', split, concat, axis_index_groups=net.near_groups,...]
    unnamed x143 -> x133, local copies, waits for them, and re-layouts: 26.1 us -> 24.1 us
  transfers between devices with their start and end apart: 71 -> 71, of which waited for: 33 -> 31; matrix products, arithmetic and copies ran while one was open for 24% -> 24% of each run, Pallas kernels for 4% -> 4%
where the time goes in v5:
time: 674 us; the launch traced here: 666 us
  waiting for transfers between devices  328 us (49%)
  starting transfers between devices  94.1 us (14%)
  matrix products  67.1 us (10%)
  local copies, waits for them, and re-layouts  63.3 us (9%)
  other arithmetic  56.3 us (8%)
  between operations  29.4 us (4%)
  Pallas kernels  27.6 us (4%)
    ppermute x59, waiting for transfers between devices, flip(): return lax.ppermute(v, AXES, pairs)  323 us
    ppermute x59, starting transfers between devices, flip(): return lax.ppermute(v, AXES, pairs)  68.1 us
    all_to_all x6, starting transfers between devices, exchange(): lax.all_to_all(w, 'dp', split, concat, axis_index_groups=net.near_groups,...  25.3 us
    dot_general x8, matrix products, tn(): lax.dot_general(left, right, (((0,), (0,)), ((), ())), preferred_element_...  25.3 us
    unnamed x133, local copies, waits for them, and re-layouts  24.1 us
    dot_general x8, matrix products, dot(): return jnp.dot(left, right, preferred_element_type=F32)  22.8 us
    dot_general x2, matrix products, nt(): lax.dot_general(left, right, (((1,), (1,)), ((), ())), preferred_element_...  19 us
    pallas_call x1, Pallas kernels, attend_back(): pl.pallas_call(functools.partial(attend_back_kernel, far), out_shape=[jax...  17.2 us
  transfers between devices with their start and end apart: 71, of which 31 were waited for; matrix products, arithmetic and copies ran while one was open for 24% of the time, Pallas kernels for 4%

profile of v5, /device:TPU:0, one launch (start us, length us, event | category | flops | bytes accessed | tf_op | source)
XLA Modules:
  0.0 665.7 jit_solution(16374181532580704690)
XLA Ops:
  23.1 18.8 %collective-permute-done = bf16[272,1024]{1,0:T(8,128)(2,1)S(1)} collective-permute-done((bf16[272,1024]{1,0:T(8,128)(2,1)S(1)}, bf16[272,1024]{1,0:T(8,128)(2,1)S(1)}, u32[]{:S(2)}, u32[]{:S(2)}) %collective-permute-start) | collective-permute-done | bytes 557088 | tf_op jit(solution)/shard_map/ppermute | solution.py:41
  59.4 25.5 %collective-permute-done.1.refs_7_.refs_10_ = bf16[2,272,1024]{2,1,0:T(8,128)(2,1)} collective-permute-done((bf16[2,272,1024]{2,1,0:T(8,128)(2,1)}, bf16[2,272,1024]{2,1,0:T(8,128)(2,1)}, u32[]{:S(2)}, u32[]{:S(2)}) %collective-permute-start.1) | collective-permute-done | bytes 1114144 | tf_op jit(solution)/shard_map/ppermute | solution.py:41
  97.4 19.6 %collective-permute-done.3.refs_9_.refs_12_ = bf16[2,272,1024]{2,1,0:T(8,128)(2,1)} collective-permute-done((bf16[2,272,1024]{2,1,0:T(8,128)(2,1)}, bf16[2,272,1024]{2,1,0:T(8,128)(2,1)}, u32[]{:S(2)}, u32[]{:S(2)}) %collective-permute-start.3) | collective-permute-done | bytes 1114144 | tf_op jit(solution)/shard_map/ppermute | solution.py:41
  117.0 10.4 %attend.1 = (bf16[512,2048]{1,0:T(8,128)(2,1)}, bf16[512,512]{1,0:T(8,128)(2,1)}, bf16[512,256]{1,0:T(8,128)(2,1)}, bf16[512,256]{1,0:T(8,128)(2,1)}, bf16[2,512...) custom-call(s32[2]{0:T(128)} %pad_add_fusion.refs_0_, bf16[512,2048]{1,0:T(8,128)(2,1)} %refs_1_.1, ...), custom_call_target="tpu_custom_call" | custom-call | flops 2684354560 | bytes 12582912 | tf_op jit(solution)/shard_map/attend/pallas_call | solution.py:247
  127.5 6.7 %collective-permute-done.6 = bf16[512,1024]{1,0:T(8,128)(2,1)S(1)} collective-permute-done((bf16[512,1024]{1,0:T(8,128)(2,1)}, bf16[512,1024]{1,0:T(8,128)(2,1)S(1)}, u32[]{:S(2)}, u32[]{:S(2)}) %collective-permute-start.6) | collective-permute-done | bytes 1048608 | tf_op jit(solution)/shard_map/ppermute | solution.py:41
  147.6 11.8 %collective-permute-done.8 = bf16[128,2048]{1,0:T(8,128)(2,1)S(1)} collective-permute-done((bf16[128,2048]{1,0:T(8,128)(2,1)S(1)}, bf16[128,2048]{1,0:T(8,128)(2,1)S(1)}, u32[]{:S(2)}, u32[]{:S(2)}) %collective-permute-start.8) | collective-permute-done | bytes 524320 | tf_op jit(solution)/shard_map/ppermute | solution.py:41
  164.9 11.7 %collective-permute-done.9 = bf16[64,2048]{1,0:T(8,128)(2,1)S(1)} collective-permute-done((bf16[64,2048]{1,0:T(8,128)(2,1)S(1)}, bf16[64,2048]{1,0:T(8,128)(2,1)S(1)}, u32[]{:S(2)}, u32[]{:S(2)}) %collective-permute-start.9) | collective-permute-done | bytes 262176 | tf_op jit(solution)/shard_map/ppermute | solution.py:41
  178.8 10.3 %collective-permute-done.10 = bf16[128,2048]{1,0:T(8,128)(2,1)S(1)} collective-permute-done((bf16[128,2048]{1,0:T(8,128)(2,1)S(1)}, bf16[128,2048]{1,0:T(8,128)(2,1)S(1)}, u32[]{:S(2)}, u32[]{:S(2)}) %collective-permute-start.10) | collective-permute-done | bytes 524320 | tf_op jit(solution)/shard_map/ppermute | solution.py:41
  205.0 11.1 %collective-permute-done.12 = bf16[128,2048]{1,0:T(8,128)(2,1)S(1)} collective-permute-done((bf16[128,2048]{1,0:T(8,128)(2,1)S(1)}, bf16[128,2048]{1,0:T(8,128)(2,1)S(1)}, u32[]{:S(2)}, u32[]{:S(2)}) %collective-permute-start.12) | collective-permute-done | bytes 524320 | tf_op jit(solution)/shard_map/ppermute | solution.py:41
  228.8 17.6 %collective-permute-done.16 = bf16[256,2048]{1,0:T(8,128)(2,1)S(1)} collective-permute-done((bf16[256,2048]{1,0:T(8,128)(2,1)}, bf16[256,2048]{1,0:T(8,128)(2,1)S(1)}, u32[]{:S(2)}, u32[]{:S(2)}) %collective-permute-start.16) | collective-permute-done | bytes 1048608 | tf_op jit(solution)/shard_map/ppermute | solution.py:41
  281.4 16.8 %collective-permute-done.18 = bf16[256,2048]{1,0:T(8,128)(2,1)S(1)} collective-permute-done((bf16[256,2048]{1,0:T(8,128)(2,1)S(1)}, bf16[256,2048]{1,0:T(8,128)(2,1)S(1)}, u32[]{:S(2)}, u32[]{:S(2)}) %collective-permute-start.18) | collective-permute-done | bytes 1048608 | tf_op jit(solution)/shard_map/ppermute | solution.py:41
  314.3 6.6 collective-permute-done.19
  341.0 7.2 %collective-permute-done.25 = bf16[128,2048]{1,0:T(8,128)(2,1)S(1)} collective-permute-done((bf16[128,2048]{1,0:T(8,128)(2,1)S(1)}, bf16[128,2048]{1,0:T(8,128)(2,1)S(1)}, u32[]{:S(2)}, u32[]{:S(2)}) %collective-permute-start.25) | collective-permute-done | bytes 524320 | tf_op jit(solution)/shard_map/ppermute | solution.py:41
  350.7 17.5 %collective-permute-done.28 = bf16[256,2048]{1,0:T(8,128)(2,1)S(1)} collective-permute-done((bf16[256,2048]{1,0:T(8,128)(2,1)S(1)}, bf16[256,2048]{1,0:T(8,128)(2,1)S(1)}, u32[]{:S(2)}, u32[]{:S(2)}) %collective-permute-start.28) | collective-permute-done | bytes 1048608 | tf_op jit(solution)/shard_map/ppermute | solution.py:41
  383.6 12.8 %fusion.11 = bf16[1024,2048]{1,0:T(8,128)(2,1)S(1)} fusion(bf16[2048,512]{1,0:T(8,128)(2,1)} %copy-done.26, bf16[2048,512]{1,0:T(8,128)(2,1)} %all-gather.6.cloned.1.call-done, bf16[2048,512]{1,0:T(8,128)(2,1)} %collective-permute-done.13, bf16[2048,512]{1,0:T(8,128)(2,1)} %all-gather.4.cloned.1.call-done, bf16[1024,1024]{1,0:T(8,128)(2,1)} %get-tuple-element.97, ...), kind=kOutput, calls=%fused_computation.17 | convolution fusion | flops 8633974784 | bytes 16777216 | tf_op jit(solution)/shard_map/dot_general | solution.py:155
  403.3 19.0 %collective-permute-done.31 = bf16[256,2048]{1,0:T(8,128)(2,1)S(1)} collective-permute-done((bf16[256,2048]{1,0:T(8,128)(2,1)S(1)}, bf16[256,2048]{1,0:T(8,128)(2,1)S(1)}, u32[]{:S(2)}, u32[]{:S(2)}) %collective-permute-start.31) | collective-permute-done | bytes 1048608 | tf_op jit(solution)/shard_map/ppermute | solution.py:41
  429.8 17.5 %collective-permute-done.35 = bf16[128,2048]{1,0:T(8,128)(2,1)S(1)} collective-permute-done((bf16[128,2048]{1,0:T(8,128)(2,1)S(1)}, bf16[128,2048]{1,0:T(8,128)(2,1)S(1)}, u32[]{:S(2)}, u32[]{:S(2)}) %collective-permute-start.35) | collective-permute-done | bytes 524320 | tf_op jit(solution)/shard_map/ppermute | solution.py:41
  465.0 9.4 %collective-permute-done.37 = bf16[128,2048]{1,0:T(8,128)(2,1)S(1)} collective-permute-done((bf16[128,2048]{1,0:T(8,128)(2,1)S(1)}, bf16[128,2048]{1,0:T(8,128)(2,1)S(1)}, u32[]{:S(2)}, u32[]{:S(2)}) %collective-permute-start.37) | collective-permute-done | bytes 524320 | tf_op jit(solution)/shard_map/ppermute | solution.py:41
  475.5 6.9 %add_convert_fusion = bf16[2048,512]{1,0:T(8,128)(2,1)} fusion(bf16[2048,512]{1,0:T(8,128)(2,1)} %collective-permute-done.54, bf16[1024,2048]{1,0:T(8,128)(2,1)} %copy-done.44, bf16[1024,1024]{1,0:T(8,128)(2,1)} %get-tuple-element.97), kind=kOutput, calls=%fused_computation.12 | convolution fusion | flops 2152726528 | bytes 9437184 | tf_op jit(solution)/shard_map/dot_general | solution.py:159
  484.2 17.2 %attend_back.1 = (bf16[512,1024]{1,0:T(8,128)(2,1)}, bf16[256,2048]{1,0:T(8,128)(2,1)}, bf16[256,2048]{1,0:T(8,128)(2,1)}) custom-call(s32[2]{0:T(128)} %pad_add_fusion.refs_0_, bf16[512,2048]{1,0:T(8,128)(2,1)} %pad_maximum_fusion.3.refs_1_, bf16[512,2048]{1,0:T(8,128)(2,1)} %copy-done, bf16[512,512]{1,0:T(8,128)(2,1)} %get-tuple-element.81.refs_3_, ...), custom_call_target="tpu_custom_call" | custom-call | flops 4563402752 | bytes 16777216 | tf_op jit(solution)/shard_map/attend_back/pallas_call | solution.py:331
  516.3 13.4 %collective-permute-done.56 = bf16[512,1024]{1,0:T(8,128)(2,1)S(1)} collective-permute-done((bf16[512,1024]{1,0:T(8,128)(2,1)S(1)}, bf16[512,1024]{1,0:T(8,128)(2,1)S(1)}, u32[]{:S(2)}, u32[]{:S(2)}) %collective-permute-start.56) | collective-permute-done | bytes 1048608 | tf_op jit(solution)/shard_map/ppermute | solution.py:41
  541.2 32.3 %collective-permute-done.57 = bf16[512,512]{1,0:T(8,128)(2,1)} collective-permute-done((bf16[512,512]{1,0:T(8,128)(2,1)}, bf16[512,512]{1,0:T(8,128)(2,1)}, u32[]{:S(2)}, u32[]{:S(2)}) %collective-permute-start.57) | collective-permute-done | bytes 524320 | tf_op jit(solution)/shard_map/ppermute | solution.py:41
  589.7 10.4 %collective-permute-done.52 = bf16[512,512]{1,0:T(8,128)(2,1)} collective-permute-done((bf16[512,512]{1,0:T(8,128)(2,1)S(1)}, bf16[512,512]{1,0:T(8,128)(2,1)}, u32[]{:S(2)}, u32[]{:S(2)}) %collective-permute-start.52) | collective-permute-done | bytes 524320 | tf_op jit(solution)/shard_map/ppermute | solution.py:41
  614.4 15.4 %collective-permute-done.50 = f32[33,128]{1,0:T(8,128)S(1)} collective-permute-done((f32[33,128]{1,0:T(8,128)S(1)}, f32[33,128]{1,0:T(8,128)S(1)}, u32[]{:S(2)}, u32[]{:S(2)}) %collective-permute-start.50) | collective-permute-done | bytes 16928 | tf_op jit(solution)/shard_map/ppermute | solution.py:41
  (426 shorter events, 290.4 us)
Async XLA Ops:
  13.2 38.0 %all-to-all-start = ((bf16[256,4,512]{0,2,1:T(8,128)(2,1)}), bf16[256,4,512]{0,2,1:T(8,128)(2,1)S(1)}, u32[]{:S(2)}, u32[]{:S(2)}) async-start(bf16[256,4,512]{0,2,1:T(8,128)(2,1)} %bitcast.8), calls=%async_computation | async-start | bytes 2097152 | tf_op jit(solution)/shard_map/all_to_all | solution.py:416
  43.1 41.8 %collective-permute-start.1 = (bf16[2,272,1024]{2,1,0:T(8,128)(2,1)}, bf16[2,272,1024]{2,1,0:T(8,128)(2,1)}, u32[]{:S(2)}, u32[]{:S(2)}) collective-permute-start(bf16[2,272,1024]{2,1,0:T(8,128)(2,1)} %pad_maximum_fusion.5.refs_6_.refs_9_), channel_id=1, source_target_pairs={{0,8},{1,9},{2,10},{3,11},{4,12},{5,13},{6,14},{7,15},{8,0},{9,1},... | collective-permute-start | bytes 3342344 | tf_op jit(solution)/shard_map/ppermute | solution.py:41
  48.0 38.4 %collective-permute-start.5 = (bf16[512,512]{1,0:T(8,128)(2,1)S(1)}, bf16[512,512]{1,0:T(8,128)(2,1)S(1)}, u32[]{:S(2)}, u32[]{:S(2)}) collective-permute-start(bf16[512,512]{1,0:T(8,128)(2,1)S(1)} %pad_maximum_fusion.21), channel_id=1, source_target_pairs={{0,16},{1,17},{2,18},{3,19},{4,20},{5,21},{6,22},{7,23},{8,24},{9,... | collective-permute-start | bytes 1572872 | tf_op jit(solution)/shard_map/ppermute | solution.py:41
  53.8 42.3 %all-to-all-start.1 = ((bf16[256,4,512]{0,2,1:T(8,128)(2,1)}), bf16[256,4,512]{0,2,1:T(8,128)(2,1)S(1)}, u32[]{:S(2)}, u32[]{:S(2)}) async-start(bf16[256,4,512]{0,2,1:T(8,128)(2,1)} %bitcast.11), calls=%async_computation.1 | async-start | bytes 2097152 | tf_op jit(solution)/shard_map/all_to_all | solution.py:416
  57.3 134.4 %all-gather.4.cloned.1.call-start = ((), (), s32[]{:S(2)}) async-start(), calls=%async_computation.9 | async-start | bytes 3145728 | tf_op jit(solution)/shard_map/all_gather | solution.py:421
  57.4 59.6 %collective-permute-start.2 = (bf16[2,272,1024]{2,1,0:T(8,128)(2,1)}, bf16[2,272,1024]{2,1,0:T(8,128)(2,1)}, u32[]{:S(2)}, u32[]{:S(2)}) collective-permute-start(bf16[2,272,1024]{2,1,0:T(8,128)(2,1)} %pad_maximum_fusion.5.refs_6_.refs_9_), channel_id=1, source_target_pairs={{0,4},{1,5},{2,6},{3,7},{4,0},{5,1},{6,2},{7,3},{8,12},{9,13},{10,... | collective-permute-start | bytes 3342344 | tf_op jit(solution)/shard_map/ppermute | solution.py:41
  87.6 46.5 %collective-permute-start.6 = (bf16[512,1024]{1,0:T(8,128)(2,1)}, bf16[512,1024]{1,0:T(8,128)(2,1)S(1)}, u32[]{:S(2)}, u32[]{:S(2)}) collective-permute-start(bf16[512,1024]{1,0:T(8,128)(2,1)} %pad_maximum_fusion.8), channel_id=1, source_target_pairs={{0,8},{1,9},{2,10},{3,11},{4,12},{5,13},{6,14},{7,15},{8,0},{9,1},... | collective-permute-start | bytes 3145736 | tf_op jit(solution)/shard_map/ppermute | solution.py:41
  142.4 76.6 %all-gather.6.cloned.1.call-start = ((), (), s32[]{:S(2)}) async-start(), calls=%async_computation.10 | async-start | bytes 3145728 | tf_op jit(solution)/shard_map/all_gather | solution.py:421
  143.1 120.6 %all-gather.8.cloned.1.call-start = ((), (), s32[]{:S(2)}) async-start(), calls=%async_computation.11 | async-start | bytes 3145728 | tf_op jit(solution)/shard_map/all_gather | solution.py:421
  191.8 33.3 %collective-permute-start.13 = (bf16[2048,512]{1,0:T(8,128)(2,1)}, bf16[2048,512]{1,0:T(8,128)(2,1)}, u32[]{:S(2)}, u32[]{:S(2)}) collective-permute-start(bf16[2048,512]{1,0:T(8,128)(2,1)} %all-gather.4.cloned.1.call-done), channel_id=1, source_target_pairs={{0,1},{1,0},{2,3},{3,2},{4,5},{5,4},{6,7},{7,6},{8,9},{9,8},{10,11... | collective-permute-start | bytes 6291464 | tf_op jit(solution)/shard_map/ppermute | solution.py:41
  191.8 342.6 %reduce-scatter.8.cloned.1.call-start = ((), (), s32[]{:S(2)}) async-start(), calls=%async_computation.14 | async-start | bytes 3145728 | tf_op jit(solution)/shard_map/reduce_scatter | solution.py:525
  383.6 192.8 %reduce-scatter.4.cloned.1.call-start = ((), (), s32[]{:S(2)}) async-start(), calls=%async_computation.12 | async-start | bytes 3145728 | tf_op jit(solution)/shard_map/reduce_scatter | solution.py:525
  402.9 48.6 %collective-permute-start.43 = (bf16[2048,512]{1,0:T(8,128)(2,1)S(1)}, bf16[2048,512]{1,0:T(8,128)(2,1)S(1)}, u32[]{:S(2)}, u32[]{:S(2)}) collective-permute-start(bf16[2048,512]{1,0:T(8,128)(2,1)S(1)} %convolution_convert_fusion.3), channel_id=1, source_target_pairs={{0,1},{1,0},{2,3},{3,2},{4,5},{5,4},{6,7},{7,6},{8,9},{9,8},{10,11... | collective-permute-start | bytes 6291464 | tf_op jit(solution)/shard_map/ppermute | solution.py:41
  429.8 45.7 %collective-permute-start.54 = (bf16[2048,512]{1,0:T(8,128)(2,1)}, bf16[2048,512]{1,0:T(8,128)(2,1)}, u32[]{:S(2)}, u32[]{:S(2)}) collective-permute-start(bf16[2048,512]{1,0:T(8,128)(2,1)} %convolution_convert_fusion.1), channel_id=1, source_target_pairs={{0,1},{1,0},{2,3},{3,2},{4,5},{5,4},{6,7},{7,6},{8,9},{9,8},{10,11... | collective-permute-start | bytes 6291464 | tf_op jit(solution)/shard_map/ppermute | solution.py:41
  455.2 146.4 %reduce-scatter.6.cloned.1.call-start = ((), (), s32[]{:S(2)}) async-start(), calls=%async_computation.13 | async-start | bytes 3145728 | tf_op jit(solution)/shard_map/reduce_scatter | solution.py:525
  511.9 64.5 %collective-permute-start.42 = (bf16[1024,512]{1,0:T(8,128)(2,1)}, bf16[1024,512]{1,0:T(8,128)(2,1)}, u32[]{:S(2)}, u32[]{:S(2)}) collective-permute-start(bf16[1024,512]{1,0:T(8,128)(2,1)} %slice.501), channel_id=1, source_target_pairs={{0,4},{1,5},{2,6},{3,7},{4,0},{5,1},{6,2},{7,3},{8,12},{9,13},{10,... | collective-permute-start | bytes 3145736 | tf_op jit(solution)/shard_map/ppermute | solution.py:41
  513.5 62.9 %collective-permute-start.44 = (bf16[1024,512]{1,0:T(8,128)(2,1)}, bf16[1024,512]{1,0:T(8,128)(2,1)}, u32[]{:S(2)}, u32[]{:S(2)}) collective-permute-start(bf16[1024,512]{1,0:T(8,128)(2,1)} %pad_maximum_fusion.17), channel_id=1, source_target_pairs={{0,8},{1,9},{2,10},{3,11},{4,12},{5,13},{6,14},{7,15},{8,0},{9,1},... | collective-permute-start | bytes 3145736 | tf_op jit(solution)/shard_map/ppermute | solution.py:41
  515.7 60.7 %collective-permute-start.45 = (bf16[256,2048]{1,0:T(8,128)(2,1)S(1)}, bf16[256,2048]{1,0:T(8,128)(2,1)S(1)}, u32[]{:S(2)}, u32[]{:S(2)}) collective-permute-start(bf16[256,2048]{1,0:T(8,128)(2,1)S(1)} %add_convert_fusion.6), channel_id=1, source_target_pairs={{0,2},{1,3},{2,0},{3,1},{4,6},{5,7},{6,4},{7,5},{8,10},{9,11},{10,... | collective-permute-start | bytes 3145736 | tf_op jit(solution)/shard_map/ppermute | solution.py:41
  531.7 41.9 %collective-permute-start.57 = (bf16[512,512]{1,0:T(8,128)(2,1)}, bf16[512,512]{1,0:T(8,128)(2,1)}, u32[]{:S(2)}, u32[]{:S(2)}) collective-permute-start(bf16[512,512]{1,0:T(8,128)(2,1)} %pad_maximum_fusion.26), channel_id=1, source_target_pairs={{0,8},{1,9},{2,10},{3,11},{4,12},{5,13},{6,14},{7,15},{8,0},{9,1},... | collective-permute-start | bytes 1572872 | tf_op jit(solution)/shard_map/ppermute | solution.py:41
  534.4 75.0 %collective-permute-start.40 = (bf16[256,2048]{1,0:T(8,128)(2,1)}, bf16[256,2048]{1,0:T(8,128)(2,1)}, u32[]{:S(2)}, u32[]{:S(2)}) collective-permute-start(bf16[256,2048]{1,0:T(8,128)(2,1)} %pad_maximum_fusion.15), channel_id=1, source_target_pairs={{0,1},{1,0},{2,3},{3,2},{4,5},{5,4},{6,7},{7,6},{8,9},{9,8},{10,11... | collective-permute-start | bytes 3145736 | tf_op jit(solution)/shard_map/ppermute | solution.py:41
  536.7 66.2 %all-to-all-start.5 = ((bf16[512,4,256]{2,0,1:T(8,128)(2,1)}), bf16[512,4,256]{2,0,1:T(8,128)(2,1)}, u32[]{:S(2)}, u32[]{:S(2)}) async-start(bf16[512,4,256]{2,0,1:T(8,128)(2,1)} %bitcast.106), calls=%async_computation.8 | async-start | bytes 2097152 | tf_op jit(solution)/shard_map/all_to_all | solution.py:416
  575.7 56.8 %collective-permute-start.58 = (bf16[512,256]{1,0:T(8,128)(2,1)S(1)}, bf16[512,256]{1,0:T(8,128)(2,1)}, u32[]{:S(2)}, u32[]{:S(2)}) collective-permute-start(bf16[512,256]{1,0:T(8,128)(2,1)S(1)} %constant_dynamic-slice_fusion), channel_id=1, source_target_pairs={{0,16},{1,17},{2,18},{3,19},{4,20},{5,21},{6,22},{7,23},{8,24},{9,... | collective-permute-start | bytes 786440 | tf_op jit(solution)/shard_map/ppermute | solution.py:41
  589.7 61.2 %collective-permute-start.46 = (f32[256,2048]{1,0:T(8,128)S(1)}, f32[256,2048]{1,0:T(8,128)}, u32[]{:S(2)}, u32[]{:S(2)}) collective-permute-start(f32[256,2048]{1,0:T(8,128)S(1)} %fusion.22), channel_id=1, source_target_pairs={{0,1},{1,0},{2,3},{3,2},{4,5},{5,4},{6,7},{7,6},{8,9},{9,8},{10,11... | collective-permute-start | bytes 6291464 | tf_op jit(solution)/shard_map/ppermute | solution.py:41
  602.9 35.3 %all-to-all-start.3 = ((bf16[4,256,512]{2,1,0:T(8,128)(2,1)}), bf16[4,256,512]{2,1,0:T(8,128)(2,1)}, u32[]{:S(2)}, u32[]{:S(2)}) async-start(bf16[4,256,512]{2,1,0:T(8,128)(2,1)} %bitcast.117), calls=%async_computation.5 | async-start | bytes 2097152 | tf_op jit(solution)/shard_map/all_to_all | solution.py:416
  (104 other events, 1383.8 us)
Sparse Core Ops, SparseCore 0:
  92.6 55.4 all-gather.3
  149.6 55.5 all-gather.5
  206.8 55.5 all-gather.7
  383.7 53.7 reduce-scatter.7
  455.3 53.9 reduce-scatter.3
  512.0 53.2 reduce-scatter.5
